TPU v7x, 128 devices: a whole 4x4x4 slice. The times are simulated.
128 devices in a mesh: band: 32 (over z, y, core), face: 4 (over x).
Axes of the slice: x: 4, y: 4, z: 4, core: 2. Of those that a mesh axis runs over, the one named last changes fastest.
Arguments:
- grid_feat: bfloat16 [262144, 227], P(('band', 'face')), may hold values from -6 to 6
- mesh_nodes: bfloat16 [65536, 512], P(('band', 'face')), may hold values from -6 to 6
- g2m_sender: int32 [128, 2048], P(('band', 'face')), may hold values from 0 to 2047, as said below
- g2m_receiver: int32 [128, 2048], P(('band', 'face')), may hold values from 0 to 511
- send_counts: int32 [128, 128], P(('band', 'face')), may hold values from 4 to 16, as said below
- edge_sender: int32 [128, 4096], P(('band', 'face')), may hold values from 0 to 1535
- edge_receiver: int32 [128, 4096], P(('band', 'face')), may hold values from 0 to 511
- embed_in: bfloat16 [227, 512], replicated, may hold values from -0.375 to 0.375
- embed_out: bfloat16 [512, 512], replicated, may hold values from -0.25 to 0.25
- proj_grid: bfloat16 [512, 512], replicated, may hold values from -0.25 to 0.25
- proj_mesh: bfloat16 [512, 512], replicated, may hold values from -0.25 to 0.25
- node_self: bfloat16 [512, 512], replicated, may hold values from -0.25 to 0.25
- node_agg: bfloat16 [512, 512], replicated, may hold values from -0.25 to 0.25
- edge_send: bfloat16 [512, 512], replicated, may hold values from -0.25 to 0.25
- edge_recv: bfloat16 [512, 512], replicated, may hold values from -0.25 to 0.25
- out_self: bfloat16 [512, 512], replicated, may hold values from -0.25 to 0.25
- out_agg: bfloat16 [512, 512], replicated, may hold values from -0.25 to 0.25
Outputs:
- mesh_out: float32 [65536, 512], P(('band', 'face'))
Inputs may be any that keep to these rules, and one draw needn't show every extreme that they name: `send_counts`: entry [i, o]: the first that many of the 16 slots from device i to owner o are live. In every draw some owner receives 16 from every device. `g2m_sender`: A row of the sending device's own grid rows; among the 16 slots from one device to one owner no row repeats. `g2m_receiver`: A row of the owner's mesh rows. `edge_sender`: see the steps for its meaning. `edge_receiver`: A row of the device's own mesh rows.
All inputs are finite; a program needn't handle non-finite values.
Results may differ from a plain program's by a relative error of at most 0.008.
Values may be sent and summed in bfloat16 or wider, within the bound.
No kernel may reach another device: no remote copies, remote signals or barrier semaphores. Data moves between devices by JAX's collectives and lax.ppermute only.
A program may use at most 64 MiB of HBM per device.

v0:
```python
import jax
import jax.numpy as jnp
from jax import lax
from jax.sharding import PartitionSpec as P


def with_halo(block, sides, width):
    for axis, dim in sides:
        count = lax.axis_size(axis)
        forward = [(i, i + 1) for i in range(count - 1)]
        forward.append((count - 1, 0))
        backward = [(target, source) for source, target in forward]
        low = lax.ppermute(
            lax.slice_in_dim(block, block.shape[dim] - width, None, axis=dim), axis, forward
        )
        high = lax.ppermute(lax.slice_in_dim(block, 0, width, axis=dim), axis, backward)
        block = jnp.concatenate([low, block, high], axis=dim)
    return block


def layer_norm(values):
    mean = jnp.mean(values, axis=-1, keepdims=True)
    centered = values - mean
    variance = jnp.mean(centered * centered, axis=-1, keepdims=True)
    return centered * lax.rsqrt(variance + 1e-05)


def pick_rows(indices, count, table):
    picker = (indices[:, None] == jnp.arange(count, dtype=jnp.int32)[None, :]).astype(jnp.bfloat16)
    return jnp.dot(picker, table, preferred_element_type=jnp.float32).astype(jnp.bfloat16)


def body(
    grid_feat,
    mesh_nodes,
    g2m_sender,
    g2m_receiver,
    send_counts,
    edge_sender,
    edge_receiver,
    embed_in,
    embed_out,
    proj_grid,
    proj_mesh,
    node_self,
    node_agg,
    edge_send,
    edge_recv,
    out_self,
    out_agg,
):
    owners = lax.axis_size(("band", "face"))
    slots = g2m_sender.shape[1]
    cap = slots // owners
    grid_rows = grid_feat.shape[0]
    mesh_rows = mesh_nodes.shape[0]
    hidden = jax.nn.silu(jnp.dot(grid_feat, embed_in, preferred_element_type=jnp.float32)).astype(
        jnp.bfloat16
    )
    latent = jnp.dot(hidden, embed_out, preferred_element_type=jnp.float32).astype(jnp.bfloat16)
    proj = jnp.dot(latent, proj_grid, preferred_element_type=jnp.float32).astype(jnp.bfloat16)
    senders = g2m_sender[0]
    receivers = g2m_receiver[0]
    within = jnp.arange(slots, dtype=jnp.int32) % cap
    live = within < jnp.repeat(send_counts[0], cap)
    sender_ids = jnp.where(live, senders, -1)
    outgoing = pick_rows(sender_ids, grid_rows, proj)
    targets = jnp.where(live, receivers, -1)
    incoming, target_in = (
        lax.all_to_all(outgoing, ("band", "face"), split_axis=0, concat_axis=0, tiled=True),
        lax.all_to_all(targets, ("band", "face"), split_axis=0, concat_axis=0, tiled=True),
    )
    receiver_rows = pick_rows(target_in, mesh_rows, mesh_nodes)
    receiver_proj = jnp.dot(receiver_rows, proj_mesh, preferred_element_type=jnp.float32)
    message = jax.nn.silu(incoming.astype(jnp.float32) + receiver_proj).astype(jnp.bfloat16)
    selector = (jnp.arange(mesh_rows, dtype=jnp.int32)[:, None] == target_in[None, :]).astype(
        jnp.bfloat16
    )
    gathered = jnp.dot(selector, message, preferred_element_type=jnp.float32).astype(jnp.bfloat16)
    inner = jnp.dot(mesh_nodes, node_self, preferred_element_type=jnp.float32) + jnp.dot(
        gathered, node_agg, preferred_element_type=jnp.float32
    )
    mesh_mid = (mesh_nodes.astype(jnp.float32) + jax.nn.silu(inner)).astype(jnp.bfloat16)
    window = with_halo(mesh_mid, (("face", 0),), mesh_rows)
    edge_from = edge_sender[0]
    edge_to = edge_receiver[0]
    from_rows = pick_rows(edge_from, 3 * mesh_rows, window)
    to_rows = pick_rows(edge_to, mesh_rows, mesh_mid)
    send_part = jnp.dot(from_rows, edge_send, preferred_element_type=jnp.float32)
    recv_part = jnp.dot(to_rows, edge_recv, preferred_element_type=jnp.float32)
    edge_msg = jax.nn.silu(send_part + recv_part).astype(jnp.bfloat16)
    edge_selector = (jnp.arange(mesh_rows, dtype=jnp.int32)[:, None] == edge_to[None, :]).astype(
        jnp.bfloat16
    )
    mesh_sum = jnp.dot(edge_selector, edge_msg, preferred_element_type=jnp.float32).astype(
        jnp.bfloat16
    )
    update = jnp.dot(mesh_mid, out_self, preferred_element_type=jnp.float32) + jnp.dot(
        mesh_sum, out_agg, preferred_element_type=jnp.float32
    )
    return layer_norm(mesh_mid.astype(jnp.float32) + jax.nn.silu(update))


def solution(mesh):
    placed = (
        P(("band", "face"), None),
        P(("band", "face"), None),
        P(("band", "face"), None),
        P(("band", "face"), None),
        P(("band", "face"), None),
        P(("band", "face"), None),
        P(("band", "face"), None),
        P(),
        P(),
        P(),
        P(),
        P(),
        P(),
        P(),
        P(),
        P(),
        P(),
    )
    return jax.shard_map(
        body, mesh=mesh, in_specs=placed, out_specs=P(("band", "face"), None), check_vma=False
    )
```

profile of v0, /device:TPU:1, one launch (start us, length us, event | category | flops | bytes accessed | tf_op | source)
XLA Modules:
  0.0 122.9 jit_solution(11548102259814916157)
XLA Ops:
  0.5 1.3 %reduce.6 = s32[2048]{0:T(1024)S(1)} reduce(s32[1,2048]{1,0:T(1,128)} %param.20, s32[]{:T(128)} %broadcast.137), dimensions={0}, to_apply=%param.20.reduce_sub_computation.3 | reduce | bytes 16388 | tf_op args[3]
  2.0 1.4 %fusion.31 = s32[128,16,1]{1,0,2:T(8,128)} fusion(s32[128,16,1]{1,0,2:T(8,128)S(1)} %squeeze.7, s32[128]{0:T(128)} %bitcast.32), kind=kLoop, calls=%fused_computation.47 | loop fusion | flops 30720 | bytes 16896 | tf_op jit(solution)/shard_map/jit(_where)/select_n | solution.py:68
  3.3 11.5 %all-to-all-start = ((s32[128,16,1]{1,2,0:T(1,128)}), s32[128,16,1]{1,2,0:T(1,128)S(1)}, u32[]{:S(2)}, u32[]{:S(2)}) async-start(s32[128,16,1]{1,2,0:T(1,128)} %bitcast.1), calls=%async_computation | async-start | bytes 131072 | tf_op jit(solution)/shard_map/all_to_all | solution.py:71
  14.8 0.7 broadcast_in_dim.28
  16.4 4.8 %convolution_convert_fusion.1 = bf16[2048,512]{1,0:T(8,128)(2,1)} fusion(bf16[512,512]{1,0:T(8,128)(2,1)} %param.25, bf16[2048,227]{0,1:T(8,128)(2,1)S(1)} %copy-done, bf16[227,512]{1,0:T(8,128)(2,1)} %param.24), kind=kOutput, calls=%fused_computation.26 | convolution fusion | flops 1556086784 | bytes 3783680 | tf_op jit(solution)/shard_map/dot_general | solution.py:60
  21.2 2.8 %convolution_convert_fusion = bf16[2048,512]{1,0:T(8,128)(2,1)S(1)} fusion(bf16[2048,512]{1,0:T(8,128)(2,1)} %convolution_convert_fusion.1, bf16[512,512]{1,0:T(8,128)(2,1)S(1)} %copy-done.2), kind=kOutput, calls=%fused_computation.25 | convolution fusion | flops 1074790400 | bytes 4718592 | tf_op jit(solution)/shard_map/dot_general | solution.py:61
  24.0 5.8 %fusion.14 = bf16[2048,512]{1,0:T(8,128)(2,1)} fusion(bf16[2048,512]{1,0:T(8,128)(2,1)S(1)} %convolution_convert_fusion, s32[2048]{0:T(1024)S(1)} %fusion.36), kind=kOutput, calls=%fused_computation.24 | convolution fusion | flops 4300210176 | bytes 4202496 | tf_op jit(solution)/shard_map/dot_general | solution.py:30
  29.8 9.7 %all-to-all-start.1 = ((bf16[128,16,512]{2,1,0:T(8,128)(2,1)}), bf16[128,16,512]{2,1,0:T(8,128)(2,1)S(1)}, u32[]{:S(2)}, u32[]{:S(2)}) async-start(bf16[128,16,512]{2,1,0:T(8,128)(2,1)} %bitcast.3), calls=%async_computation.1 | async-start | bytes 4194304 | tf_op jit(solution)/shard_map/all_to_all | solution.py:70
  39.6 2.1 %copy.22 = bf16[512,512]{0,1:T(8,128)(2,1)} copy(bf16[512,512]{1,0:T(8,128)(2,1)} %param.18) | data formatting | bytes 1048576 | tf_op args[1]
  41.7 2.7 %fusion.43 = f32[512,512]{0,1:T(8,128)} fusion(bf16[512,512]{1,0:T(8,128)(2,1)} %param.18, bf16[512,512]{1,0:T(8,128)(2,1)} %param.28), kind=kOutput, calls=%fused_computation.62 | convolution fusion | flops 268435456 | bytes 2097152 | tf_op jit(solution)/shard_map/dot_general | solution.py:80
  44.3 0.8 reduce.7
  45.2 3.6 %fusion.13 = bf16[2048,512]{1,0:T(8,128)(2,1)} fusion(bf16[512,512]{1,0:T(8,128)(2,1)} %param.18, s32[2048]{0:T(1024)S(1)} %eq.87), kind=kOutput, calls=%fused_computation.23 | convolution fusion | flops 1075838976 | bytes 2629632 | tf_op jit(solution)/shard_map/dot_general | solution.py:30
  48.8 21.7 %all-to-all-done.1 = bf16[128,16,512]{2,1,0:T(8,128)(2,1)S(1)} async-done(((bf16[128,16,512]{2,1,0:T(8,128)(2,1)}), bf16[128,16,512]{2,1,0:T(8,128)(2,1)S(1)}, u32[]{:S(2)}, u32[]{:S(2)}) %all-to-all-start.1) | async-done | bytes 2097184 | tf_op jit(solution)/shard_map/all_to_all | solution.py:70
  70.4 5.4 %fusion.27 = bf16[512,512]{1,0:T(8,128)(2,1)} fusion(s32[2048]{0:T(1024)S(1)} %eq.87, bf16[2048,512]{1,0:T(8,128)(2,1)S(1)} %bitcast.30, bf16[2048,512]{1,0:T(8,128)(2,1)} %fusion.13, bf16[512,512]{1,0:T(8,128)(2,1)} %param.27), kind=kOutput, calls=%fused_computation.36 | convolution fusion | flops 2156134400 | bytes 5251072 | tf_op jit(solution)/shard_map/dot_general | solution.py:79
  75.8 2.4 %add_convert_fusion = bf16[512,512]{0,1:T(8,128)(2,1)S(1)} fusion(f32[512,512]{0,1:T(8,128)} %fusion.43, bf16[512,512]{1,0:T(8,128)(2,1)} %fusion.27, bf16[512,512]{1,0:T(8,128)(2,1)} %param.29, bf16[512,512]{0,1:T(8,128)(2,1)} %copy.22), kind=kOutput, calls=%fused_computation.40 | convolution fusion | flops 270532608 | bytes 3145728 | tf_op jit(solution)/shard_map/dot_general | solution.py:80
  78.8 2.4 %collective-permute-start.1 = (bf16[512,512]{0,1:T(8,128)(2,1)S(1)}, bf16[512,512]{0,1:T(8,128)(2,1)S(1)}, u32[]{:S(2)}, u32[]{:S(2)}) collective-permute-start(bf16[512,512]{0,1:T(8,128)(2,1)S(1)} %add_convert_fusion), channel_id=1, source_target_pairs={{1,0},{2,1},{3,2},{0,3},{5,4},{6,5},{7,6},{4,7},{9,8},{10,9},{11,1... | collective-permute-start | bytes 1572872 | tf_op jit(solution)/shard_map/ppermute | solution.py:16
  81.7 3.9 %fusion.6 = bf16[4096,512]{1,0:T(8,128)(2,1)} fusion(bf16[512,512]{0,1:T(8,128)(2,1)S(1)} %add_convert_fusion, s32[4096]{0:T(1024)S(1)} %bitcast.35), kind=kOutput, calls=%fused_computation.11 | convolution fusion | flops 2151677952 | bytes 4734976 | tf_op jit(solution)/shard_map/dot_general | solution.py:30
  85.6 7.2 %collective-permute-done = bf16[512,512]{0,1:T(8,128)(2,1)S(1)} collective-permute-done((bf16[512,512]{0,1:T(8,128)(2,1)S(1)}, bf16[512,512]{0,1:T(8,128)(2,1)S(1)}, u32[]{:S(2)}, u32[]{:S(2)}) %collective-permute-start) | collective-permute-done | bytes 524320 | tf_op jit(solution)/shard_map/ppermute | solution.py:13
  92.8 0.8 copy-done.5
  93.6 0.8 copy-done.6
  94.4 13.4 %fusion.12 = f32[4096,512]{1,0:T(8,128)} fusion(bf16[512,512]{1,0:T(8,128)(2,1)S(1)} %copy-done.3, s32[4096]{0:T(1024)S(1)} %bitcast.34, bf16[512,512]{0,1:T(8,128)(2,1)} %copy-done.6, bf16[512,512]{0,1:T(8,128)(2,1)S(1)} %add_convert_fusion, bf16[512,512]{0,1:T(8,128)(2,1)} %copy-done.5), kind=kOutput, calls=%fused_computation.22 | convolution fusion | flops 8603041792 | bytes 10502144 | tf_op jit(solution)/shard_map/dot_general | solution.py:89
  107.8 11.7 %fusion.28 = bf16[512,512]{1,0:T(8,128)(2,1)} fusion(f32[4096,512]{1,0:T(8,128)} %fusion.12, bf16[4096,512]{1,0:T(8,128)(2,1)} %fusion.6, bf16[512,512]{1,0:T(8,128)(2,1)} %param.31, s32[4096]{0:T(1024)S(1)} %bitcast.36), kind=kOutput, calls=%fused_computation.37 | convolution fusion | flops 4309909504 | bytes 13647872 | tf_op jit(solution)/shard_map/dot_general | solution.py:95
  119.5 1.7 %fusion.42 = (f32[512]{0:T(512)S(1)}, f32[512,512]{0,1:T(8,128)S(1)}) fusion(f32[512,512]{0,1:T(8,128)S(1)} %fusion.44, bf16[512,512]{1,0:T(8,128)(2,1)} %fusion.28, bf16[512,512]{1,0:T(8,128)(2,1)S(1)} %copy-done.4, bf16[512,512]{0,1:T(8,128)(2,1)S(1)} %add_convert_fusion), kind=kOutput, calls=%fused_computation.61 | convolution fusion | flops 270532096 | bytes 3672064 | tf_op jit(solution)/shard_map/dot_general | solution.py:98
  121.6 1.3 %copy.24 = f32[512,512]{1,0:T(8,128)} copy(f32[512,512]{0,1:T(8,128)S(1)} %subtract_multiply_fusion) | data formatting | bytes 2097152 | tf_op jit(solution)/shard_map/mul | solution.py:25
  (29 shorter events, 2.9 us)
Async XLA Ops:
  0.0 16.4 %copy-start = (bf16[2048,227]{0,1:T(8,128)(2,1)S(1)}, bf16[2048,227]{0,1:T(8,128)(2,1)}, u32[]{:S(2)}) copy-start(bf16[2048,227]{0,1:T(8,128)(2,1)} %param.17) | copy-start | bytes 2789380
  3.3 26.5 %all-to-all-start = ((s32[128,16,1]{1,2,0:T(1,128)}), s32[128,16,1]{1,2,0:T(1,128)S(1)}, u32[]{:S(2)}, u32[]{:S(2)}) async-start(s32[128,16,1]{1,2,0:T(1,128)} %bitcast.1), calls=%async_computation | async-start | bytes 131072 | tf_op jit(solution)/shard_map/all_to_all | solution.py:71
  16.4 4.8 %copy-start.2 = (bf16[512,512]{1,0:T(8,128)(2,1)S(1)}, bf16[512,512]{1,0:T(8,128)(2,1)}, u32[]{:S(2)}) copy-start(bf16[512,512]{1,0:T(8,128)(2,1)} %param.26) | copy-start | bytes 1572868
  29.8 40.6 %all-to-all-start.1 = ((bf16[128,16,512]{2,1,0:T(8,128)(2,1)}), bf16[128,16,512]{2,1,0:T(8,128)(2,1)S(1)}, u32[]{:S(2)}, u32[]{:S(2)}) async-start(bf16[128,16,512]{2,1,0:T(8,128)(2,1)} %bitcast.3), calls=%async_computation.1 | async-start | bytes 4194304 | tf_op jit(solution)/shard_map/all_to_all | solution.py:70
  75.8 5.3 %copy-start.1 = (bf16[512,512]{1,0:T(8,128)(2,1)S(1)}, bf16[512,512]{1,0:T(8,128)(2,1)}, u32[]{:S(2)}) copy-start(bf16[512,512]{1,0:T(8,128)(2,1)} %param.32) | copy-start | bytes 1572868
  75.8 5.8 %copy-start.8 = (s32[1,4096]{1,0:T(1,128)S(1)}, s32[1,4096]{1,0:T(1,128)}, u32[]{:S(2)}) copy-start(s32[1,4096]{1,0:T(1,128)} %param.23) | copy-start | bytes 49156
  78.2 14.6 %collective-permute-start = (bf16[512,512]{0,1:T(8,128)(2,1)S(1)}, bf16[512,512]{0,1:T(8,128)(2,1)S(1)}, u32[]{:S(2)}, u32[]{:S(2)}) collective-permute-start(bf16[512,512]{0,1:T(8,128)(2,1)S(1)} %add_convert_fusion), channel_id=1, source_target_pairs={{0,1},{1,2},{2,3},{3,0},{4,5},{5,6},{6,7},{7,4},{8,9},{9,10},{10,1... | collective-permute-start | bytes 1572872 | tf_op jit(solution)/shard_map/ppermute | solution.py:13
  78.8 14.0 %collective-permute-start.1 = (bf16[512,512]{0,1:T(8,128)(2,1)S(1)}, bf16[512,512]{0,1:T(8,128)(2,1)S(1)}, u32[]{:S(2)}, u32[]{:S(2)}) collective-permute-start(bf16[512,512]{0,1:T(8,128)(2,1)S(1)} %add_convert_fusion), channel_id=1, source_target_pairs={{1,0},{2,1},{3,2},{0,3},{5,4},{6,5},{7,6},{4,7},{9,8},{10,9},{11,1... | collective-permute-start | bytes 1572872 | tf_op jit(solution)/shard_map/ppermute | solution.py:16
  81.7 12.8 %copy-start.3 = (bf16[512,512]{1,0:T(8,128)(2,1)S(1)}, bf16[512,512]{1,0:T(8,128)(2,1)}, u32[]{:S(2)}) copy-start(bf16[512,512]{1,0:T(8,128)(2,1)} %param.30) | copy-start | bytes 1572868
  81.7 12.7 %copy-start.7 = (s32[1,4096]{1,0:T(1,128)S(1)}, s32[1,4096]{1,0:T(1,128)}, u32[]{:S(2)}) copy-start(s32[1,4096]{1,0:T(1,128)} %param.22) | copy-start | bytes 49156
  92.8 0.8 copy-start.5
  93.6 0.8 copy-start.6
  107.8 11.7 %copy-start.4 = (bf16[512,512]{1,0:T(8,128)(2,1)S(1)}, bf16[512,512]{1,0:T(8,128)(2,1)}, u32[]{:S(2)}) copy-start(bf16[512,512]{1,0:T(8,128)(2,1)} %param.33) | copy-start | bytes 1572868
where the time goes:
time: 124 us; the launch traced here: 123 us
  matrix products  58.7 us (47%)
  waiting for transfers between devices  28.8 us (23%)
  starting transfers between devices  24.2 us (20%)
  local copies, waits for them, and re-layouts  6.51 us (5%)
  other arithmetic  4.54 us (4%)
    all_to_all x1, waiting for transfers between devices, body(): lax.all_to_all(outgoing, ('band', 'face'), split_axis=0, concat_axis=0, t...  21.7 us
    dot_general x1, matrix products, body(): jnp.dot(from_rows, edge_send, preferred_element_type=jnp.float32)  13.4 us
    dot_general x3, matrix products, pick_rows(): jnp.dot(picker, table, preferred_element_type=jnp.float32)  13.3 us
    dot_general x1, matrix products, body(): jnp.dot(edge_selector, edge_msg, preferred_element_type=jnp.float32)  11.7 us
    all_to_all x1, starting transfers between devices, body(): lax.all_to_all(targets, ('band', 'face'), split_axis=0, concat_axis=0, ti...  11.5 us
    all_to_all x1, starting transfers between devices, body(): lax.all_to_all(outgoing, ('band', 'face'), split_axis=0, concat_axis=0, t...  9.75 us
    ppermute x1, waiting for transfers between devices, with_halo(): lax.ppermute(lax.slice_in_dim(block, block.shape[dim] - width, None, axis...  7.18 us
    dot_general x1, matrix products, body(): jnp.dot(selector, message, preferred_element_type=jnp.float32)  5.4 us
  transfers between devices with their start and end apart: 4, of which 2 were waited for; matrix products, arithmetic and copies ran while one was open for 23% of the time, Pallas kernels for 0%

commit v1 on v0

v1 whole, which is shorter than its diff:
```python
import functools

import jax
import jax.numpy as jnp
from jax import lax
from jax.experimental import pallas as pl
from jax.experimental.pallas import tpu as pltpu
from jax.sharding import PartitionSpec as P

BF16 = jnp.bfloat16
F32 = jnp.float32
I32 = jnp.int32
WIDE = 256
SLOTS = 256
EDGES = 512
BLOCKS = 3
FEW = 256
SPAN = 256
ALIGN = 16
VMEM_BYTES = 40 * 1024 * 1024


def dot(a, b):
    return jnp.dot(a, b, preferred_element_type=F32)


def dot_rows(a, b):
    return lax.dot_general(a, b, (((1,), (1,)), ((), ())), preferred_element_type=F32)


def silu(v):
    half = 0.5 * v
    return half + half * jnp.tanh(half)


def one_hot(hit):
    return jnp.where(hit, 1.0, 0.0).astype(BF16)


def iota(shape, dim):
    return lax.broadcasted_iota(I32, shape, dim)


def as_column(row):
    return jnp.broadcast_to(row, (8, row.shape[1])).T[:, 0:1]


def part(ref, index):
    rows = ref.shape[1]
    return ref.at[index * rows : (index + 1) * rows, :]


def start_copies(pairs, sems):
    copies = [
        pltpu.make_async_copy(source, target, sems.at[i]) for i, (source, target) in enumerate(pairs)
    ]
    for copy in copies:
        copy.start()
    return copies


def call(kernel, outs, hbm, vmem, scratch=(), out_specs=None):
    there = pl.BlockSpec(memory_space=pltpu.HBM)
    here = pl.BlockSpec(memory_space=pltpu.VMEM)
    if out_specs is None:
        out_specs = jax.tree.map(lambda _: here, outs)
    args = [pltpu.with_memory_space_constraint(arg, pltpu.HBM) for arg in hbm]
    args += [pltpu.with_memory_space_constraint(arg, pltpu.VMEM) for arg in vmem]
    return pl.pallas_call(
        kernel,
        out_shape=outs,
        in_specs=[there] * len(hbm) + [here] * len(vmem),
        out_specs=out_specs,
        scratch_shapes=list(scratch),
        compiler_params=pltpu.CompilerParams(vmem_limit_bytes=VMEM_BYTES),
    )(*args)


def pack_kernel(
    mesh_rows,
    feat_hbm,
    sender_hbm,
    receiver_hbm,
    count_hbm,
    from_hbm,
    to_hbm,
    out_hbm,
    key_hbm,
    feat_ref,
    sender_ref,
    receiver_ref,
    count_ref,
    from_ref,
    to_ref,
    out_ref,
    key_ref,
    in_sem,
    feat_sem,
    out_sem,
    key_sem,
):
    feats, rows = feat_ref.shape
    slots = sender_ref.shape[1]
    owners = count_ref.shape[1]
    cap = slots // owners
    half = mesh_rows // 2
    small = start_copies(
        (
            (sender_hbm, sender_ref),
            (receiver_hbm, receiver_ref),
            (count_hbm, count_ref),
            (from_hbm, from_ref),
            (to_hbm, to_ref),
        ),
        in_sem,
    )
    pieces = feat_sem.shape[0]
    piece = rows // pieces
    cuts = [slice(i * piece, (i + 1) * piece) for i in range(pieces)]
    large = start_copies([(feat_hbm.at[:, cut], feat_ref.at[:, cut]) for cut in cuts], feat_sem)
    for copy in small:
        copy.wait()
    source = from_ref[...]
    row = lax.rem(source, mesh_rows)
    second = row // half
    mine = (source >= mesh_rows) & (source < 2 * mesh_rows)
    side = jnp.where(source < mesh_rows, half, 0)
    part = jnp.where(mine, 0, 1 + second)
    place = jnp.where(mine, row, row - second * half + side)
    key_ref[...] = (part * mesh_rows + to_ref[...]) * mesh_rows + place
    key_copy = pltpu.make_async_copy(key_ref, key_hbm, key_sem)
    key_copy.start()
    counts = jnp.broadcast_to(count_ref[...].astype(F32).astype(BF16), (8, owners))
    for copy in large:
        copy.wait()
    feat = feat_ref[...]
    outs = []
    for block, start in enumerate(range(0, slots, SLOTS)):
        here = slice(start, start + SLOTS)
        slot = iota((owners, SLOTS), 1) + start
        owner = iota((owners, SLOTS), 0)
        within_owner = (slot >= owner * cap) & (slot < owner * cap + cap)
        count = dot(counts, one_hot(within_owner)).astype(I32)
        lane = iota((8, SLOTS), 1) + start
        live = lax.rem(lane, cap) < count
        receiver = jnp.broadcast_to(receiver_ref[:, here], (8, SLOTS))
        sender = jnp.broadcast_to(sender_ref[:, here], (8, SLOTS))
        high = jnp.where(live, receiver >> 5, -1)
        low = jnp.where(live, receiver & 31, 0)
        line = iota((8, SLOTS), 0)
        columns = jnp.where(line == 0, sender, jnp.where(line == 1, high, low)).T
        picker = one_hot(columns[:, 0:1] == iota((SLOTS, rows), 1))
        column = iota((SLOTS, WIDE), 1)
        digits = jnp.where(
            column == feats, columns[:, 1:2], jnp.where(column == feats + 1, columns[:, 2:3], 0)
        )
        out_ref[here, :] = digits.astype(F32).astype(BF16)
        out_ref[here, :feats] = dot_rows(picker, feat).astype(BF16)
        copy = pltpu.make_async_copy(out_ref.at[here, :], out_hbm.at[here, :], out_sem.at[block])
        copy.start()
        outs.append(copy)
    for copy in outs:
        copy.wait()
    key_copy.wait()


def weights_kernel(
    embed_out_hbm,
    proj_grid_hbm,
    mesh_hbm,
    proj_mesh_hbm,
    node_self_hbm,
    key_hbm,
    fold_ref,
    proj_ref,
    self_ref,
    key_ref,
    embed_out_ref,
    proj_grid_ref,
    mesh_ref,
    proj_mesh_ref,
    node_self_ref,
    sems,
):
    pairs = (
        (embed_out_hbm, embed_out_ref),
        (proj_grid_hbm, proj_grid_ref),
        (mesh_hbm, mesh_ref),
        (proj_mesh_hbm, proj_mesh_ref),
        (node_self_hbm, node_self_ref),
        (key_hbm, key_ref),
    )
    copies = start_copies(pairs, sems)
    for copy in copies:
        copy.wait()
    fold_ref[...] = dot(embed_out_ref[...], proj_grid_ref[...]).astype(BF16)
    mesh = mesh_ref[...]
    proj_ref[...] = dot(mesh, proj_mesh_ref[...]).astype(BF16)
    self_ref[...] = dot(mesh, node_self_ref[...])


def gather_kernel(
    feats,
    mesh_hbm,
    node_agg_hbm,
    edge_send_hbm,
    edge_recv_hbm,
    out_self_hbm,
    out_agg_hbm,
    x_ref,
    embed_ref,
    fold_ref,
    proj_ref,
    self_ref,
    low_ref,
    high_ref,
    weight_ref,
    msg_ref,
    mesh_ref,
    node_agg_ref,
    sems,
):
    pairs = (
        (mesh_hbm, mesh_ref),
        (node_agg_hbm, node_agg_ref),
        (edge_send_hbm, part(weight_ref, 0)),
        (edge_recv_hbm, part(weight_ref, 1)),
        (out_self_hbm, part(weight_ref, 2)),
        (out_agg_hbm, part(weight_ref, 3)),
    )
    copies = start_copies(pairs, sems)
    slots = x_ref.shape[0]
    mesh_rows = mesh_ref.shape[0]
    half = mesh_rows // 2
    embed = embed_ref[...]
    fold = fold_ref[...]
    proj = proj_ref[...]

    def weight(place):
        return jnp.where(place == feats, 32.0, jnp.where(place == feats + 1, 1.0, 0.0)).astype(BF16)

    across = weight(iota((WIDE, 128), 0))
    along = weight(iota((8, WIDE), 1))
    targets = []
    for start in range(0, slots, SLOTS):
        here = slice(start, start + SLOTS)
        x = x_ref[here, :]
        hidden = silu(dot(x, embed)).astype(BF16)
        target = dot(x, across).astype(I32)[:, 0:1]
        picker = one_hot(target == iota((SLOTS, mesh_rows), 1))
        msg_ref[here, :] = silu(dot(hidden, fold) + dot(picker, proj)).astype(BF16)
        targets.append(dot_rows(along, x))
    target = jnp.concatenate(targets, axis=1).astype(I32)[0:1, :]
    for copy in copies:
        copy.wait()
    node_agg = node_agg_ref[...]
    for start, out_ref in ((0, low_ref), (half, high_ref)):
        here = slice(start, start + half)
        selector = one_hot(target == iota((half, slots), 0) + start)
        gathered = dot(selector, msg_ref[...]).astype(BF16)
        inner = self_ref[here, :] + dot(gathered, node_agg)
        out_ref[...] = (mesh_ref[here, :].astype(F32) + silu(inner)).astype(BF16)


def fetch_keys(key_in_ref, key_ref, key_scalar, sem):
    edges = key_in_ref.shape[1]
    copy = pltpu.make_async_copy(key_in_ref, key_scalar, sem)
    copy.start()
    key_ref[:, :edges] = key_in_ref[...]
    key_ref[:, edges:] = jnp.full((1, key_ref.shape[1] - edges), -1, I32)
    return copy


def edge_sums(part, key_scalar, key_ref, table_ref, recv_ref, acc_ref):
    mesh_rows = table_ref.shape[0]
    edges = key_scalar.shape[1]

    def first_at_least(limit):
        def halve(_, ends):
            low, high = ends
            middle = (low + high) // 2
            below = key_scalar[0, jnp.minimum(middle, edges - 1)] < limit
            go = low < high
            return (
                jnp.where(go & below, middle + 1, low),
                jnp.where(go & jnp.logical_not(below), middle, high),
            )

        ends = (jnp.int32(0), jnp.int32(edges))
        return lax.fori_loop(0, edges.bit_length(), halve, ends)[0]

    first = first_at_least(part * mesh_rows * mesh_rows)
    last = first_at_least((part + 1) * mesh_rows * mesh_rows)
    origin = first // 128 * 128

    def receiver_at(index):
        key = key_scalar[0, jnp.clip(index, 0, edges - 1)]
        return key // mesh_rows - part * mesh_rows

    def split(start, count):
        keys = key_ref[:, pl.ds(pl.multiple_of(start, 128), count)]
        column = as_column(keys)
        place = column & (mesh_rows - 1)
        receiver = lax.div(column, mesh_rows) - part * mesh_rows
        line = lax.div(keys, mesh_rows) - part * mesh_rows
        line = jnp.where((keys < 0) | (line < 0) | (line >= mesh_rows), -mesh_rows, line)
        return place, receiver, line

    table = table_ref[...]
    bases = []
    narrow = jnp.bool_(True)
    for block in range(BLOCKS):
        start = origin + block * EDGES
        low = receiver_at(jnp.maximum(start, first))
        high = receiver_at(jnp.minimum(start + EDGES, last) - 1)
        empty = start >= last
        base = jnp.where(empty, 0, low // ALIGN * ALIGN)
        narrow = narrow & (empty | (high - base < SPAN))
        bases.append(pl.multiple_of(base, ALIGN))

    @pl.when(narrow)
    def _():
        for block in range(BLOCKS):
            base = bases[block]
            place, receiver, line = split(origin + block * EDGES, EDGES)
            from_table = one_hot(place == iota((EDGES, mesh_rows), 1))
            from_recv = one_hot(receiver - base == iota((EDGES, SPAN), 1))
            window = pl.ds(base, SPAN)
            message = silu(dot(from_table, table) + dot(from_recv, recv_ref[window, :]))
            selector = one_hot(line - base == iota((SPAN, EDGES), 0))
            acc_ref[window, :] += dot(selector, message.astype(BF16))

    def general(block, carry):
        place, receiver, line = split(origin + block * FEW, FEW)
        from_table = one_hot(place == iota((FEW, mesh_rows), 1))
        from_recv = one_hot(receiver == iota((FEW, mesh_rows), 1))
        message = silu(dot(from_table, table) + dot(from_recv, recv_ref[:mesh_rows, :]))
        selector = one_hot(line == iota((mesh_rows, FEW), 0))
        acc_ref[:mesh_rows, :] += dot(selector, message.astype(BF16))
        return carry

    done = jnp.where(narrow, BLOCKS * EDGES // FEW, 0)
    lax.fori_loop(done, (last - origin + FEW - 1) // FEW, general, 0)


def own_kernel(
    key_in_ref,
    low_ref,
    high_ref,
    weight_ref,
    acc_ref,
    recv_ref,
    own_ref,
    key_ref,
    table_ref,
    key_scalar,
    sem,
):
    mesh_rows, width = table_ref.shape
    half = mesh_rows // 2
    copy = fetch_keys(key_in_ref, key_ref, key_scalar, sem)
    acc_ref[...] = jnp.zeros_like(acc_ref)
    recv_ref[mesh_rows:, :] = jnp.zeros((SPAN, width), BF16)
    for start, mid_ref in ((0, low_ref), (half, high_ref)):
        here = slice(start, start + half)
        mid = mid_ref[...]
        table_ref[here, :] = dot(mid, part(weight_ref, 0)[...]).astype(BF16)
        recv_ref[here, :] = dot(mid, part(weight_ref, 1)[...]).astype(BF16)
        own_ref[here, :] = dot(mid, part(weight_ref, 2)[...])
    copy.wait()
    edge_sums(0, key_scalar, key_ref, table_ref, recv_ref, acc_ref)


def near_kernel(
    key_in_ref,
    right_ref,
    left_ref,
    weight_ref,
    recv_ref,
    acc_in_ref,
    acc_ref,
    key_ref,
    table_ref,
    key_scalar,
    sem,
):
    half = table_ref.shape[0] // 2
    copy = fetch_keys(key_in_ref, key_ref, key_scalar, sem)
    acc_ref[...] = acc_in_ref[...]
    table_ref[:half, :] = dot(right_ref[...], part(weight_ref, 0)[...]).astype(BF16)
    table_ref[half:, :] = dot(left_ref[...], part(weight_ref, 0)[...]).astype(BF16)
    copy.wait()
    edge_sums(1, key_scalar, key_ref, table_ref, recv_ref, acc_ref)


def far_kernel(
    key_in_ref,
    right_ref,
    left_ref,
    weight_ref,
    recv_ref,
    acc_in_ref,
    low_ref,
    high_ref,
    own_ref,
    out_ref,
    key_ref,
    table_ref,
    acc_ref,
    key_scalar,
    sem,
):
    mesh_rows = table_ref.shape[0]
    half = mesh_rows // 2
    copy = fetch_keys(key_in_ref, key_ref, key_scalar, sem)
    acc_ref[...] = acc_in_ref[...]
    table_ref[:half, :] = dot(right_ref[...], part(weight_ref, 0)[...]).astype(BF16)
    table_ref[half:, :] = dot(left_ref[...], part(weight_ref, 0)[...]).astype(BF16)
    copy.wait()
    edge_sums(2, key_scalar, key_ref, table_ref, recv_ref, acc_ref)
    out_agg = part(weight_ref, 3)[...]
    for start, mid_ref in ((0, low_ref), (half, high_ref)):
        here = slice(start, start + half)
        update = own_ref[here, :] + dot(acc_ref[here, :].astype(BF16), out_agg)
        values = mid_ref[...].astype(F32) + silu(update)
        mean = jnp.mean(values, axis=-1, keepdims=True)
        centered = values - mean
        variance = jnp.mean(centered * centered, axis=-1, keepdims=True)
        out_ref[here, :] = centered * lax.rsqrt(variance + 1e-05)


def body(
    grid_feat,
    mesh_nodes,
    g2m_sender,
    g2m_receiver,
    send_counts,
    edge_sender,
    edge_receiver,
    embed_in,
    embed_out,
    proj_grid,
    proj_mesh,
    node_self,
    node_agg,
    edge_send,
    edge_recv,
    out_self,
    out_agg,
):
    owners = lax.axis_size(("band", "face"))
    faces = lax.axis_size("face")
    slots = g2m_sender.shape[1]
    grid_rows, feats = grid_feat.shape
    edges = edge_sender.shape[1]
    mesh_rows, width = mesh_nodes.shape
    half = mesh_rows // 2
    there = pl.BlockSpec(memory_space=pltpu.HBM)
    dma = pltpu.SemaphoreType.DMA
    weight = pltpu.VMEM((width, width), BF16)
    rows = pltpu.VMEM((mesh_rows, width), BF16)
    rows_half = pltpu.VMEM((half, width), BF16)
    rows_wide = pltpu.VMEM((mesh_rows, width), F32)
    sums = pltpu.VMEM((mesh_rows + SPAN, width), F32)

    packed, keys = call(
        functools.partial(pack_kernel, mesh_rows),
        (jax.ShapeDtypeStruct((slots, WIDE), BF16), jax.ShapeDtypeStruct((1, edges), I32)),
        (grid_feat.T, g2m_sender, g2m_receiver, send_counts, edge_sender, edge_receiver),
        (),
        scratch=[
            pltpu.VMEM((feats, grid_rows), BF16),
            pltpu.VMEM((1, slots), I32),
            pltpu.VMEM((1, slots), I32),
            pltpu.VMEM((1, owners), I32),
            pltpu.VMEM((1, edges), I32),
            pltpu.VMEM((1, edges), I32),
            pltpu.VMEM((slots, WIDE), BF16),
            pltpu.VMEM((1, edges), I32),
            dma((5,)),
            dma((4,)),
            dma((slots // SLOTS,)),
            dma,
        ],
        out_specs=(there, there),
    )
    keys = lax.sort(keys.reshape(edges), is_stable=False).reshape(1, edges)
    arrived = lax.all_to_all(
        packed.reshape(owners, slots // owners, WIDE),
        ("band", "face"),
        split_axis=0,
        concat_axis=0,
        tiled=True,
    ).reshape(slots, WIDE)
    fold, proj, own, keys = call(
        weights_kernel,
        (weight, rows, rows_wide, pltpu.VMEM((1, edges), I32)),
        (embed_out, proj_grid, mesh_nodes, proj_mesh, node_self, keys),
        (),
        scratch=[weight] * 2 + [rows] + [weight] * 2 + [dma((6,))],
    )
    embed = jnp.pad(embed_in, ((0, WIDE - feats), (0, 0)))
    low, high, weights = call(
        functools.partial(gather_kernel, feats),
        (rows_half, rows_half, pltpu.VMEM((4 * width, width), BF16)),
        (mesh_nodes, node_agg, edge_send, edge_recv, out_self, out_agg),
        (arrived, embed, fold, proj, own),
        scratch=[pltpu.VMEM((slots, width), BF16), rows, weight, dma((6,))],
    )

    forward = [(i, (i + 1) % faces) for i in range(faces)]
    backward = [(target, source) for source, target in forward]
    near, far = (
        (lax.ppermute(part, "face", backward), lax.ppermute(part, "face", forward))
        for part in (low, high)
    )
    key_scratch = [pltpu.VMEM((1, edges + BLOCKS * EDGES), I32)]
    key_scalars = [pltpu.SMEM((1, edges), I32), dma]
    acc, recv, own = call(
        own_kernel,
        (sums, pltpu.VMEM((mesh_rows + SPAN, width), BF16), rows_wide),
        (),
        (keys, low, high, weights),
        scratch=key_scratch + [rows] + key_scalars,
    )
    acc = call(
        near_kernel,
        sums,
        (),
        (keys, *near, weights, recv, acc),
        scratch=key_scratch + [rows] + key_scalars,
    )
    return call(
        far_kernel,
        jax.ShapeDtypeStruct((mesh_rows, width), F32),
        (),
        (keys, *far, weights, recv, acc, low, high, own),
        scratch=key_scratch + [rows, sums] + key_scalars,
    )


def solution(mesh):
    split = P(("band", "face"), None)
    return jax.shard_map(
        body,
        mesh=mesh,
        in_specs=(split,) * 7 + (P(),) * 10,
        out_specs=split,
        check_vma=False,
    )
```

time: 124 us -> 67.4 us (0.54)
  matrix products: 58.7 us -> 0 us
  Pallas kernels: 0 us -> 31.7 us
  waiting for transfers between devices: 28.8 us -> 14 us
  starting transfers between devices: 24.2 us -> 15.1 us
  local copies, waits for them, and re-layouts: 6.51 us -> 0.02 us
    dot_general x12 -> x0, matrix products: 58.7 us -> none  [the longest x1 13.4 us: body(): jnp.dot(from_rows, edge_send, preferred_element_type=jnp.float32)]
    pallas_call x0 -> x6, Pallas kernels: none -> 31.7 us  [call(): pl.pallas_call(kernel, out_shape=outs, in_specs=[there] * len(hbm) + [her...]
    all_to_all x2 -> x1, waiting for transfers between devices: 21.7 us -> 11.3 us  [body(): lax.all_to_all(packed.reshape(owners, slots // owners, WIDE), ('band', 'f...]
    all_to_all x2 -> x1, starting transfers between devices: 21.2 us -> 11.5 us  [body(): lax.all_to_all(packed.reshape(owners, slots // owners, WIDE), ('band', 'f...]
    sort x0 -> x1, other arithmetic: none -> 5.53 us  [body(): keys = lax.sort(keys.reshape(edges), is_stable=False).reshape(1, edges)]
    ppermute x2 -> x4, waiting for transfers between devices: 7.19 us -> 2.64 us  [the longest x2 2.58 us: body(): lax.ppermute(part, 'face', forward)]
    unnamed x20 -> x2, local copies, waits for them, and re-layouts: 4.23 us -> 0.01 us
    select_n x2 -> x0, other arithmetic: 2.08 us -> none  [the longest x1 1.37 us: body(): targets = jnp.where(live, receivers, -1)]
  transfers between devices with their start and end apart: 4 -> 5, of which waited for: 2 -> 4; matrix products, arithmetic and copies ran while one was open for 23% -> 8% of each run, Pallas kernels for 0% -> 17%
where the time goes in v1:
time: 67.4 us; the launch traced here: 66.6 us
  Pallas kernels  31.7 us (47%)
  starting transfers between devices  15.1 us (22%)
  waiting for transfers between devices  14 us (21%)
  other arithmetic  5.53 us (8%)
    pallas_call x6, Pallas kernels, call(): pl.pallas_call(kernel, out_shape=outs, in_specs=[there] * len(hbm) + [her...  31.7 us
    all_to_all x1, starting transfers between devices, body(): lax.all_to_all(packed.reshape(owners, slots // owners, WIDE), ('band', 'f...  11.5 us
    all_to_all x1, waiting for transfers between devices, body(): lax.all_to_all(packed.reshape(owners, slots // owners, WIDE), ('band', 'f...  11.3 us
    sort x1, other arithmetic, body(): keys = lax.sort(keys.reshape(edges), is_stable=False).reshape(1, edges)  5.53 us
    ppermute x2, starting transfers between devices, body(): lax.ppermute(part, 'face', backward)  2.97 us
    ppermute x2, waiting for transfers between devices, body(): lax.ppermute(part, 'face', forward)  2.58 us
  transfers between devices with their start and end apart: 5, of which 4 were waited for; matrix products, arithmetic and copies ran while one was open for 8% of the time, Pallas kernels for 17%

profile of v1, /device:TPU:1, one launch (start us, length us, event | category | flops | bytes accessed | tf_op | source)
XLA Modules:
  0.0 66.6 jit_solution(4206157038657151897)
XLA Ops:
  0.0 0.0 copy-start
  0.0 6.1 %shard_map.163 = (bf16[2048,256]{1,0:T(8,128)(2,1)}, s32[1,4096]{1,0:T(1,128)S(1)}) custom-call(bf16[227,2048]{1,0:T(8,128)(2,1)} %bitcast.7, s32[1,2048]{1,0:T(1,128)} %sender_hbm.1, s32[1,2048]{1,0:T(1,128)} %receiver_hbm.1, s32[1,128]{1,0:T(1,128)} %count_hbm.1, s32[1,4096]{1,0:T(1,128)} %from_hbm.1, s32[1,4096]{1,0:T(1,128)} %to_hbm.1), custom_call_target="tpu_custom_call" | custom-call | tf_op jit(solution)/shard_map/pallas_call | solution.py:69
  6.1 11.5 %all-to-all-start = ((bf16[128,16,256]{2,1,0:T(8,128)(2,1)}), bf16[128,16,256]{2,1,0:T(8,128)(2,1)S(1)}, u32[]{:S(2)}, u32[]{:S(2)}) async-start(bf16[128,16,256]{2,1,0:T(8,128)(2,1)} %bitcast.3), calls=%async_computation | async-start | bytes 2097152 | tf_op jit(solution)/shard_map/all_to_all | solution.py:488
  17.7 5.5 %sort.7 = s32[4096]{0:T(1024)} sort(s32[4096]{0:T(1024)S(1)} %bitcast.6), dimensions={0}, to_apply=%region_0.0 | sort | flops 49152 | bytes 32768 | tf_op jit(solution)/shard_map/sort | solution.py:487
  23.2 0.0 copy-done
  23.2 2.7 %shard_map.164 = (bf16[512,512]{1,0:T(8,128)(2,1)S(1)}, bf16[512,512]{1,0:T(8,128)(2,1)S(1)}, f32[512,512]{1,0:T(8,128)S(1)}, s32[1,4096]{1,0:T(1,128)S(1)}) custom-call(bf16[512,512]{1,0:T(8,128)(2,1)} %embed_out_hbm.1, bf16[512,512]{1,0:T(8,128)(2,1)} %proj_grid_hbm.1, bf16[512,512]{1,0:T(8,128)(2,1)} %mesh_hbm.3, bf16[512,512]{1,0:T(8,128)(2,1)} %proj_mesh_hbm.1, ...), custom_call_target="tpu_custom_call" | custom-call | tf_op jit(solution)/shard_map/pallas_call | solution.py:69
  25.9 11.3 %all-to-all-done = bf16[128,16,256]{2,1,0:T(8,128)(2,1)S(1)} async-done(((bf16[128,16,256]{2,1,0:T(8,128)(2,1)}), bf16[128,16,256]{2,1,0:T(8,128)(2,1)S(1)}, u32[]{:S(2)}, u32[]{:S(2)}) %all-to-all-start) | async-done | bytes 1048608 | tf_op jit(solution)/shard_map/all_to_all | solution.py:488
  37.2 8.6 %shard_map.165 = (bf16[256,512]{1,0:T(8,128)(2,1)S(1)}, bf16[256,512]{1,0:T(8,128)(2,1)S(1)}, bf16[2048,512]{1,0:T(8,128)(2,1)S(1)}) custom-call(bf16[512,512]{1,0:T(8,128)(2,1)} %mesh_hbm.3, bf16[512,512]{1,0:T(8,128)(2,1)} %node_agg_hbm.1, bf16[512,512]{1,0:T(8,128)(2,1)} %edge_send_hbm.1, bf16[512,512]{1,0:T(8,128)(2,1)} %edge_recv_hbm.1, ...), custom_call_target="tpu_custom_call" | custom-call | tf_op jit(solution)/shard_map/pallas_call | solution.py:69
  45.9 0.9 %collective-permute-start.2 = (bf16[256,512]{1,0:T(8,128)(2,1)S(1)}, bf16[256,512]{1,0:T(8,128)(2,1)S(1)}, u32[]{:S(2)}, u32[]{:S(2)}) collective-permute-start(bf16[256,512]{1,0:T(8,128)(2,1)S(1)} %get-tuple-element.25.low_ref), channel_id=1, source_target_pairs={{1,0},{2,1},{3,2},{0,3},{5,4},{6,5},{7,6},{4,7},{9,8},{10,9},{11,1... | collective-permute-start | bytes 786440 | tf_op jit(solution)/shard_map/ppermute | solution.py:514
  46.8 0.6 collective-permute-start.3
  47.4 2.1 %collective-permute-start = (bf16[256,512]{1,0:T(8,128)(2,1)S(1)}, bf16[256,512]{1,0:T(8,128)(2,1)S(1)}, u32[]{:S(2)}, u32[]{:S(2)}) collective-permute-start(bf16[256,512]{1,0:T(8,128)(2,1)S(1)} %get-tuple-element.23.high_ref), channel_id=1, source_target_pairs={{1,0},{2,1},{3,2},{0,3},{5,4},{6,5},{7,6},{4,7},{9,8},{10,9},{11,1... | collective-permute-start | bytes 786440 | tf_op jit(solution)/shard_map/ppermute | solution.py:514
  49.5 0.0 collective-permute-start.1
  49.5 4.1 %shard_map.166 = (f32[768,512]{1,0:T(8,128)S(1)}, bf16[768,512]{1,0:T(8,128)(2,1)S(1)}, f32[512,512]{1,0:T(8,128)S(1)}) custom-call(s32[1,4096]{1,0:T(1,128)S(1)} %get-tuple-element.18.key_in_ref, bf16[256,512]{1,0:T(8,128)(2,1)S(1)} %get-tuple-element.25.low_ref, bf16[256,512]{1,0:T(8,128)(2,1)S(1)} %get-tuple-element.23.high_ref, ...), custom_call_target="tpu_custom_call" | custom-call | tf_op jit(solution)/shard_map/pallas_call | solution.py:69
  53.6 0.0 collective-permute-done.2.right_ref
  53.6 1.2 %collective-permute-done.3.left_ref = bf16[256,512]{1,0:T(8,128)(2,1)S(1)} collective-permute-done((bf16[256,512]{1,0:T(8,128)(2,1)S(1)}, bf16[256,512]{1,0:T(8,128)(2,1)S(1)}, u32[]{:S(2)}, u32[]{:S(2)}) %collective-permute-start.3) | collective-permute-done | bytes 262176 | tf_op jit(solution)/shard_map/ppermute | solution.py:514
  54.8 4.2 %shard_map.167.acc_in_ref = f32[768,512]{1,0:T(8,128)S(1)} custom-call(s32[1,4096]{1,0:T(1,128)S(1)} %get-tuple-element.18.key_in_ref, bf16[256,512]{1,0:T(8,128)(2,1)S(1)} %collective-permute-done.2.right_ref, bf16[256,512]{1,0:T(8,128)(2,1)S(1)} %collective-permute-done.3.left_ref, bf16[2048,512]{1,0:T(8,128)(2,1)S(1)} %get-tuple-element.24.weight_ref, ...), custom_call_target="tpu_custom_call" | custom-call | tf_op jit(solution)/shard_map/pallas_call | solution.py:69
  59.0 0.1 collective-permute-done.right_ref
  59.1 1.4 %collective-permute-done.1.left_ref = bf16[256,512]{1,0:T(8,128)(2,1)S(1)} collective-permute-done((bf16[256,512]{1,0:T(8,128)(2,1)S(1)}, bf16[256,512]{1,0:T(8,128)(2,1)S(1)}, u32[]{:S(2)}, u32[]{:S(2)}) %collective-permute-start.1) | collective-permute-done | bytes 262176 | tf_op jit(solution)/shard_map/ppermute | solution.py:514
  60.4 6.0 %shard_map.168 = f32[512,512]{1,0:T(8,128)} custom-call(s32[1,4096]{1,0:T(1,128)S(1)} %get-tuple-element.18.key_in_ref, bf16[256,512]{1,0:T(8,128)(2,1)S(1)} %collective-permute-done.right_ref, bf16[256,512]{1,0:T(8,128)(2,1)S(1)} %collective-permute-done.1.left_ref, bf16[2048,512]{1,0:T(8,128)(2,1)S(1)} %get-tuple-element.24.weight_ref, ...), custom_call_target="tpu_custom_call" | custom-call | tf_op jit(solution)/shard_map/pallas_call | solution.py:69
  (1 shorter events, 0.0 us)
Async XLA Ops:
  0.0 23.2 %copy-start = (bf16[227,512]{1,0:T(8,128)(2,1)S(1)}, bf16[227,512]{1,0:T(8,128)(2,1)}, u32[]{:S(2)}) copy-start(bf16[227,512]{1,0:T(8,128)(2,1)} %param.24) | copy-start | bytes 697348
  6.1 31.1 %all-to-all-start = ((bf16[128,16,256]{2,1,0:T(8,128)(2,1)}), bf16[128,16,256]{2,1,0:T(8,128)(2,1)S(1)}, u32[]{:S(2)}, u32[]{:S(2)}) async-start(bf16[128,16,256]{2,1,0:T(8,128)(2,1)} %bitcast.3), calls=%async_computation | async-start | bytes 2097152 | tf_op jit(solution)/shard_map/all_to_all | solution.py:488
  45.9 7.7 %collective-permute-start.2 = (bf16[256,512]{1,0:T(8,128)(2,1)S(1)}, bf16[256,512]{1,0:T(8,128)(2,1)S(1)}, u32[]{:S(2)}, u32[]{:S(2)}) collective-permute-start(bf16[256,512]{1,0:T(8,128)(2,1)S(1)} %get-tuple-element.25.low_ref), channel_id=1, source_target_pairs={{1,0},{2,1},{3,2},{0,3},{5,4},{6,5},{7,6},{4,7},{9,8},{10,9},{11,1... | collective-permute-start | bytes 786440 | tf_op jit(solution)/shard_map/ppermute | solution.py:514
  46.8 8.0 %collective-permute-start.3 = (bf16[256,512]{1,0:T(8,128)(2,1)S(1)}, bf16[256,512]{1,0:T(8,128)(2,1)S(1)}, u32[]{:S(2)}, u32[]{:S(2)}) collective-permute-start(bf16[256,512]{1,0:T(8,128)(2,1)S(1)} %get-tuple-element.25.low_ref), channel_id=1, source_target_pairs={{0,1},{1,2},{2,3},{3,0},{4,5},{5,6},{6,7},{7,4},{8,9},{9,10},{10,1... | collective-permute-start | bytes 786440 | tf_op jit(solution)/shard_map/ppermute | solution.py:514
  47.4 11.6 %collective-permute-start = (bf16[256,512]{1,0:T(8,128)(2,1)S(1)}, bf16[256,512]{1,0:T(8,128)(2,1)S(1)}, u32[]{:S(2)}, u32[]{:S(2)}) collective-permute-start(bf16[256,512]{1,0:T(8,128)(2,1)S(1)} %get-tuple-element.23.high_ref), channel_id=1, source_target_pairs={{1,0},{2,1},{3,2},{0,3},{5,4},{6,5},{7,6},{4,7},{9,8},{10,9},{11,1... | collective-permute-start | bytes 786440 | tf_op jit(solution)/shard_map/ppermute | solution.py:514
  49.5 11.0 %collective-permute-start.1 = (bf16[256,512]{1,0:T(8,128)(2,1)S(1)}, bf16[256,512]{1,0:T(8,128)(2,1)S(1)}, u32[]{:S(2)}, u32[]{:S(2)}) collective-permute-start(bf16[256,512]{1,0:T(8,128)(2,1)S(1)} %get-tuple-element.23.high_ref), channel_id=1, source_target_pairs={{0,1},{1,2},{2,3},{3,0},{4,5},{5,6},{6,7},{7,4},{8,9},{9,10},{10,1... | collective-permute-start | bytes 786440 | tf_op jit(solution)/shard_map/ppermute | solution.py:514

commit v2 on v1

v2 whole, which is shorter than its diff:
```python
import functools

import jax
import jax.numpy as jnp
from jax import lax
from jax.experimental import pallas as pl
from jax.experimental.pallas import tpu as pltpu
from jax.sharding import PartitionSpec as P

BF16 = jnp.bfloat16
F32 = jnp.float32
I32 = jnp.int32
WIDE = 256
SLOTS = 1024
ARRIVED = 1024
BLOCKS = 3
EDGES = 512
PARTS = 3
FEW = 256
SPAN = 256
ALIGN = 16
VMEM_BYTES = 40 * 1024 * 1024


def dot(a, b):
    return jnp.dot(a, b, preferred_element_type=F32)


def dot_rows(a, b):
    return lax.dot_general(a, b, (((1,), (1,)), ((), ())), preferred_element_type=F32)


def silu(v):
    half = 0.5 * v
    return half + half * jnp.tanh(half)


def one_hot(hit):
    return jnp.where(hit, 1.0, 0.0).astype(BF16)


def iota(shape, dim):
    return lax.broadcasted_iota(I32, shape, dim)


def as_column(row):
    return jnp.broadcast_to(row, (8, row.shape[1])).T[:, 0:1]


def part(ref, index):
    rows = ref.shape[1]
    return ref.at[index * rows : (index + 1) * rows, :]


def start_copies(pairs, sems):
    copies = [
        pltpu.make_async_copy(source, target, sems.at[i]) for i, (source, target) in enumerate(pairs)
    ]
    for copy in copies:
        copy.start()
    return copies


def call(kernel, outs, hbm, vmem, scratch=(), out_specs=None, smem=(), aliases=None):
    def spec(space):
        return pl.BlockSpec(memory_space=space)

    if out_specs is None:
        out_specs = jax.tree.map(lambda _: spec(pltpu.VMEM), outs)
    args = list(smem)
    args += [pltpu.with_memory_space_constraint(arg, pltpu.HBM) for arg in hbm]
    args += [pltpu.with_memory_space_constraint(arg, pltpu.VMEM) for arg in vmem]
    spaces = [pltpu.SMEM] * len(smem) + [pltpu.HBM] * len(hbm) + [pltpu.VMEM] * len(vmem)
    return pl.pallas_call(
        kernel,
        out_shape=outs,
        in_specs=[spec(space) for space in spaces],
        out_specs=out_specs,
        scratch_shapes=list(scratch),
        input_output_aliases=aliases or {},
        compiler_params=pltpu.CompilerParams(vmem_limit_bytes=VMEM_BYTES),
    )(*args)


def pack_kernel(
    mesh_rows,
    feat_hbm,
    sender_hbm,
    receiver_hbm,
    count_hbm,
    from_hbm,
    to_hbm,
    out_hbm,
    key_hbm,
    feat_ref,
    sender_ref,
    receiver_ref,
    count_ref,
    from_ref,
    to_ref,
    column_ref,
    pad_ref,
    out_ref,
    key_ref,
    in_sem,
    feat_sem,
    out_sem,
    key_sem,
):
    feats, rows = feat_ref.shape
    slots = sender_ref.shape[1]
    owners = count_ref.shape[1]
    cap = slots // owners
    half = mesh_rows // 2
    small = start_copies(
        (
            (sender_hbm, sender_ref),
            (receiver_hbm, receiver_ref),
            (count_hbm, count_ref),
            (from_hbm, from_ref),
            (to_hbm, to_ref),
        ),
        in_sem,
    )
    pieces = feat_sem.shape[0]
    piece = rows // pieces
    cuts = [slice(i * piece, (i + 1) * piece) for i in range(pieces)]
    large = start_copies([(feat_hbm.at[:, cut], feat_ref.at[:, cut]) for cut in cuts], feat_sem)
    for copy in small:
        copy.wait()
    source = from_ref[...]
    row = lax.rem(source, mesh_rows)
    second = row // half
    mine = (source >= mesh_rows) & (source < 2 * mesh_rows)
    side = jnp.where(source < mesh_rows, half, 0)
    part = jnp.where(mine, 0, 1 + second)
    place = jnp.where(mine, row, row - second * half + side)
    key_ref[...] = (part * mesh_rows + to_ref[...]) * mesh_rows + place
    key_copy = pltpu.make_async_copy(key_ref, key_hbm, key_sem)
    key_copy.start()
    counts = jnp.broadcast_to(count_ref[...].astype(F32).astype(BF16), (8, owners))
    slot = iota((owners, slots), 1)
    first = iota((owners, slots), 0) * cap
    count = dot(counts, one_hot((slot >= first) & (slot < first + cap))).astype(I32)
    live = lax.rem(iota((8, slots), 1), cap) < count
    receiver = jnp.broadcast_to(receiver_ref[...], (8, slots))
    sender = jnp.broadcast_to(sender_ref[...], (8, slots))
    high = jnp.where(live, receiver >> 5, -1)
    low = jnp.where(live, receiver & 31, 0)
    line = iota((8, slots), 0)
    column_ref[...] = jnp.where(line == 0, sender, jnp.where(line == 1, high, low)).T
    for copy in large:
        copy.wait()
    whole = feats // ALIGN * ALIGN
    pad_ref[:whole, :] = feat_ref[:whole, :]
    line = iota((WIDE - whole, rows), 0)
    rest = jnp.zeros((WIDE - whole, rows), F32)
    for i in range(whole, feats):
        rest = jnp.where(line == i - whole, feat_ref[i : i + 1, :].astype(F32), rest)
    pad_ref[whole:, :] = rest.astype(BF16)

    def leave(block):
        here = pl.ds(pl.multiple_of(block * SLOTS, SLOTS), SLOTS)
        return pltpu.make_async_copy(out_ref.at[here, :], out_hbm.at[here, :], out_sem.at[block])

    def step(block, carry):
        start = pl.multiple_of(block * SLOTS, SLOTS)
        here = pl.ds(start, SLOTS)
        columns = column_ref[here, :]
        picker = one_hot(columns[:, 0:1] == iota((SLOTS, rows), 1))
        column = iota((SLOTS, WIDE), 1)
        digits = jnp.where(
            column == feats, columns[:, 1:2], jnp.where(column == feats + 1, columns[:, 2:3], 0)
        )
        out_ref[here, :] = (dot_rows(picker, pad_ref[...]) + digits.astype(F32)).astype(BF16)
        leave(block).start()
        return carry

    lax.fori_loop(0, slots // SLOTS, step, 0)
    for block in range(slots // SLOTS):
        leave(block).wait()
    key_copy.wait()


def weights_kernel(
    embed_out_hbm,
    proj_grid_hbm,
    mesh_hbm,
    proj_mesh_hbm,
    node_self_hbm,
    key_hbm,
    fold_ref,
    proj_ref,
    self_ref,
    key_ref,
    plan_ref,
    embed_out_ref,
    proj_grid_ref,
    mesh_ref,
    proj_mesh_ref,
    node_self_ref,
    key_scalar,
    sems,
):
    edges = key_hbm.shape[1]
    pairs = (
        (embed_out_hbm, embed_out_ref),
        (proj_grid_hbm, proj_grid_ref),
        (mesh_hbm, mesh_ref),
        (proj_mesh_hbm, proj_mesh_ref),
        (node_self_hbm, node_self_ref),
        (key_hbm, key_ref.at[:, :edges]),
        (key_hbm, key_scalar),
    )
    copies = start_copies(pairs, sems)
    key_ref[:, edges:] = jnp.full((1, key_ref.shape[1] - edges), -1, I32)
    for copy in copies:
        copy.wait()
    plan_edges(key_scalar, plan_ref, mesh_ref.shape[0])
    fold_ref[...] = dot(embed_out_ref[...], proj_grid_ref[...]).astype(BF16)
    mesh = mesh_ref[...]
    proj_ref[...] = dot(mesh, proj_mesh_ref[...]).astype(BF16)
    self_ref[...] = dot(mesh, node_self_ref[...])


def gather_kernel(
    feats,
    mesh_hbm,
    node_agg_hbm,
    edge_send_hbm,
    edge_recv_hbm,
    out_self_hbm,
    out_agg_hbm,
    x_ref,
    embed_ref,
    fold_ref,
    proj_ref,
    self_ref,
    low_ref,
    high_ref,
    weight_ref,
    sum_ref,
    mesh_ref,
    node_agg_ref,
    sems,
):
    pairs = (
        (mesh_hbm, mesh_ref),
        (node_agg_hbm, node_agg_ref),
        (edge_send_hbm, part(weight_ref, 0)),
        (edge_recv_hbm, part(weight_ref, 1)),
        (out_self_hbm, part(weight_ref, 2)),
        (out_agg_hbm, part(weight_ref, 3)),
    )
    copies = start_copies(pairs, sems)
    slots = x_ref.shape[0]
    mesh_rows = mesh_ref.shape[0]
    half = mesh_rows // 2

    def weight(place):
        return jnp.where(place == feats, 32.0, jnp.where(place == feats + 1, 1.0, 0.0)).astype(BF16)

    across = weight(iota((WIDE, 128), 0))
    along = weight(iota((8, WIDE), 1))
    sum_ref[...] = jnp.zeros_like(sum_ref)

    def step(block, carry):
        x = x_ref[pl.ds(pl.multiple_of(block * ARRIVED, ARRIVED), ARRIVED), :]
        hidden = silu(dot(x, embed_ref[...])).astype(BF16)
        column = dot(x, across).astype(I32)[:, 0:1]
        picker = one_hot(column == iota((ARRIVED, mesh_rows), 1))
        message = silu(dot(hidden, fold_ref[...]) + dot(picker, proj_ref[...])).astype(BF16)
        line = dot_rows(along, x).astype(I32)[0:1, :]
        selector = one_hot(line == iota((mesh_rows, ARRIVED), 0))
        sum_ref[...] += dot(selector, message)
        return carry

    lax.fori_loop(0, slots // ARRIVED, step, 0)
    for copy in copies:
        copy.wait()
    for start, out_ref in ((0, low_ref), (half, high_ref)):
        here = slice(start, start + half)
        inner = self_ref[here, :] + dot(sum_ref[here, :].astype(BF16), node_agg_ref[...])
        out_ref[...] = (mesh_ref[here, :].astype(F32) + silu(inner)).astype(BF16)


def plan_edges(key_scalar, plan_ref, mesh_rows):
    edges = key_scalar.shape[1]

    def first_at_least(limit):
        def halve(_, ends):
            low, high = ends
            middle = (low + high) // 2
            below = key_scalar[0, jnp.minimum(middle, edges - 1)] < limit
            go = low < high
            return (
                jnp.where(go & below, middle + 1, low),
                jnp.where(go & jnp.logical_not(below), middle, high),
            )

        ends = (jnp.int32(0), jnp.int32(edges))
        return lax.fori_loop(0, edges.bit_length(), halve, ends)[0]

    first = jnp.int32(0)
    for index in range(PARTS):
        last = jnp.int32(edges)
        if index < PARTS - 1:
            last = first_at_least((index + 1) * mesh_rows * mesh_rows)
        origin = first // 128 * 128

        def receiver_at(place):
            key = key_scalar[0, jnp.clip(place, 0, edges - 1)]
            return key // mesh_rows - index * mesh_rows

        narrow = jnp.bool_(True)
        for block in range(BLOCKS):
            start = origin + block * EDGES
            low = receiver_at(jnp.maximum(start, first))
            high = receiver_at(jnp.minimum(start + EDGES, last) - 1)
            empty = start >= last
            base = jnp.where(empty, 0, low // ALIGN * ALIGN)
            narrow = narrow & (empty | (high - base < SPAN))
            plan_ref[index, 3 + block] = base
        plan_ref[index, 0] = origin
        plan_ref[index, 1] = last
        plan_ref[index, 2] = narrow.astype(I32)
        first = last


def edge_sums(index, plan_ref, key_ref, table_ref, recv_ref, acc_ref):
    mesh_rows = table_ref.shape[0]
    origin = plan_ref[index, 0]
    last = plan_ref[index, 1]
    narrow = plan_ref[index, 2] == 1

    def split(start, count):
        keys = key_ref[:, pl.ds(pl.multiple_of(start, 128), count)]
        column = as_column(keys)
        place = column & (mesh_rows - 1)
        receiver = lax.div(column, mesh_rows) - index * mesh_rows
        line = lax.div(keys, mesh_rows) - index * mesh_rows
        line = jnp.where((keys < 0) | (line < 0) | (line >= mesh_rows), -mesh_rows, line)
        return place, receiver, line

    @pl.when(narrow)
    def _():
        for block in range(BLOCKS):
            base = pl.multiple_of(plan_ref[index, 3 + block], ALIGN)
            place, receiver, line = split(origin + block * EDGES, EDGES)
            from_table = one_hot(place == iota((EDGES, mesh_rows), 1))
            from_recv = one_hot(receiver - base == iota((EDGES, SPAN), 1))
            reach = pl.ds(base, SPAN)
            message = silu(dot(from_table, table_ref[...]) + dot(from_recv, recv_ref[reach, :]))
            selector = one_hot(line - base == iota((SPAN, EDGES), 0))
            acc_ref[reach, :] += dot(selector, message.astype(BF16))
    def general(block, carry):
        place, receiver, line = split(origin + block * FEW, FEW)
        from_table = one_hot(place == iota((FEW, mesh_rows), 1))
        from_recv = one_hot(receiver == iota((FEW, mesh_rows), 1))
        message = silu(dot(from_table, table_ref[...]) + dot(from_recv, recv_ref[:mesh_rows, :]))
        selector = one_hot(line == iota((mesh_rows, FEW), 0))
        acc_ref[:mesh_rows, :] += dot(selector, message.astype(BF16))
        return carry

    done = jnp.where(narrow, BLOCKS * EDGES // FEW, 0)
    lax.fori_loop(done, (last - origin + FEW - 1) // FEW, general, 0)


def own_kernel(
    plan_ref, key_ref, low_ref, high_ref, weight_ref, acc_ref, recv_ref, own_ref, later_ref, table_ref
):
    mesh_rows, width = table_ref.shape
    half = mesh_rows // 2
    acc_ref[...] = jnp.zeros_like(acc_ref)
    recv_ref[mesh_rows:, :] = jnp.zeros((SPAN, width), BF16)
    later_ref[...] = high_ref[...]
    for start, mid_ref in ((0, low_ref), (half, high_ref)):
        here = slice(start, start + half)
        mid = mid_ref[...]
        table_ref[here, :] = dot(mid, part(weight_ref, 0)[...]).astype(BF16)
        recv_ref[here, :] = dot(mid, part(weight_ref, 1)[...]).astype(BF16)
        own_ref[here, :] = dot(mid, part(weight_ref, 2)[...])
    edge_sums(0, plan_ref, key_ref, table_ref, recv_ref, acc_ref)


def near_kernel(
    plan_ref, acc_in_ref, key_ref, right_ref, left_ref, weight_ref, recv_ref, acc_ref, table_ref
):
    half = table_ref.shape[0] // 2
    table_ref[:half, :] = dot(right_ref[...], part(weight_ref, 0)[...]).astype(BF16)
    table_ref[half:, :] = dot(left_ref[...], part(weight_ref, 0)[...]).astype(BF16)
    edge_sums(1, plan_ref, key_ref, table_ref, recv_ref, acc_ref)


def far_kernel(
    plan_ref,
    acc_in_ref,
    key_ref,
    right_ref,
    left_ref,
    weight_ref,
    recv_ref,
    low_ref,
    high_ref,
    own_ref,
    out_hbm,
    table_ref,
    acc_ref,
    out_ref,
    sems,
):
    mesh_rows = table_ref.shape[0]
    half = mesh_rows // 2
    acc_ref[...] = acc_in_ref[...]
    table_ref[:half, :] = dot(right_ref[...], part(weight_ref, 0)[...]).astype(BF16)
    table_ref[half:, :] = dot(left_ref[...], part(weight_ref, 0)[...]).astype(BF16)
    edge_sums(2, plan_ref, key_ref, table_ref, recv_ref, acc_ref)
    copies = []
    rows = mesh_rows // sems.shape[0]
    for index in range(sems.shape[0]):
        start = index * rows
        here = slice(start, start + rows)
        update = own_ref[here, :] + dot(acc_ref[here, :].astype(BF16), part(weight_ref, 3)[...])
        mid_ref = low_ref if start < half else high_ref
        mid = mid_ref[start % half : start % half + rows, :]
        values = mid.astype(F32) + silu(update)
        mean = jnp.mean(values, axis=-1, keepdims=True)
        centered = values - mean
        variance = jnp.mean(centered * centered, axis=-1, keepdims=True)
        out_ref[here, :] = centered * lax.rsqrt(variance + 1e-05)
        copies += start_copies([(out_ref.at[here, :], out_hbm.at[here, :])], sems.at[index : index + 1])
    for copy in copies:
        copy.wait()


def body(
    grid_feat,
    mesh_nodes,
    g2m_sender,
    g2m_receiver,
    send_counts,
    edge_sender,
    edge_receiver,
    embed_in,
    embed_out,
    proj_grid,
    proj_mesh,
    node_self,
    node_agg,
    edge_send,
    edge_recv,
    out_self,
    out_agg,
):
    owners = lax.axis_size(("band", "face"))
    faces = lax.axis_size("face")
    slots = g2m_sender.shape[1]
    grid_rows, feats = grid_feat.shape
    edges = edge_sender.shape[1]
    mesh_rows, width = mesh_nodes.shape
    half = mesh_rows // 2
    there = pl.BlockSpec(memory_space=pltpu.HBM)
    dma = pltpu.SemaphoreType.DMA
    weight = pltpu.VMEM((width, width), BF16)
    rows = pltpu.VMEM((mesh_rows, width), BF16)
    rows_half = pltpu.VMEM((half, width), BF16)
    rows_wide = pltpu.VMEM((mesh_rows, width), F32)
    sums = pltpu.VMEM((mesh_rows + SPAN, width), F32)

    packed, keys = call(
        functools.partial(pack_kernel, mesh_rows),
        (jax.ShapeDtypeStruct((slots, WIDE), BF16), jax.ShapeDtypeStruct((1, edges), I32)),
        (grid_feat.T, g2m_sender, g2m_receiver, send_counts, edge_sender, edge_receiver),
        (),
        scratch=[
            pltpu.VMEM((feats, grid_rows), BF16),
            pltpu.VMEM((1, slots), I32),
            pltpu.VMEM((1, slots), I32),
            pltpu.VMEM((1, owners), I32),
            pltpu.VMEM((1, edges), I32),
            pltpu.VMEM((1, edges), I32),
            pltpu.VMEM((slots, 8), I32),
            pltpu.VMEM((WIDE, grid_rows), BF16),
            pltpu.VMEM((slots, WIDE), BF16),
            pltpu.VMEM((1, edges), I32),
            dma((5,)),
            dma((4,)),
            dma((slots // SLOTS,)),
            dma,
        ],
        out_specs=(there, there),
    )
    keys = lax.sort(keys.reshape(edges), is_stable=False).reshape(1, edges)
    arrived = lax.all_to_all(
        packed.reshape(owners, slots // owners, WIDE),
        ("band", "face"),
        split_axis=0,
        concat_axis=0,
        tiled=True,
    ).reshape(slots, WIDE)
    fold, proj, own, keys, plan = call(
        weights_kernel,
        (
            weight,
            rows,
            rows_wide,
            pltpu.VMEM((1, edges + BLOCKS * EDGES), I32),
            jax.ShapeDtypeStruct((PARTS, 3 + BLOCKS), I32),
        ),
        (embed_out, proj_grid, mesh_nodes, proj_mesh, node_self, keys),
        (),
        scratch=[weight] * 2 + [rows] + [weight] * 2 + [pltpu.SMEM((1, edges), I32), dma((7,))],
        out_specs=[pl.BlockSpec(memory_space=pltpu.VMEM)] * 4 + [pl.BlockSpec(memory_space=pltpu.SMEM)],
    )
    embed = jnp.pad(embed_in, ((0, WIDE - feats), (0, 0)))
    low, high, weights = call(
        functools.partial(gather_kernel, feats),
        (rows_half, rows_half, pltpu.VMEM((4 * width, width), BF16)),
        (mesh_nodes, node_agg, edge_send, edge_recv, out_self, out_agg),
        (arrived, embed, fold, proj, own),
        scratch=[rows_wide, rows, weight, dma((6,))],
    )

    forward = [(i, (i + 1) % faces) for i in range(faces)]
    backward = [(target, source) for source, target in forward]

    def neighbours(rows):
        return lax.ppermute(rows, "face", backward), lax.ppermute(rows, "face", forward)

    near = neighbours(low)
    acc, recv, own, later = call(
        own_kernel,
        (sums, pltpu.VMEM((mesh_rows + SPAN, width), BF16), rows_wide, rows_half),
        (),
        (keys, low, high, weights),
        scratch=[rows],
        smem=(plan,),
    )
    far = neighbours(later)
    acc = call(
        near_kernel,
        sums,
        (),
        (acc, keys, *near, weights, recv),
        scratch=[rows],
        smem=(plan,),
        aliases={1: 0},
    )
    return call(
        far_kernel,
        jax.ShapeDtypeStruct((mesh_rows, width), F32),
        (),
        (acc, keys, *far, weights, recv, low, high, own),
        scratch=[rows, sums, rows_wide, dma((4,))],
        out_specs=there,
        smem=(plan,),
    )


def solution(mesh):
    split = P(("band", "face"), None)
    return jax.shard_map(
        body,
        mesh=mesh,
        in_specs=(split,) * 7 + (P(),) * 10,
        out_specs=split,
        check_vma=False,
    )
```

time: 67.4 us -> 64.4 us (0.955)
  Pallas kernels: 31.7 us -> 28.7 us
  starting transfers between devices: 15.1 us -> 17.2 us
  waiting for transfers between devices: 14 us -> 11.9 us
    pallas_call x6, Pallas kernels: 31.7 us -> 28.7 us  [call(): pl.pallas_call(kernel, out_shape=outs, in_specs=[spec(space) for space in...]
    ppermute x4, starting transfers between devices: 3.59 us -> 5.66 us  [the longest x2 5.03 us: neighbours(): lax.ppermute(rows, 'face', backward)]
    all_to_all x1, waiting for transfers between devices: 11.3 us -> 10.2 us  [body(): lax.all_to_all(packed.reshape(owners, slots // owners, WIDE), ('band', 'f...]
    ppermute x4, waiting for transfers between devices: 2.64 us -> 1.77 us  [the longest x2 1.76 us: neighbours(): lax.ppermute(rows, 'face', forward)]
  transfers between devices with their start and end apart: 5 -> 5, of which waited for: 4 -> 2; matrix products, arithmetic and copies ran while one was open for 8% -> 9% of each run, Pallas kernels for 17% -> 18%
where the time goes in v2:
time: 64.4 us; the launch traced here: 63.6 us
  Pallas kernels  28.7 us (45%)
  starting transfers between devices  17.2 us (27%)
  waiting for transfers between devices  11.9 us (18%)
  other arithmetic  5.53 us (9%)
    pallas_call x6, Pallas kernels, call(): pl.pallas_call(kernel, out_shape=outs, in_specs=[spec(space) for space in...  28.7 us
    all_to_all x1, starting transfers between devices, body(): lax.all_to_all(packed.reshape(owners, slots // owners, WIDE), ('band', 'f...  11.5 us
    all_to_all x1, waiting for transfers between devices, body(): lax.all_to_all(packed.reshape(owners, slots // owners, WIDE), ('band', 'f...  10.2 us
    sort x1, other arithmetic, body(): keys = lax.sort(keys.reshape(edges), is_stable=False).reshape(1, edges)  5.53 us
    ppermute x2, starting transfers between devices, neighbours(): lax.ppermute(rows, 'face', backward)  5.03 us
    ppermute x2, waiting for transfers between devices, neighbours(): lax.ppermute(rows, 'face', forward)  1.76 us
  transfers between devices with their start and end apart: 5, of which 2 were waited for; matrix products, arithmetic and copies ran while one was open for 9% of the time, Pallas kernels for 18%

profile of v2, /device:TPU:1, one launch (start us, length us, event | category | flops | bytes accessed | tf_op | source)
XLA Modules:
  0.0 63.6 jit_solution(10159758518829461631)
XLA Ops:
  0.0 0.0 copy-start
  0.0 5.4 %shard_map.163 = (bf16[2048,256]{1,0:T(8,128)(2,1)}, s32[1,4096]{1,0:T(1,128)S(1)}) custom-call(bf16[227,2048]{1,0:T(8,128)(2,1)} %bitcast.7, s32[1,2048]{1,0:T(1,128)} %sender_hbm.1, s32[1,2048]{1,0:T(1,128)} %receiver_hbm.1, s32[1,128]{1,0:T(1,128)} %count_hbm.1, s32[1,4096]{1,0:T(1,128)} %from_hbm.1, s32[1,4096]{1,0:T(1,128)} %to_hbm.1), custom_call_target="tpu_custom_call" | custom-call | tf_op jit(solution)/shard_map/pallas_call | solution.py:74
  5.4 11.5 %all-to-all-start = ((bf16[128,16,256]{2,1,0:T(8,128)(2,1)}), bf16[128,16,256]{2,1,0:T(8,128)(2,1)S(1)}, u32[]{:S(2)}, u32[]{:S(2)}) async-start(bf16[128,16,256]{2,1,0:T(8,128)(2,1)} %bitcast.3), calls=%async_computation | async-start | bytes 2097152 | tf_op jit(solution)/shard_map/all_to_all | solution.py:494
  16.9 5.5 %sort.7 = s32[4096]{0:T(1024)} sort(s32[4096]{0:T(1024)S(1)} %bitcast.6), dimensions={0}, to_apply=%region_0.0 | sort | flops 49152 | bytes 32768 | tf_op jit(solution)/shard_map/sort | solution.py:493
  22.4 0.0 copy-done
  22.5 3.9 %shard_map.164 = (bf16[512,512]{1,0:T(8,128)(2,1)S(1)}, bf16[512,512]{1,0:T(8,128)(2,1)S(1)}, f32[512,512]{1,0:T(8,128)S(1)}, s32[1,5632]{1,0:T(1,128)S(1)}, s32[3,6]{1,0:T(4,128)S(1)}) custom-call(bf16[512,512]{1,0:T(8,128)(2,1)} %embed_out_hbm.1, bf16[512,512]{1,0:T(8,128)(2,1)} %proj_grid_hbm.1, bf16[512,512]{1,0:T(8,128)(2,1)} %mesh_hbm.3, ...), custom_call_target="tpu_custom_call" | custom-call | tf_op jit(solution)/shard_map/pallas_call | solution.py:74
  26.3 10.2 %all-to-all-done = bf16[128,16,256]{2,1,0:T(8,128)(2,1)S(1)} async-done(((bf16[128,16,256]{2,1,0:T(8,128)(2,1)}), bf16[128,16,256]{2,1,0:T(8,128)(2,1)S(1)}, u32[]{:S(2)}, u32[]{:S(2)}) %all-to-all-start) | async-done | bytes 1048608 | tf_op jit(solution)/shard_map/all_to_all | solution.py:494
  36.5 6.2 %shard_map.165 = (bf16[256,512]{1,0:T(8,128)(2,1)S(1)}, bf16[256,512]{1,0:T(8,128)(2,1)S(1)}, bf16[2048,512]{1,0:T(8,128)(2,1)S(1)}) custom-call(bf16[512,512]{1,0:T(8,128)(2,1)} %mesh_hbm.3, bf16[512,512]{1,0:T(8,128)(2,1)} %node_agg_hbm.1, bf16[512,512]{1,0:T(8,128)(2,1)} %edge_send_hbm.1, bf16[512,512]{1,0:T(8,128)(2,1)} %edge_recv_hbm.1, ...), custom_call_target="tpu_custom_call" | custom-call | tf_op jit(solution)/shard_map/pallas_call | solution.py:74
  42.7 0.4 collective-permute-start.1
  43.0 2.4 %collective-permute-start = (bf16[256,512]{1,0:T(8,128)(2,1)S(1)}, bf16[256,512]{1,0:T(8,128)(2,1)S(1)}, u32[]{:S(2)}, u32[]{:S(2)}) collective-permute-start(bf16[256,512]{1,0:T(8,128)(2,1)S(1)} %get-tuple-element.26.low_ref), channel_id=1, source_target_pairs={{1,0},{2,1},{3,2},{0,3},{5,4},{6,5},{7,6},{4,7},{9,8},{10,9},{11,1... | collective-permute-start | bytes 786440 | tf_op jit(solution)/shard_map/ppermute | solution.py:528
  45.4 4.3 %shard_map.166 = (f32[768,512]{1,0:T(8,128)S(1)}, bf16[768,512]{1,0:T(8,128)(2,1)S(1)}, f32[512,512]{1,0:T(8,128)S(1)}, bf16[256,512]{1,0:T(8,128)(2,1)S(1)}) custom-call(s32[3,6]{1,0:T(4,128)S(1)} %get-tuple-element.20.plan_ref, s32[1,5632]{1,0:T(1,128)S(1)} %get-tuple-element.21.key_ref, bf16[256,512]{1,0:T(8,128)(2,1)S(1)} %get-tuple-element.26.low_ref, ...), custom_call_target="tpu_custom_call" | custom-call | tf_op jit(solution)/shard_map/pallas_call | solution.py:74
  49.7 0.3 collective-permute-start.3
  49.9 2.7 %collective-permute-start.2 = (bf16[256,512]{1,0:T(8,128)(2,1)S(1)}, bf16[256,512]{1,0:T(8,128)(2,1)S(1)}, u32[]{:S(2)}, u32[]{:S(2)}) collective-permute-start(bf16[256,512]{1,0:T(8,128)(2,1)S(1)} %get-tuple-element.31), channel_id=1, source_target_pairs={{1,0},{2,1},{3,2},{0,3},{5,4},{6,5},{7,6},{4,7},{9,8},{10,9},{11,1... | collective-permute-start | bytes 786440 | tf_op jit(solution)/shard_map/ppermute | solution.py:528
  52.6 0.0 collective-permute-done.1.left_ref
  52.6 0.0 collective-permute-done.right_ref
  52.6 3.6 %shard_map.167.acc_in_ref = f32[768,512]{1,0:T(8,128)S(1)} custom-call(s32[3,6]{1,0:T(4,128)S(1)} %get-tuple-element.20.plan_ref, f32[768,512]{1,0:T(8,128)S(1)} %get-tuple-element.29.acc_in_ref, s32[1,5632]{1,0:T(1,128)S(1)} %get-tuple-element.21.key_ref, bf16[256,512]{1,0:T(8,128)(2,1)S(1)} %collective-permute-done.right_ref, ...), custom_call_target="tpu_custom_call", output_to_operand_aliasing={{}: (1, {})} | custom-call | tf_op jit(solution)/shard_map/pallas_call | solution.py:74
  56.2 1.8 %collective-permute-done.3.left_ref = bf16[256,512]{1,0:T(8,128)(2,1)S(1)} collective-permute-done((bf16[256,512]{1,0:T(8,128)(2,1)S(1)}, bf16[256,512]{1,0:T(8,128)(2,1)S(1)}, u32[]{:S(2)}, u32[]{:S(2)}) %collective-permute-start.3) | collective-permute-done | bytes 262176 | tf_op jit(solution)/shard_map/ppermute | solution.py:528
  58.0 0.0 collective-permute-done.2.right_ref
  58.0 5.4 %shard_map.168 = f32[512,512]{1,0:T(8,128)} custom-call(s32[3,6]{1,0:T(4,128)S(1)} %get-tuple-element.20.plan_ref, f32[768,512]{1,0:T(8,128)S(1)} %shard_map.167.acc_in_ref, s32[1,5632]{1,0:T(1,128)S(1)} %get-tuple-element.21.key_ref, bf16[256,512]{1,0:T(8,128)(2,1)S(1)} %collective-permute-done.2.right_ref, ...), custom_call_target="tpu_custom_call" | custom-call | tf_op jit(solution)/shard_map/pallas_call | solution.py:74
  (1 shorter events, 0.0 us)
Async XLA Ops:
  0.0 22.4 %copy-start = (bf16[227,512]{1,0:T(8,128)(2,1)S(1)}, bf16[227,512]{1,0:T(8,128)(2,1)}, u32[]{:S(2)}) copy-start(bf16[227,512]{1,0:T(8,128)(2,1)} %param.24) | copy-start | bytes 697348
  5.4 31.1 %all-to-all-start = ((bf16[128,16,256]{2,1,0:T(8,128)(2,1)}), bf16[128,16,256]{2,1,0:T(8,128)(2,1)S(1)}, u32[]{:S(2)}, u32[]{:S(2)}) async-start(bf16[128,16,256]{2,1,0:T(8,128)(2,1)} %bitcast.3), calls=%async_computation | async-start | bytes 2097152 | tf_op jit(solution)/shard_map/all_to_all | solution.py:494
  42.7 9.9 %collective-permute-start.1 = (bf16[256,512]{1,0:T(8,128)(2,1)S(1)}, bf16[256,512]{1,0:T(8,128)(2,1)S(1)}, u32[]{:S(2)}, u32[]{:S(2)}) collective-permute-start(bf16[256,512]{1,0:T(8,128)(2,1)S(1)} %get-tuple-element.26.low_ref), channel_id=1, source_target_pairs={{0,1},{1,2},{2,3},{3,0},{4,5},{5,6},{6,7},{7,4},{8,9},{9,10},{10,1... | collective-permute-start | bytes 786440 | tf_op jit(solution)/shard_map/ppermute | solution.py:528
  43.0 9.6 %collective-permute-start = (bf16[256,512]{1,0:T(8,128)(2,1)S(1)}, bf16[256,512]{1,0:T(8,128)(2,1)S(1)}, u32[]{:S(2)}, u32[]{:S(2)}) collective-permute-start(bf16[256,512]{1,0:T(8,128)(2,1)S(1)} %get-tuple-element.26.low_ref), channel_id=1, source_target_pairs={{1,0},{2,1},{3,2},{0,3},{5,4},{6,5},{7,6},{4,7},{9,8},{10,9},{11,1... | collective-permute-start | bytes 786440 | tf_op jit(solution)/shard_map/ppermute | solution.py:528
  49.7 8.3 %collective-permute-start.3 = (bf16[256,512]{1,0:T(8,128)(2,1)S(1)}, bf16[256,512]{1,0:T(8,128)(2,1)S(1)}, u32[]{:S(2)}, u32[]{:S(2)}) collective-permute-start(bf16[256,512]{1,0:T(8,128)(2,1)S(1)} %get-tuple-element.31), channel_id=1, source_target_pairs={{0,1},{1,2},{2,3},{3,0},{4,5},{5,6},{6,7},{7,4},{8,9},{9,10},{10,1... | collective-permute-start | bytes 786440 | tf_op jit(solution)/shard_map/ppermute | solution.py:528
  49.9 8.1 %collective-permute-start.2 = (bf16[256,512]{1,0:T(8,128)(2,1)S(1)}, bf16[256,512]{1,0:T(8,128)(2,1)S(1)}, u32[]{:S(2)}, u32[]{:S(2)}) collective-permute-start(bf16[256,512]{1,0:T(8,128)(2,1)S(1)} %get-tuple-element.31), channel_id=1, source_target_pairs={{1,0},{2,1},{3,2},{0,3},{5,4},{6,5},{7,6},{4,7},{9,8},{10,9},{11,1... | collective-permute-start | bytes 786440 | tf_op jit(solution)/shard_map/ppermute | solution.py:528

commit v3 on v2

--- a/solution.py
+++ b/solution.py
@@ -11,6 +11,7 @@
 F32 = jnp.float32
 I32 = jnp.int32
 WIDE = 256
+DEAD = 1024
 SLOTS = 1024
 ARRIVED = 1024
 BLOCKS = 3
@@ -41,6 +42,10 @@
 
 def iota(shape, dim):
     return lax.broadcasted_iota(I32, shape, dim)
+
+
+def receiver_code(receiver):
+    return jnp.where(receiver <= DEAD // 4, receiver, DEAD // 4 - receiver)
 
 
 def as_column(row):
@@ -145,10 +150,8 @@
     live = lax.rem(iota((8, slots), 1), cap) < count
     receiver = jnp.broadcast_to(receiver_ref[...], (8, slots))
     sender = jnp.broadcast_to(sender_ref[...], (8, slots))
-    high = jnp.where(live, receiver >> 5, -1)
-    low = jnp.where(live, receiver & 31, 0)
-    line = iota((8, slots), 0)
-    column_ref[...] = jnp.where(line == 0, sender, jnp.where(line == 1, high, low)).T
+    code = jnp.where(live, receiver_code(receiver), DEAD)
+    column_ref[...] = jnp.where(iota((8, slots), 0) == 0, sender, code).T
     for copy in large:
         copy.wait()
     whole = feats // ALIGN * ALIGN
@@ -169,10 +172,8 @@
         columns = column_ref[here, :]
         picker = one_hot(columns[:, 0:1] == iota((SLOTS, rows), 1))
         column = iota((SLOTS, WIDE), 1)
-        digits = jnp.where(
-            column == feats, columns[:, 1:2], jnp.where(column == feats + 1, columns[:, 2:3], 0)
-        )
-        out_ref[here, :] = (dot_rows(picker, pad_ref[...]) + digits.astype(F32)).astype(BF16)
+        code = jnp.where(column == feats, columns[:, 1:2], 0).astype(F32)
+        out_ref[here, :] = (dot_rows(picker, pad_ref[...]) + code).astype(BF16)
         leave(block).start()
         return carry
 
@@ -223,6 +224,11 @@
     self_ref[...] = dot(mesh, node_self_ref[...])
 
 
+def next_rows(sums, own, mesh, node_agg):
+    inner = own + dot(sums.astype(BF16), node_agg)
+    return (mesh.astype(F32) + silu(inner)).astype(BF16)
+
+
 def gather_kernel(
     feats,
     mesh_hbm,
@@ -237,51 +243,43 @@
     proj_ref,
     self_ref,
     low_ref,
-    high_ref,
+    send_ref,
+    msg_ref,
+    line_ref,
     weight_ref,
     sum_ref,
-    mesh_ref,
-    node_agg_ref,
     sems,
 ):
-    pairs = (
-        (mesh_hbm, mesh_ref),
-        (node_agg_hbm, node_agg_ref),
-        (edge_send_hbm, part(weight_ref, 0)),
-        (edge_recv_hbm, part(weight_ref, 1)),
-        (out_self_hbm, part(weight_ref, 2)),
-        (out_agg_hbm, part(weight_ref, 3)),
-    )
-    copies = start_copies(pairs, sems)
+    sources = (edge_send_hbm, edge_recv_hbm, out_self_hbm, out_agg_hbm, node_agg_hbm, mesh_hbm)
+    copies = start_copies([(hbm, part(weight_ref, i)) for i, hbm in enumerate(sources)], sems)
     slots = x_ref.shape[0]
-    mesh_rows = mesh_ref.shape[0]
+    mesh_rows = self_ref.shape[0]
     half = mesh_rows // 2
-
-    def weight(place):
-        return jnp.where(place == feats, 32.0, jnp.where(place == feats + 1, 1.0, 0.0)).astype(BF16)
-
-    across = weight(iota((WIDE, 128), 0))
-    along = weight(iota((8, WIDE), 1))
+    lanes = feats // 128 * 128
+    along = one_hot(iota((8, WIDE - lanes), 1) == feats - lanes)
     sum_ref[...] = jnp.zeros_like(sum_ref)
 
     def step(block, carry):
-        x = x_ref[pl.ds(pl.multiple_of(block * ARRIVED, ARRIVED), ARRIVED), :]
+        here = pl.ds(pl.multiple_of(block * ARRIVED, ARRIVED), ARRIVED)
+        x = x_ref[here, :]
         hidden = silu(dot(x, embed_ref[...])).astype(BF16)
-        column = dot(x, across).astype(I32)[:, 0:1]
-        picker = one_hot(column == iota((ARRIVED, mesh_rows), 1))
+        column = x[:, feats : feats + 1].astype(F32)
+        codes = receiver_code(iota((ARRIVED, mesh_rows), 1)).astype(F32)
+        picker = one_hot(column == codes)
         message = silu(dot(hidden, fold_ref[...]) + dot(picker, proj_ref[...])).astype(BF16)
-        line = dot_rows(along, x).astype(I32)[0:1, :]
-        selector = one_hot(line == iota((mesh_rows, ARRIVED), 0))
-        sum_ref[...] += dot(selector, message)
+        msg_ref[here, :] = message
+        line = dot_rows(along, x[:, lanes:])
+        line_ref[:, here] = line
+        codes = receiver_code(iota((half, ARRIVED), 0)).astype(F32)
+        sum_ref[...] += dot(one_hot(line[0:1, :] == codes), message)
         return carry
 
     lax.fori_loop(0, slots // ARRIVED, step, 0)
     for copy in copies:
         copy.wait()
-    for start, out_ref in ((0, low_ref), (half, high_ref)):
-        here = slice(start, start + half)
-        inner = self_ref[here, :] + dot(sum_ref[here, :].astype(BF16), node_agg_ref[...])
-        out_ref[...] = (mesh_ref[here, :].astype(F32) + silu(inner)).astype(BF16)
+    mesh = part(weight_ref, 5)[:half, :]
+    low_ref[...] = next_rows(sum_ref[...], self_ref[:half, :], mesh, part(weight_ref, 4)[...])
+    send_ref[...] = dot(low_ref[...], part(weight_ref, 0)[...]).astype(BF16)
 
 
 def plan_edges(key_scalar, plan_ref, mesh_rows):
@@ -367,28 +365,44 @@
 
 
 def own_kernel(
-    plan_ref, key_ref, low_ref, high_ref, weight_ref, acc_ref, recv_ref, own_ref, later_ref, table_ref
+    plan_ref,
+    key_ref,
+    low_ref,
+    send_low_ref,
+    msg_ref,
+    line_ref,
+    self_ref,
+    weight_ref,
+    acc_ref,
+    recv_ref,
+    own_ref,
+    high_ref,
+    send_high_ref,
+    table_ref,
 ):
     mesh_rows, width = table_ref.shape
     half = mesh_rows // 2
+    codes = receiver_code(iota((half, msg_ref.shape[0]), 0) + half).astype(F32)
+    sums = dot(one_hot(line_ref[0:1, :] == codes), msg_ref[...])
+    mesh = part(weight_ref, 5)[half:, :]
+    high_ref[...] = next_rows(sums, self_ref[half:, :], mesh, part(weight_ref, 4)[...])
+    send_high_ref[...] = dot(high_ref[...], part(weight_ref, 0)[...]).astype(BF16)
+    table_ref[:half, :] = send_low_ref[...]
+    table_ref[half:, :] = send_high_ref[...]
     acc_ref[...] = jnp.zeros_like(acc_ref)
     recv_ref[mesh_rows:, :] = jnp.zeros((SPAN, width), BF16)
-    later_ref[...] = high_ref[...]
     for start, mid_ref in ((0, low_ref), (half, high_ref)):
         here = slice(start, start + half)
         mid = mid_ref[...]
-        table_ref[here, :] = dot(mid, part(weight_ref, 0)[...]).astype(BF16)
         recv_ref[here, :] = dot(mid, part(weight_ref, 1)[...]).astype(BF16)
         own_ref[here, :] = dot(mid, part(weight_ref, 2)[...])
     edge_sums(0, plan_ref, key_ref, table_ref, recv_ref, acc_ref)
 
 
-def near_kernel(
-    plan_ref, acc_in_ref, key_ref, right_ref, left_ref, weight_ref, recv_ref, acc_ref, table_ref
-):
+def near_kernel(plan_ref, acc_in_ref, key_ref, right_ref, left_ref, recv_ref, acc_ref, table_ref):
     half = table_ref.shape[0] // 2
-    table_ref[:half, :] = dot(right_ref[...], part(weight_ref, 0)[...]).astype(BF16)
-    table_ref[half:, :] = dot(left_ref[...], part(weight_ref, 0)[...]).astype(BF16)
+    table_ref[:half, :] = right_ref[...]
+    table_ref[half:, :] = left_ref[...]
     edge_sums(1, plan_ref, key_ref, table_ref, recv_ref, acc_ref)
 
 
@@ -404,16 +418,15 @@
     high_ref,
     own_ref,
     out_hbm,
+    acc_ref,
     table_ref,
-    acc_ref,
     out_ref,
     sems,
 ):
     mesh_rows = table_ref.shape[0]
     half = mesh_rows // 2
-    acc_ref[...] = acc_in_ref[...]
-    table_ref[:half, :] = dot(right_ref[...], part(weight_ref, 0)[...]).astype(BF16)
-    table_ref[half:, :] = dot(left_ref[...], part(weight_ref, 0)[...]).astype(BF16)
+    table_ref[:half, :] = right_ref[...]
+    table_ref[half:, :] = left_ref[...]
     edge_sums(2, plan_ref, key_ref, table_ref, recv_ref, acc_ref)
     copies = []
     rows = mesh_rows // sems.shape[0]
@@ -484,7 +497,7 @@
             pltpu.VMEM((slots, WIDE), BF16),
             pltpu.VMEM((1, edges), I32),
             dma((5,)),
-            dma((4,)),
+            dma((1,)),
             dma((slots // SLOTS,)),
             dma,
         ],
@@ -513,12 +526,18 @@
         out_specs=[pl.BlockSpec(memory_space=pltpu.VMEM)] * 4 + [pl.BlockSpec(memory_space=pltpu.SMEM)],
     )
     embed = jnp.pad(embed_in, ((0, WIDE - feats), (0, 0)))
-    low, high, weights = call(
+    low, send_low, messages, line, weights = call(
         functools.partial(gather_kernel, feats),
-        (rows_half, rows_half, pltpu.VMEM((4 * width, width), BF16)),
+        (
+            rows_half,
+            rows_half,
+            pltpu.VMEM((slots, width), BF16),
+            pltpu.VMEM((8, slots), F32),
+            pltpu.VMEM((6 * width, width), BF16),
+        ),
         (mesh_nodes, node_agg, edge_send, edge_recv, out_self, out_agg),
         (arrived, embed, fold, proj, own),
-        scratch=[rows_wide, rows, weight, dma((6,))],
+        scratch=[pltpu.VMEM((half, width), F32), dma((6,))],
     )
 
     forward = [(i, (i + 1) % faces) for i in range(faces)]
@@ -527,34 +546,36 @@
     def neighbours(rows):
         return lax.ppermute(rows, "face", backward), lax.ppermute(rows, "face", forward)
 
-    near = neighbours(low)
-    acc, recv, own, later = call(
+    near = neighbours(send_low)
+    acc, recv, own, high, send_high = call(
         own_kernel,
-        (sums, pltpu.VMEM((mesh_rows + SPAN, width), BF16), rows_wide, rows_half),
+        (sums, pltpu.VMEM((mesh_rows + SPAN, width), BF16), rows_wide, rows_half, rows_half),
         (),
-        (keys, low, high, weights),
+        (keys, low, send_low, messages, line, own, weights),
         scratch=[rows],
         smem=(plan,),
     )
-    far = neighbours(later)
+    far = neighbours(send_high)
     acc = call(
         near_kernel,
         sums,
         (),
-        (acc, keys, *near, weights, recv),
+        (acc, keys, *near, recv),
         scratch=[rows],
         smem=(plan,),
         aliases={1: 0},
     )
-    return call(
+    out, _ = call(
         far_kernel,
-        jax.ShapeDtypeStruct((mesh_rows, width), F32),
+        (jax.ShapeDtypeStruct((mesh_rows, width), F32), sums),
         (),
         (acc, keys, *far, weights, recv, low, high, own),
-        scratch=[rows, sums, rows_wide, dma((4,))],
-        out_specs=there,
+        scratch=[rows, rows_wide, dma((4,))],
+        out_specs=(there, pl.BlockSpec(memory_space=pltpu.VMEM)),
         smem=(plan,),
-    )
+        aliases={1: 1},
+    )
+    return out
 
 
 def solution(mesh):

time: 64.4 us -> 64.2 us (level)
  waiting for transfers between devices: 11.9 us -> 14.5 us
  starting transfers between devices: 17.2 us -> 15.2 us
  Pallas kernels: 28.7 us -> 27.5 us
    ppermute x2, starting transfers between devices: 5.03 us -> 3.11 us  [neighbours(): lax.ppermute(rows, 'face', backward)]
    ppermute x2, waiting for transfers between devices: 0.01 us -> 1.3 us  [neighbours(): lax.ppermute(rows, 'face', backward)]
    ppermute x2, waiting for transfers between devices: 1.76 us -> 2.98 us  [neighbours(): lax.ppermute(rows, 'face', forward)]
    pallas_call x6, Pallas kernels: 28.7 us -> 27.5 us  [call(): pl.pallas_call(kernel, out_shape=outs, in_specs=[spec(space) for space in...]
  transfers between devices with their start and end apart: 5 -> 5, of which waited for: 2 -> 4; matrix products, arithmetic and copies ran while one was open for 9% -> 9% of each run, Pallas kernels for 18% -> 19%
where the time goes in v3:
time: 64.2 us; the launch traced here: 62.9 us
  Pallas kernels  27.5 us (43%)
  starting transfers between devices  15.2 us (24%)
  waiting for transfers between devices  14.5 us (23%)
  other arithmetic  5.53 us (9%)
    pallas_call x6, Pallas kernels, call(): pl.pallas_call(kernel, out_shape=outs, in_specs=[spec(space) for space in...  27.5 us
    all_to_all x1, starting transfers between devices, body(): lax.all_to_all(packed.reshape(owners, slots // owners, WIDE), ('band', 'f...  11.5 us
    all_to_all x1, waiting for transfers between devices, body(): lax.all_to_all(packed.reshape(owners, slots // owners, WIDE), ('band', 'f...  10.2 us
    sort x1, other arithmetic, body(): keys = lax.sort(keys.reshape(edges), is_stable=False).reshape(1, edges)  5.53 us
    ppermute x2, starting transfers between devices, neighbours(): lax.ppermute(rows, 'face', backward)  3.11 us
    ppermute x2, waiting for transfers between devices, neighbours(): lax.ppermute(rows, 'face', forward)  2.98 us
    ppermute x2, waiting for transfers between devices, neighbours(): lax.ppermute(rows, 'face', backward)  1.3 us
  transfers between devices with their start and end apart: 5, of which 4 were waited for; matrix products, arithmetic and copies ran while one was open for 9% of the time, Pallas kernels for 19%

profile of v3, /device:TPU:1, one launch (start us, length us, event | category | flops | bytes accessed | tf_op | source)
XLA Modules:
  0.0 62.9 jit_solution(10839311086909035790)
XLA Ops:
  0.0 0.0 copy-start
  0.0 4.9 %shard_map.163 = (bf16[2048,256]{1,0:T(8,128)(2,1)}, s32[1,4096]{1,0:T(1,128)S(1)}) custom-call(bf16[227,2048]{1,0:T(8,128)(2,1)} %bitcast.7, s32[1,2048]{1,0:T(1,128)} %sender_hbm.1, s32[1,2048]{1,0:T(1,128)} %receiver_hbm.1, s32[1,128]{1,0:T(1,128)} %count_hbm.1, s32[1,4096]{1,0:T(1,128)} %from_hbm.1, s32[1,4096]{1,0:T(1,128)} %to_hbm.1), custom_call_target="tpu_custom_call" | custom-call | tf_op jit(solution)/shard_map/pallas_call | solution.py:79
  5.0 11.5 %all-to-all-start = ((bf16[128,16,256]{2,1,0:T(8,128)(2,1)}), bf16[128,16,256]{2,1,0:T(8,128)(2,1)S(1)}, u32[]{:S(2)}, u32[]{:S(2)}) async-start(bf16[128,16,256]{2,1,0:T(8,128)(2,1)} %bitcast.3), calls=%async_computation | async-start | bytes 2097152 | tf_op jit(solution)/shard_map/all_to_all | solution.py:507
  16.5 5.5 %sort.7 = s32[4096]{0:T(1024)} sort(s32[4096]{0:T(1024)S(1)} %bitcast.6), dimensions={0}, to_apply=%region_0.0 | sort | flops 49152 | bytes 32768 | tf_op jit(solution)/shard_map/sort | solution.py:506
  22.0 0.0 copy-done
  22.0 3.9 %shard_map.164 = (bf16[512,512]{1,0:T(8,128)(2,1)S(1)}, bf16[512,512]{1,0:T(8,128)(2,1)S(1)}, f32[512,512]{1,0:T(8,128)S(1)}, s32[1,5632]{1,0:T(1,128)S(1)}, s32[3,6]{1,0:T(4,128)S(1)}) custom-call(bf16[512,512]{1,0:T(8,128)(2,1)} %embed_out_hbm.1, bf16[512,512]{1,0:T(8,128)(2,1)} %proj_grid_hbm.1, bf16[512,512]{1,0:T(8,128)(2,1)} %mesh_hbm.3, ...), custom_call_target="tpu_custom_call" | custom-call | tf_op jit(solution)/shard_map/pallas_call | solution.py:79
  25.9 10.2 %all-to-all-done = bf16[128,16,256]{2,1,0:T(8,128)(2,1)S(1)} async-done(((bf16[128,16,256]{2,1,0:T(8,128)(2,1)}), bf16[128,16,256]{2,1,0:T(8,128)(2,1)S(1)}, u32[]{:S(2)}, u32[]{:S(2)}) %all-to-all-start) | async-done | bytes 1048608 | tf_op jit(solution)/shard_map/all_to_all | solution.py:507
  36.1 5.5 %shard_map.165 = (bf16[256,512]{1,0:T(8,128)(2,1)S(1)}, bf16[256,512]{1,0:T(8,128)(2,1)S(1)}, bf16[2048,512]{1,0:T(8,128)(2,1)S(1)}, f32[8,2048]{1,0:T(8,128)S(1)}, bf16[3072,512]{1,0:T(8,128)(2,1)S(1)}) custom-call(bf16[512,512]{1,0:T(8,128)(2,1)} %mesh_hbm.3, bf16[512,512]{1,0:T(8,128)(2,1)} %node_agg_hbm.1, bf16[512,512]{1,0:T(8,128)(2,1)} %edge_send_hbm.1, ...), custom_call_target="tpu_custom_call" | custom-call | tf_op jit(solution)/shard_map/pallas_call | solution.py:79
  41.6 0.9 %collective-permute-start = (bf16[256,512]{1,0:T(8,128)(2,1)S(1)}, bf16[256,512]{1,0:T(8,128)(2,1)S(1)}, u32[]{:S(2)}, u32[]{:S(2)}) collective-permute-start(bf16[256,512]{1,0:T(8,128)(2,1)S(1)} %get-tuple-element.31.send_low_ref), channel_id=1, source_target_pairs={{1,0},{2,1},{3,2},{0,3},{5,4},{6,5},{7,6},{4,7},{9,8},{10,9},{11,1... | collective-permute-start | bytes 786440 | tf_op jit(solution)/shard_map/ppermute | solution.py:547
  42.6 0.6 collective-permute-start.1
  43.2 5.0 %shard_map.166 = (f32[768,512]{1,0:T(8,128)S(1)}, bf16[768,512]{1,0:T(8,128)(2,1)S(1)}, f32[512,512]{1,0:T(8,128)S(1)}, bf16[256,512]{1,0:T(8,128)(2,1)S(1)}, bf16[256,512]{1,0:T(8,128)(2,1)S(1)}) custom-call(s32[3,6]{1,0:T(4,128)S(1)} %get-tuple-element.24.plan_ref, s32[1,5632]{1,0:T(1,128)S(1)} %get-tuple-element.25.key_ref, ...), custom_call_target="tpu_custom_call" | custom-call | tf_op jit(solution)/shard_map/pallas_call | solution.py:79
  48.2 2.2 %collective-permute-start.2 = (bf16[256,512]{1,0:T(8,128)(2,1)S(1)}, bf16[256,512]{1,0:T(8,128)(2,1)S(1)}, u32[]{:S(2)}, u32[]{:S(2)}) collective-permute-start(bf16[256,512]{1,0:T(8,128)(2,1)S(1)} %get-tuple-element.37), channel_id=1, source_target_pairs={{1,0},{2,1},{3,2},{0,3},{5,4},{6,5},{7,6},{4,7},{9,8},{10,9},{11,1... | collective-permute-start | bytes 786440 | tf_op jit(solution)/shard_map/ppermute | solution.py:547
  50.4 0.0 collective-permute-start.3
  50.4 0.0 collective-permute-done.right_ref
  50.4 0.3 collective-permute-done.1.left_ref
  50.6 3.2 %shard_map.167.acc_in_ref = f32[768,512]{1,0:T(8,128)S(1)} custom-call(s32[3,6]{1,0:T(4,128)S(1)} %get-tuple-element.24.plan_ref, f32[768,512]{1,0:T(8,128)S(1)} %get-tuple-element.35.acc_in_ref, s32[1,5632]{1,0:T(1,128)S(1)} %get-tuple-element.25.key_ref, bf16[256,512]{1,0:T(8,128)(2,1)S(1)} %collective-permute-done.right_ref, ...), custom_call_target="tpu_custom_call", output_to_operand_aliasing={{}: (1, {})} | custom-call | tf_op jit(solution)/shard_map/pallas_call | solution.py:79
  53.8 1.3 %collective-permute-done.2.right_ref = bf16[256,512]{1,0:T(8,128)(2,1)S(1)} collective-permute-done((bf16[256,512]{1,0:T(8,128)(2,1)S(1)}, bf16[256,512]{1,0:T(8,128)(2,1)S(1)}, u32[]{:S(2)}, u32[]{:S(2)}) %collective-permute-start.2) | collective-permute-done | bytes 262176 | tf_op jit(solution)/shard_map/ppermute | solution.py:547
  55.1 2.7 %collective-permute-done.3.left_ref = bf16[256,512]{1,0:T(8,128)(2,1)S(1)} collective-permute-done((bf16[256,512]{1,0:T(8,128)(2,1)S(1)}, bf16[256,512]{1,0:T(8,128)(2,1)S(1)}, u32[]{:S(2)}, u32[]{:S(2)}) %collective-permute-start.3) | collective-permute-done | bytes 262176 | tf_op jit(solution)/shard_map/ppermute | solution.py:547
  57.9 4.9 %shard_map.168 = (f32[512,512]{1,0:T(8,128)}, f32[768,512]{1,0:T(8,128)S(1)}) custom-call(s32[3,6]{1,0:T(4,128)S(1)} %get-tuple-element.24.plan_ref, f32[768,512]{1,0:T(8,128)S(1)} %shard_map.167.acc_in_ref, s32[1,5632]{1,0:T(1,128)S(1)} %get-tuple-element.25.key_ref, ...), custom_call_target="tpu_custom_call", output_to_operand_aliasing={{1}: (1, {})} | custom-call | tf_op jit(solution)/shard_map/pallas_call | solution.py:79
  (1 shorter events, 0.0 us)
Async XLA Ops:
  0.0 22.0 %copy-start = (bf16[227,512]{1,0:T(8,128)(2,1)S(1)}, bf16[227,512]{1,0:T(8,128)(2,1)}, u32[]{:S(2)}) copy-start(bf16[227,512]{1,0:T(8,128)(2,1)} %param.24) | copy-start | bytes 697348
  5.0 31.1 %all-to-all-start = ((bf16[128,16,256]{2,1,0:T(8,128)(2,1)}), bf16[128,16,256]{2,1,0:T(8,128)(2,1)S(1)}, u32[]{:S(2)}, u32[]{:S(2)}) async-start(bf16[128,16,256]{2,1,0:T(8,128)(2,1)} %bitcast.3), calls=%async_computation | async-start | bytes 2097152 | tf_op jit(solution)/shard_map/all_to_all | solution.py:507
  41.6 8.8 %collective-permute-start = (bf16[256,512]{1,0:T(8,128)(2,1)S(1)}, bf16[256,512]{1,0:T(8,128)(2,1)S(1)}, u32[]{:S(2)}, u32[]{:S(2)}) collective-permute-start(bf16[256,512]{1,0:T(8,128)(2,1)S(1)} %get-tuple-element.31.send_low_ref), channel_id=1, source_target_pairs={{1,0},{2,1},{3,2},{0,3},{5,4},{6,5},{7,6},{4,7},{9,8},{10,9},{11,1... | collective-permute-start | bytes 786440 | tf_op jit(solution)/shard_map/ppermute | solution.py:547
  42.6 8.1 %collective-permute-start.1 = (bf16[256,512]{1,0:T(8,128)(2,1)S(1)}, bf16[256,512]{1,0:T(8,128)(2,1)S(1)}, u32[]{:S(2)}, u32[]{:S(2)}) collective-permute-start(bf16[256,512]{1,0:T(8,128)(2,1)S(1)} %get-tuple-element.31.send_low_ref), channel_id=1, source_target_pairs={{0,1},{1,2},{2,3},{3,0},{4,5},{5,6},{6,7},{7,4},{8,9},{9,10},{10,1... | collective-permute-start | bytes 786440 | tf_op jit(solution)/shard_map/ppermute | solution.py:547
  48.2 6.9 %collective-permute-start.2 = (bf16[256,512]{1,0:T(8,128)(2,1)S(1)}, bf16[256,512]{1,0:T(8,128)(2,1)S(1)}, u32[]{:S(2)}, u32[]{:S(2)}) collective-permute-start(bf16[256,512]{1,0:T(8,128)(2,1)S(1)} %get-tuple-element.37), channel_id=1, source_target_pairs={{1,0},{2,1},{3,2},{0,3},{5,4},{6,5},{7,6},{4,7},{9,8},{10,9},{11,1... | collective-permute-start | bytes 786440 | tf_op jit(solution)/shard_map/ppermute | solution.py:547
  50.4 7.5 %collective-permute-start.3 = (bf16[256,512]{1,0:T(8,128)(2,1)S(1)}, bf16[256,512]{1,0:T(8,128)(2,1)S(1)}, u32[]{:S(2)}, u32[]{:S(2)}) collective-permute-start(bf16[256,512]{1,0:T(8,128)(2,1)S(1)} %get-tuple-element.37), channel_id=1, source_target_pairs={{0,1},{1,2},{2,3},{3,0},{4,5},{5,6},{6,7},{7,4},{8,9},{9,10},{10,1... | collective-permute-start | bytes 786440 | tf_op jit(solution)/shard_map/ppermute | solution.py:547

commit v4 on v3

--- a/solution.py
+++ b/solution.py
@@ -364,24 +364,21 @@
     lax.fori_loop(done, (last - origin + FEW - 1) // FEW, general, 0)
 
 
-def own_kernel(
-    plan_ref,
-    key_ref,
+def high_kernel(
     low_ref,
     send_low_ref,
     msg_ref,
     line_ref,
     self_ref,
     weight_ref,
-    acc_ref,
-    recv_ref,
-    own_ref,
     high_ref,
     send_high_ref,
     table_ref,
+    recv_ref,
+    own_ref,
 ):
-    mesh_rows, width = table_ref.shape
-    half = mesh_rows // 2
+    half, width = low_ref.shape
+    mesh_rows = 2 * half
     codes = receiver_code(iota((half, msg_ref.shape[0]), 0) + half).astype(F32)
     sums = dot(one_hot(line_ref[0:1, :] == codes), msg_ref[...])
     mesh = part(weight_ref, 5)[half:, :]
@@ -389,13 +386,16 @@
     send_high_ref[...] = dot(high_ref[...], part(weight_ref, 0)[...]).astype(BF16)
     table_ref[:half, :] = send_low_ref[...]
     table_ref[half:, :] = send_high_ref[...]
-    acc_ref[...] = jnp.zeros_like(acc_ref)
     recv_ref[mesh_rows:, :] = jnp.zeros((SPAN, width), BF16)
     for start, mid_ref in ((0, low_ref), (half, high_ref)):
         here = slice(start, start + half)
         mid = mid_ref[...]
         recv_ref[here, :] = dot(mid, part(weight_ref, 1)[...]).astype(BF16)
         own_ref[here, :] = dot(mid, part(weight_ref, 2)[...])
+
+
+def own_kernel(plan_ref, key_ref, table_ref, recv_ref, acc_ref):
+    acc_ref[...] = jnp.zeros_like(acc_ref)
     edge_sums(0, plan_ref, key_ref, table_ref, recv_ref, acc_ref)
 
 
@@ -547,15 +547,14 @@
         return lax.ppermute(rows, "face", backward), lax.ppermute(rows, "face", forward)
 
     near = neighbours(send_low)
-    acc, recv, own, high, send_high = call(
-        own_kernel,
-        (sums, pltpu.VMEM((mesh_rows + SPAN, width), BF16), rows_wide, rows_half, rows_half),
+    high, send_high, table, recv, own = call(
+        high_kernel,
+        (rows_half, rows_half, rows, pltpu.VMEM((mesh_rows + SPAN, width), BF16), rows_wide),
         (),
-        (keys, low, send_low, messages, line, own, weights),
-        scratch=[rows],
-        smem=(plan,),
+        (low, send_low, messages, line, own, weights),
     )
     far = neighbours(send_high)
+    acc = call(own_kernel, sums, (), (keys, table, recv), smem=(plan,))
     acc = call(
         near_kernel,
         sums,

time: 64.2 us -> 61.2 us (0.953); the launches traced: 62.9 us -> 61 us
  waiting for transfers between devices: 14.5 us -> 10.5 us
  starting transfers between devices: 15.2 us -> 17 us
    ppermute x2, waiting for transfers between devices: 2.98 us -> 0.36 us  [neighbours(): lax.ppermute(rows, 'face', forward)]
    ppermute x2, starting transfers between devices: 3.11 us -> 5.04 us  [neighbours(): lax.ppermute(rows, 'face', backward)]
    ppermute x2, waiting for transfers between devices: 1.3 us -> 0.01 us  [neighbours(): lax.ppermute(rows, 'face', backward)]
    pallas_call x6 -> x7, Pallas kernels: 27.5 us -> 27.6 us  [call(): pl.pallas_call(kernel, out_shape=outs, in_specs=[spec(space) for space in...]
  transfers between devices with their start and end apart: 5 -> 5, of which waited for: 4 -> 2; matrix products, arithmetic and copies ran while one was open for 9% -> 9% of each run, Pallas kernels for 19% -> 20%
where the time goes in v4:
time: 61.2 us; the launch traced here: 61 us
  Pallas kernels  27.6 us (45%)
  starting transfers between devices  17 us (28%)
  waiting for transfers between devices  10.5 us (17%)
  other arithmetic  5.53 us (9%)
    pallas_call x7, Pallas kernels, call(): pl.pallas_call(kernel, out_shape=outs, in_specs=[spec(space) for space in...  27.6 us
    all_to_all x1, starting transfers between devices, body(): lax.all_to_all(packed.reshape(owners, slots // owners, WIDE), ('band', 'f...  11.5 us
    all_to_all x1, waiting for transfers between devices, body(): lax.all_to_all(packed.reshape(owners, slots // owners, WIDE), ('band', 'f...  10.2 us
    sort x1, other arithmetic, body(): keys = lax.sort(keys.reshape(edges), is_stable=False).reshape(1, edges)  5.53 us
    ppermute x2, starting transfers between devices, neighbours(): lax.ppermute(rows, 'face', backward)  5.04 us
  transfers between devices with their start and end apart: 5, of which 2 were waited for; matrix products, arithmetic and copies ran while one was open for 9% of the time, Pallas kernels for 20%

profile of v4, /device:TPU:1, one launch (start us, length us, event | category | flops | bytes accessed | tf_op | source)
XLA Modules:
  0.0 61.0 jit_solution(5939124928375511512)
XLA Ops:
  0.0 0.0 copy-start
  0.0 4.9 %shard_map.163 = (bf16[2048,256]{1,0:T(8,128)(2,1)}, s32[1,4096]{1,0:T(1,128)S(1)}) custom-call(bf16[227,2048]{1,0:T(8,128)(2,1)} %bitcast.7, s32[1,2048]{1,0:T(1,128)} %sender_hbm.1, s32[1,2048]{1,0:T(1,128)} %receiver_hbm.1, s32[1,128]{1,0:T(1,128)} %count_hbm.1, s32[1,4096]{1,0:T(1,128)} %from_hbm.1, s32[1,4096]{1,0:T(1,128)} %to_hbm.1), custom_call_target="tpu_custom_call" | custom-call | tf_op jit(solution)/shard_map/pallas_call | solution.py:79
  5.0 11.5 %all-to-all-start = ((bf16[128,16,256]{2,1,0:T(8,128)(2,1)}), bf16[128,16,256]{2,1,0:T(8,128)(2,1)S(1)}, u32[]{:S(2)}, u32[]{:S(2)}) async-start(bf16[128,16,256]{2,1,0:T(8,128)(2,1)} %bitcast.3), calls=%async_computation | async-start | bytes 2097152 | tf_op jit(solution)/shard_map/all_to_all | solution.py:507
  16.5 5.5 %sort.7 = s32[4096]{0:T(1024)} sort(s32[4096]{0:T(1024)S(1)} %bitcast.6), dimensions={0}, to_apply=%region_0.0 | sort | flops 49152 | bytes 32768 | tf_op jit(solution)/shard_map/sort | solution.py:506
  22.0 0.0 copy-done
  22.0 3.9 %shard_map.164 = (bf16[512,512]{1,0:T(8,128)(2,1)S(1)}, bf16[512,512]{1,0:T(8,128)(2,1)S(1)}, f32[512,512]{1,0:T(8,128)S(1)}, s32[1,5632]{1,0:T(1,128)S(1)}, s32[3,6]{1,0:T(4,128)S(1)}) custom-call(bf16[512,512]{1,0:T(8,128)(2,1)} %embed_out_hbm.1, bf16[512,512]{1,0:T(8,128)(2,1)} %proj_grid_hbm.1, bf16[512,512]{1,0:T(8,128)(2,1)} %mesh_hbm.3, ...), custom_call_target="tpu_custom_call" | custom-call | tf_op jit(solution)/shard_map/pallas_call | solution.py:79
  25.9 10.2 %all-to-all-done = bf16[128,16,256]{2,1,0:T(8,128)(2,1)S(1)} async-done(((bf16[128,16,256]{2,1,0:T(8,128)(2,1)}), bf16[128,16,256]{2,1,0:T(8,128)(2,1)S(1)}, u32[]{:S(2)}, u32[]{:S(2)}) %all-to-all-start) | async-done | bytes 1048608 | tf_op jit(solution)/shard_map/all_to_all | solution.py:507
  36.1 5.5 %shard_map.165 = (bf16[256,512]{1,0:T(8,128)(2,1)S(1)}, bf16[256,512]{1,0:T(8,128)(2,1)S(1)}, bf16[2048,512]{1,0:T(8,128)(2,1)S(1)}, f32[8,2048]{1,0:T(8,128)S(1)}, bf16[3072,512]{1,0:T(8,128)(2,1)S(1)}) custom-call(bf16[512,512]{1,0:T(8,128)(2,1)} %mesh_hbm.3, bf16[512,512]{1,0:T(8,128)(2,1)} %node_agg_hbm.1, bf16[512,512]{1,0:T(8,128)(2,1)} %edge_send_hbm.1, ...), custom_call_target="tpu_custom_call" | custom-call | tf_op jit(solution)/shard_map/pallas_call | solution.py:79
  41.5 0.4 collective-permute-start.1
  41.9 2.4 %collective-permute-start = (bf16[256,512]{1,0:T(8,128)(2,1)S(1)}, bf16[256,512]{1,0:T(8,128)(2,1)S(1)}, u32[]{:S(2)}, u32[]{:S(2)}) collective-permute-start(bf16[256,512]{1,0:T(8,128)(2,1)S(1)} %get-tuple-element.31.send_low_ref), channel_id=1, source_target_pairs={{1,0},{2,1},{3,2},{0,3},{5,4},{6,5},{7,6},{4,7},{9,8},{10,9},{11,1... | collective-permute-start | bytes 786440 | tf_op jit(solution)/shard_map/ppermute | solution.py:547
  44.3 1.8 %shard_map.166 = (bf16[256,512]{1,0:T(8,128)(2,1)S(1)}, bf16[256,512]{1,0:T(8,128)(2,1)S(1)}, bf16[512,512]{1,0:T(8,128)(2,1)S(1)}, bf16[768,512]{1,0:T(8,128)(2,1)S(1)}, f32[512,512]{1,0:T(8,128)S(1)}) custom-call(bf16[256,512]{1,0:T(8,128)(2,1)S(1)} %get-tuple-element.30.low_ref, bf16[256,512]{1,0:T(8,128)(2,1)S(1)} %get-tuple-element.31.send_low_ref, ...), custom_call_target="tpu_custom_call" | custom-call | tf_op jit(solution)/shard_map/pallas_call | solution.py:79
  46.1 0.1 collective-permute-start.3
  46.2 2.7 %collective-permute-start.2 = (bf16[256,512]{1,0:T(8,128)(2,1)S(1)}, bf16[256,512]{1,0:T(8,128)(2,1)S(1)}, u32[]{:S(2)}, u32[]{:S(2)}) collective-permute-start(bf16[256,512]{1,0:T(8,128)(2,1)S(1)} %get-tuple-element.37), channel_id=1, source_target_pairs={{1,0},{2,1},{3,2},{0,3},{5,4},{6,5},{7,6},{4,7},{9,8},{10,9},{11,1... | collective-permute-start | bytes 786440 | tf_op jit(solution)/shard_map/ppermute | solution.py:547
  48.8 3.4 %shard_map.167.acc_in_ref = f32[768,512]{1,0:T(8,128)S(1)} custom-call(s32[3,6]{1,0:T(4,128)S(1)} %get-tuple-element.24.plan_ref, s32[1,5632]{1,0:T(1,128)S(1)} %get-tuple-element.25.key_ref, bf16[512,512]{1,0:T(8,128)(2,1)S(1)} %get-tuple-element.35.table_ref, bf16[768,512]{1,0:T(8,128)(2,1)S(1)} %get-tuple-element.36.recv_ref), custom_call_target="tpu_custom_call" | custom-call | tf_op jit(solution)/shard_map/pallas_call | solution.py:79
  52.3 0.0 collective-permute-done.1.left_ref
  52.3 0.0 collective-permute-done.right_ref
  52.3 3.2 %shard_map.168.acc_in_ref = f32[768,512]{1,0:T(8,128)S(1)} custom-call(s32[3,6]{1,0:T(4,128)S(1)} %get-tuple-element.24.plan_ref, f32[768,512]{1,0:T(8,128)S(1)} %shard_map.167.acc_in_ref, s32[1,5632]{1,0:T(1,128)S(1)} %get-tuple-element.25.key_ref, bf16[256,512]{1,0:T(8,128)(2,1)S(1)} %collective-permute-done.right_ref, ...), custom_call_target="tpu_custom_call", output_to_operand_aliasing={{}: (1, {})} | custom-call | tf_op jit(solution)/shard_map/pallas_call | solution.py:79
  55.5 0.4 collective-permute-done.3.left_ref
  55.9 0.0 collective-permute-done.2.right_ref
  55.9 4.9 %shard_map.169 = (f32[512,512]{1,0:T(8,128)}, f32[768,512]{1,0:T(8,128)S(1)}) custom-call(s32[3,6]{1,0:T(4,128)S(1)} %get-tuple-element.24.plan_ref, f32[768,512]{1,0:T(8,128)S(1)} %shard_map.168.acc_in_ref, s32[1,5632]{1,0:T(1,128)S(1)} %get-tuple-element.25.key_ref, ...), custom_call_target="tpu_custom_call", output_to_operand_aliasing={{1}: (1, {})} | custom-call | tf_op jit(solution)/shard_map/pallas_call | solution.py:79
  (1 shorter events, 0.0 us)
Async XLA Ops:
  0.0 22.0 %copy-start = (bf16[227,512]{1,0:T(8,128)(2,1)S(1)}, bf16[227,512]{1,0:T(8,128)(2,1)}, u32[]{:S(2)}) copy-start(bf16[227,512]{1,0:T(8,128)(2,1)} %param.24) | copy-start | bytes 697348
  5.0 31.1 %all-to-all-start = ((bf16[128,16,256]{2,1,0:T(8,128)(2,1)}), bf16[128,16,256]{2,1,0:T(8,128)(2,1)S(1)}, u32[]{:S(2)}, u32[]{:S(2)}) async-start(bf16[128,16,256]{2,1,0:T(8,128)(2,1)} %bitcast.3), calls=%async_computation | async-start | bytes 2097152 | tf_op jit(solution)/shard_map/all_to_all | solution.py:507
  41.5 10.7 %collective-permute-start.1 = (bf16[256,512]{1,0:T(8,128)(2,1)S(1)}, bf16[256,512]{1,0:T(8,128)(2,1)S(1)}, u32[]{:S(2)}, u32[]{:S(2)}) collective-permute-start(bf16[256,512]{1,0:T(8,128)(2,1)S(1)} %get-tuple-element.31.send_low_ref), channel_id=1, source_target_pairs={{0,1},{1,2},{2,3},{3,0},{4,5},{5,6},{6,7},{7,4},{8,9},{9,10},{10,1... | collective-permute-start | bytes 786440 | tf_op jit(solution)/shard_map/ppermute | solution.py:547
  41.9 10.4 %collective-permute-start = (bf16[256,512]{1,0:T(8,128)(2,1)S(1)}, bf16[256,512]{1,0:T(8,128)(2,1)S(1)}, u32[]{:S(2)}, u32[]{:S(2)}) collective-permute-start(bf16[256,512]{1,0:T(8,128)(2,1)S(1)} %get-tuple-element.31.send_low_ref), channel_id=1, source_target_pairs={{1,0},{2,1},{3,2},{0,3},{5,4},{6,5},{7,6},{4,7},{9,8},{10,9},{11,1... | collective-permute-start | bytes 786440 | tf_op jit(solution)/shard_map/ppermute | solution.py:547
  46.1 9.8 %collective-permute-start.3 = (bf16[256,512]{1,0:T(8,128)(2,1)S(1)}, bf16[256,512]{1,0:T(8,128)(2,1)S(1)}, u32[]{:S(2)}, u32[]{:S(2)}) collective-permute-start(bf16[256,512]{1,0:T(8,128)(2,1)S(1)} %get-tuple-element.37), channel_id=1, source_target_pairs={{0,1},{1,2},{2,3},{3,0},{4,5},{5,6},{6,7},{7,4},{8,9},{9,10},{10,1... | collective-permute-start | bytes 786440 | tf_op jit(solution)/shard_map/ppermute | solution.py:547
  46.2 9.7 %collective-permute-start.2 = (bf16[256,512]{1,0:T(8,128)(2,1)S(1)}, bf16[256,512]{1,0:T(8,128)(2,1)S(1)}, u32[]{:S(2)}, u32[]{:S(2)}) collective-permute-start(bf16[256,512]{1,0:T(8,128)(2,1)S(1)} %get-tuple-element.37), channel_id=1, source_target_pairs={{1,0},{2,1},{3,2},{0,3},{5,4},{6,5},{7,6},{4,7},{9,8},{10,9},{11,1... | collective-permute-start | bytes 786440 | tf_op jit(solution)/shard_map/ppermute | solution.py:547

commit v5 on v4

--- a/solution.py
+++ b/solution.py
@@ -14,10 +14,9 @@
 DEAD = 1024
 SLOTS = 1024
 ARRIVED = 1024
+PARTS = 6
 BLOCKS = 3
-EDGES = 512
-PARTS = 3
-FEW = 256
+EDGES = 256
 SPAN = 256
 ALIGN = 16
 VMEM_BYTES = 40 * 1024 * 1024
@@ -137,10 +136,10 @@
     row = lax.rem(source, mesh_rows)
     second = row // half
     mine = (source >= mesh_rows) & (source < 2 * mesh_rows)
-    side = jnp.where(source < mesh_rows, half, 0)
-    part = jnp.where(mine, 0, 1 + second)
-    place = jnp.where(mine, row, row - second * half + side)
-    key_ref[...] = (part * mesh_rows + to_ref[...]) * mesh_rows + place
+    left = (source < mesh_rows).astype(I32)
+    part = jnp.where(mine, second, 2 + 2 * second + left)
+    place = row - second * half
+    key_ref[...] = (part * mesh_rows + to_ref[...]) * half + place
     key_copy = pltpu.make_async_copy(key_ref, key_hbm, key_sem)
     key_copy.start()
     counts = jnp.broadcast_to(count_ref[...].astype(F32).astype(BF16), (8, owners))
@@ -194,12 +193,15 @@
     proj_ref,
     self_ref,
     key_ref,
+    line_ref,
+    column_ref,
     plan_ref,
     embed_out_ref,
     proj_grid_ref,
     mesh_ref,
     proj_mesh_ref,
     node_self_ref,
+    place_ref,
     key_scalar,
     sems,
 ):
@@ -217,7 +219,7 @@
     key_ref[:, edges:] = jnp.full((1, key_ref.shape[1] - edges), -1, I32)
     for copy in copies:
         copy.wait()
-    plan_edges(key_scalar, plan_ref, mesh_ref.shape[0])
+    plan_edges(key_scalar, key_ref, plan_ref, line_ref, place_ref, column_ref, mesh_ref.shape[0])
     fold_ref[...] = dot(embed_out_ref[...], proj_grid_ref[...]).astype(BF16)
     mesh = mesh_ref[...]
     proj_ref[...] = dot(mesh, proj_mesh_ref[...]).astype(BF16)
@@ -254,7 +256,7 @@
     copies = start_copies([(hbm, part(weight_ref, i)) for i, hbm in enumerate(sources)], sems)
     slots = x_ref.shape[0]
     mesh_rows = self_ref.shape[0]
-    half = mesh_rows // 2
+    early = low_ref.shape[0]
     lanes = feats // 128 * 128
     along = one_hot(iota((8, WIDE - lanes), 1) == feats - lanes)
     sum_ref[...] = jnp.zeros_like(sum_ref)
@@ -270,20 +272,21 @@
         msg_ref[here, :] = message
         line = dot_rows(along, x[:, lanes:])
         line_ref[:, here] = line
-        codes = receiver_code(iota((half, ARRIVED), 0)).astype(F32)
+        codes = receiver_code(iota((early, ARRIVED), 0)).astype(F32)
         sum_ref[...] += dot(one_hot(line[0:1, :] == codes), message)
         return carry
 
     lax.fori_loop(0, slots // ARRIVED, step, 0)
     for copy in copies:
         copy.wait()
-    mesh = part(weight_ref, 5)[:half, :]
-    low_ref[...] = next_rows(sum_ref[...], self_ref[:half, :], mesh, part(weight_ref, 4)[...])
+    mesh = part(weight_ref, 5)[:early, :]
+    low_ref[...] = next_rows(sum_ref[...], self_ref[:early, :], mesh, part(weight_ref, 4)[...])
     send_ref[...] = dot(low_ref[...], part(weight_ref, 0)[...]).astype(BF16)
 
 
-def plan_edges(key_scalar, plan_ref, mesh_rows):
+def plan_edges(key_scalar, key_ref, plan_ref, line_ref, place_ref, column_ref, mesh_rows):
     edges = key_scalar.shape[1]
+    half = mesh_rows // 2
 
     def first_at_least(limit):
         def halve(_, ends):
@@ -300,68 +303,97 @@
         return lax.fori_loop(0, edges.bit_length(), halve, ends)[0]
 
     first = jnp.int32(0)
+    lines = []
+    places = []
     for index in range(PARTS):
         last = jnp.int32(edges)
         if index < PARTS - 1:
-            last = first_at_least((index + 1) * mesh_rows * mesh_rows)
-        origin = first // 128 * 128
-
-        def receiver_at(place):
-            key = key_scalar[0, jnp.clip(place, 0, edges - 1)]
-            return key // mesh_rows - index * mesh_rows
-
-        narrow = jnp.bool_(True)
+            last = first_at_least((index + 1) * mesh_rows * half)
+        share = (last - first + BLOCKS - 1) // BLOCKS
+
+        def receiver_at(position):
+            key = key_scalar[0, jnp.clip(position, 0, edges - 1)]
+            return key // half - index * mesh_rows
+
+        narrow = share <= EDGES
         for block in range(BLOCKS):
-            start = origin + block * EDGES
-            low = receiver_at(jnp.maximum(start, first))
-            high = receiver_at(jnp.minimum(start + EDGES, last) - 1)
-            empty = start >= last
-            base = jnp.where(empty, 0, low // ALIGN * ALIGN)
-            narrow = narrow & (empty | (high - base < SPAN))
+            start = jnp.minimum(first + block * share, last)
+            end = jnp.minimum(start + share, last)
+            empty = start >= end
+            base = jnp.where(empty, 0, receiver_at(start) // ALIGN * ALIGN)
+            narrow = narrow & (empty | (receiver_at(end - 1) - base < SPAN))
             plan_ref[index, 3 + block] = base
-        plan_ref[index, 0] = origin
+            begin = pl.multiple_of(start // 128 * 128, 128)
+            width = EDGES + 128
+            keys = jnp.broadcast_to(key_ref[:, pl.ds(begin, width)], (8, width))
+            keys = pltpu.roll(keys, lax.rem(width - (start - begin), width), axis=1)[0:1, :EDGES]
+            live = iota((1, EDGES), 1) < end - start
+            receiver = lax.div(keys, half) - index * mesh_rows - base
+            lines.append(jnp.where(live, receiver, -mesh_rows))
+            places.append(keys & (half - 1))
+        plan_ref[index, 0] = first
         plan_ref[index, 1] = last
         plan_ref[index, 2] = narrow.astype(I32)
         first = last
-
-
-def edge_sums(index, plan_ref, key_ref, table_ref, recv_ref, acc_ref):
-    mesh_rows = table_ref.shape[0]
-    origin = plan_ref[index, 0]
-    last = plan_ref[index, 1]
-    narrow = plan_ref[index, 2] == 1
-
-    def split(start, count):
-        keys = key_ref[:, pl.ds(pl.multiple_of(start, 128), count)]
-        column = as_column(keys)
-        place = column & (mesh_rows - 1)
-        receiver = lax.div(column, mesh_rows) - index * mesh_rows
-        line = lax.div(keys, mesh_rows) - index * mesh_rows
-        line = jnp.where((keys < 0) | (line < 0) | (line >= mesh_rows), -mesh_rows, line)
-        return place, receiver, line
+    rows = line_ref.shape[0]
+    for block in range(PARTS * BLOCKS):
+        line_ref[block : block + 1, :] = lines[block]
+        place_ref[block : block + 1, :] = places[block]
+    for block in range(PARTS * BLOCKS, rows):
+        line_ref[block : block + 1, :] = jnp.full((1, EDGES), -mesh_rows, I32)
+        place_ref[block : block + 1, :] = jnp.zeros((1, EDGES), I32)
+    column_ref[:, :rows] = line_ref[...].T
+    column_ref[:, rows:] = place_ref[...].T
+
+
+def edge_sums(parts, plan_refs, recv_ref, acc_ref):
+    plan_ref, key_ref, line_ref, column_ref = plan_refs
+    half = parts[0][1].shape[0]
+    mesh_rows = 2 * half
+    rows = line_ref.shape[0]
+    narrow = functools.reduce(jnp.logical_and, [plan_ref[index, 2] == 1 for index, _ in parts])
 
     @pl.when(narrow)
     def _():
-        for block in range(BLOCKS):
-            base = pl.multiple_of(plan_ref[index, 3 + block], ALIGN)
-            place, receiver, line = split(origin + block * EDGES, EDGES)
-            from_table = one_hot(place == iota((EDGES, mesh_rows), 1))
-            from_recv = one_hot(receiver - base == iota((EDGES, SPAN), 1))
-            reach = pl.ds(base, SPAN)
-            message = silu(dot(from_table, table_ref[...]) + dot(from_recv, recv_ref[reach, :]))
-            selector = one_hot(line - base == iota((SPAN, EDGES), 0))
-            acc_ref[reach, :] += dot(selector, message.astype(BF16))
-    def general(block, carry):
-        place, receiver, line = split(origin + block * FEW, FEW)
-        from_table = one_hot(place == iota((FEW, mesh_rows), 1))
-        from_recv = one_hot(receiver == iota((FEW, mesh_rows), 1))
-        message = silu(dot(from_table, table_ref[...]) + dot(from_recv, recv_ref[:mesh_rows, :]))
-        selector = one_hot(line == iota((mesh_rows, FEW), 0))
-        acc_ref[:mesh_rows, :] += dot(selector, message.astype(BF16))
-        return carry
-
-    done = jnp.where(narrow, BLOCKS * EDGES // FEW, 0)
-    lax.fori_loop(done, (last - origin + FEW - 1) // FEW, general, 0)
+        pending = []
+
+        def scatter():
+            row, reach, message = pending.pop(0)
+            selector = one_hot(line_ref[row : row + 1, :] == iota((SPAN, EDGES), 0))
+            acc_ref[reach, :] += dot(selector, message)
+
+        for index, table in parts:
+            for block in range(BLOCKS):
+                row = index * BLOCKS + block
+                reach = pl.ds(pl.multiple_of(plan_ref[index, 3 + block], ALIGN), SPAN)
+                receiver = column_ref[:, row : row + 1]
+                place = column_ref[:, rows + row : rows + row + 1]
+                from_table = one_hot(place == iota((EDGES, half), 1))
+                from_recv = one_hot(receiver == iota((EDGES, SPAN), 1))
+                pre = dot(from_table, table[...]) + dot(from_recv, recv_ref[reach, :])
+                if pending:
+                    scatter()
+                pending.append((row, reach, silu(pre).astype(BF16)))
+        scatter()
+
+    for index, table in parts:
+        origin = plan_ref[index, 0] // 128 * 128
+
+        def general(block, carry):
+            keys = key_ref[:, pl.ds(pl.multiple_of(origin + block * EDGES, 128), EDGES)]
+            column = as_column(keys)
+            receiver = lax.div(column, half) - index * mesh_rows
+            from_table = one_hot((column & (half - 1)) == iota((EDGES, half), 1))
+            from_recv = one_hot(receiver == iota((EDGES, mesh_rows), 1))
+            message = silu(dot(from_table, table[...]) + dot(from_recv, recv_ref[:mesh_rows, :]))
+            line = lax.div(keys, half) - index * mesh_rows
+            line = jnp.where((keys < 0) | (line < 0) | (line >= mesh_rows), -mesh_rows, line)
+            selector = one_hot(line == iota((mesh_rows, EDGES), 0))
+            acc_ref[:mesh_rows, :] += dot(selector, message.astype(BF16))
+            return carry
+
+        blocks = (plan_ref[index, 1] - origin + EDGES - 1) // EDGES
+        lax.fori_loop(0, jnp.where(narrow, 0, blocks), general, 0)
 
 
 def high_kernel(
@@ -377,39 +409,44 @@
     recv_ref,
     own_ref,
 ):
-    half, width = low_ref.shape
-    mesh_rows = 2 * half
-    codes = receiver_code(iota((half, msg_ref.shape[0]), 0) + half).astype(F32)
+    early, width = low_ref.shape
+    late = high_ref.shape[0]
+    mesh_rows = early + late
+    codes = receiver_code(iota((late, msg_ref.shape[0]), 0) + early).astype(F32)
     sums = dot(one_hot(line_ref[0:1, :] == codes), msg_ref[...])
-    mesh = part(weight_ref, 5)[half:, :]
-    high_ref[...] = next_rows(sums, self_ref[half:, :], mesh, part(weight_ref, 4)[...])
+    mesh = part(weight_ref, 5)[early:, :]
+    high_ref[...] = next_rows(sums, self_ref[early:, :], mesh, part(weight_ref, 4)[...])
     send_high_ref[...] = dot(high_ref[...], part(weight_ref, 0)[...]).astype(BF16)
-    table_ref[:half, :] = send_low_ref[...]
-    table_ref[half:, :] = send_high_ref[...]
+    table_ref[:early, :] = send_low_ref[...]
+    table_ref[early:, :] = send_high_ref[...]
     recv_ref[mesh_rows:, :] = jnp.zeros((SPAN, width), BF16)
-    for start, mid_ref in ((0, low_ref), (half, high_ref)):
-        here = slice(start, start + half)
+    for start, mid_ref in ((0, low_ref), (early, high_ref)):
+        here = slice(start, start + mid_ref.shape[0])
         mid = mid_ref[...]
         recv_ref[here, :] = dot(mid, part(weight_ref, 1)[...]).astype(BF16)
         own_ref[here, :] = dot(mid, part(weight_ref, 2)[...])
 
 
-def own_kernel(plan_ref, key_ref, table_ref, recv_ref, acc_ref):
+def own_kernel(plan_ref, key_ref, line_ref, column_ref, table_ref, recv_ref, acc_ref):
+    half = table_ref.shape[0] // 2
     acc_ref[...] = jnp.zeros_like(acc_ref)
-    edge_sums(0, plan_ref, key_ref, table_ref, recv_ref, acc_ref)
-
-
-def near_kernel(plan_ref, acc_in_ref, key_ref, right_ref, left_ref, recv_ref, acc_ref, table_ref):
-    half = table_ref.shape[0] // 2
-    table_ref[:half, :] = right_ref[...]
-    table_ref[half:, :] = left_ref[...]
-    edge_sums(1, plan_ref, key_ref, table_ref, recv_ref, acc_ref)
+    parts = [(0, table_ref.at[:half, :]), (1, table_ref.at[half:, :])]
+    edge_sums(parts, (plan_ref, key_ref, line_ref, column_ref), recv_ref, acc_ref)
+
+
+def near_kernel(
+    plan_ref, acc_in_ref, key_ref, line_ref, column_ref, right_ref, left_ref, recv_ref, acc_ref
+):
+    parts = [(2, right_ref), (3, left_ref)]
+    edge_sums(parts, (plan_ref, key_ref, line_ref, column_ref), recv_ref, acc_ref)
 
 
 def far_kernel(
     plan_ref,
     acc_in_ref,
     key_ref,
+    line_ref,
+    column_ref,
     right_ref,
     left_ref,
     weight_ref,
@@ -419,23 +456,20 @@
     own_ref,
     out_hbm,
     acc_ref,
-    table_ref,
     out_ref,
     sems,
 ):
-    mesh_rows = table_ref.shape[0]
-    half = mesh_rows // 2
-    table_ref[:half, :] = right_ref[...]
-    table_ref[half:, :] = left_ref[...]
-    edge_sums(2, plan_ref, key_ref, table_ref, recv_ref, acc_ref)
+    early = low_ref.shape[0]
+    mesh_rows = early + high_ref.shape[0]
+    parts = [(4, right_ref), (5, left_ref)]
+    edge_sums(parts, (plan_ref, key_ref, line_ref, column_ref), recv_ref, acc_ref)
     copies = []
     rows = mesh_rows // sems.shape[0]
     for index in range(sems.shape[0]):
         start = index * rows
         here = slice(start, start + rows)
         update = own_ref[here, :] + dot(acc_ref[here, :].astype(BF16), part(weight_ref, 3)[...])
-        mid_ref = low_ref if start < half else high_ref
-        mid = mid_ref[start % half : start % half + rows, :]
+        mid = low_ref[here, :] if start < early else high_ref[start - early : start - early + rows, :]
         values = mid.astype(F32) + silu(update)
         mean = jnp.mean(values, axis=-1, keepdims=True)
         centered = values - mean
@@ -477,6 +511,8 @@
     weight = pltpu.VMEM((width, width), BF16)
     rows = pltpu.VMEM((mesh_rows, width), BF16)
     rows_half = pltpu.VMEM((half, width), BF16)
+    lines = pltpu.VMEM((PARTS * BLOCKS + -PARTS * BLOCKS % 8, EDGES), I32)
+    columns = pltpu.VMEM((EDGES, 2 * lines.shape[0]), I32)
     rows_wide = pltpu.VMEM((mesh_rows, width), F32)
     sums = pltpu.VMEM((mesh_rows + SPAN, width), F32)
 
@@ -511,22 +547,24 @@
         concat_axis=0,
         tiled=True,
     ).reshape(slots, WIDE)
-    fold, proj, own, keys, plan = call(
+    fold, proj, own, keys, line, column, plan = call(
         weights_kernel,
         (
             weight,
             rows,
             rows_wide,
-            pltpu.VMEM((1, edges + BLOCKS * EDGES), I32),
+            pltpu.VMEM((1, edges + 2 * EDGES), I32),
+            lines,
+            columns,
             jax.ShapeDtypeStruct((PARTS, 3 + BLOCKS), I32),
         ),
         (embed_out, proj_grid, mesh_nodes, proj_mesh, node_self, keys),
         (),
-        scratch=[weight] * 2 + [rows] + [weight] * 2 + [pltpu.SMEM((1, edges), I32), dma((7,))],
-        out_specs=[pl.BlockSpec(memory_space=pltpu.VMEM)] * 4 + [pl.BlockSpec(memory_space=pltpu.SMEM)],
+        scratch=[weight] * 2 + [rows] + [weight] * 2 + [lines, pltpu.SMEM((1, edges), I32), dma((7,))],
+        out_specs=[pl.BlockSpec(memory_space=pltpu.VMEM)] * 6 + [pl.BlockSpec(memory_space=pltpu.SMEM)],
     )
     embed = jnp.pad(embed_in, ((0, WIDE - feats), (0, 0)))
-    low, send_low, messages, line, weights = call(
+    low, send_low, messages, target, weights = call(
         functools.partial(gather_kernel, feats),
         (
             rows_half,
@@ -547,20 +585,19 @@
         return lax.ppermute(rows, "face", backward), lax.ppermute(rows, "face", forward)
 
     near = neighbours(send_low)
-    high, send_high, table, recv, own = call(
+    high, send_high, own_table, recv, own = call(
         high_kernel,
         (rows_half, rows_half, rows, pltpu.VMEM((mesh_rows + SPAN, width), BF16), rows_wide),
         (),
-        (low, send_low, messages, line, own, weights),
+        (low, send_low, messages, target, own, weights),
     )
     far = neighbours(send_high)
-    acc = call(own_kernel, sums, (), (keys, table, recv), smem=(plan,))
+    acc = call(own_kernel, sums, (), (keys, line, column, own_table, recv), smem=(plan,))
     acc = call(
         near_kernel,
         sums,
         (),
-        (acc, keys, *near, recv),
-        scratch=[rows],
+        (acc, keys, line, column, *near, recv),
         smem=(plan,),
         aliases={1: 0},
     )
@@ -568,8 +605,8 @@
         far_kernel,
         (jax.ShapeDtypeStruct((mesh_rows, width), F32), sums),
         (),
-        (acc, keys, *far, weights, recv, low, high, own),
-        scratch=[rows, rows_wide, dma((4,))],
+        (acc, keys, line, column, *far, weights, recv, low, high, own),
+        scratch=[rows_wide, dma((4,))],
         out_specs=(there, pl.BlockSpec(memory_space=pltpu.VMEM)),
         smem=(plan,),
         aliases={1: 1},

time: 61.2 us -> 60.5 us (0.989)
  Pallas kernels: 27.6 us -> 26.2 us
  local copies, waits for them, and re-layouts: 0.02 us -> 1.23 us
    all_to_all x1, waiting for transfers between devices: 10.2 us -> 8.13 us  [body(): lax.all_to_all(packed.reshape(owners, slots // owners, WIDE), ('band', 'f...]
    ppermute x2, waiting for transfers between devices: 0.36 us -> 1.91 us  [neighbours(): lax.ppermute(rows, 'face', forward)]
    pallas_call x7, Pallas kernels: 27.6 us -> 26.2 us  [call(): pl.pallas_call(kernel, out_shape=outs, in_specs=[spec(space) for space in...]
    unnamed x2 -> x10, local copies, waits for them, and re-layouts: 0.01 us -> 1.21 us
  transfers between devices with their start and end apart: 5 -> 5, of which waited for: 2 -> 2; matrix products, arithmetic and copies ran while one was open for 9% -> 9% of each run, Pallas kernels for 20% -> 19%
where the time goes in v5:
time: 60.5 us; the launch traced here: 60.3 us
  Pallas kernels  26.2 us (43%)
  starting transfers between devices  17 us (28%)
  waiting for transfers between devices  10 us (17%)
  other arithmetic  5.54 us (9%)
  local copies, waits for them, and re-layouts  1.23 us (2%)
    pallas_call x7, Pallas kernels, call(): pl.pallas_call(kernel, out_shape=outs, in_specs=[spec(space) for space in...  26.2 us
    all_to_all x1, starting transfers between devices, body(): lax.all_to_all(packed.reshape(owners, slots // owners, WIDE), ('band', 'f...  11.5 us
    all_to_all x1, waiting for transfers between devices, body(): lax.all_to_all(packed.reshape(owners, slots // owners, WIDE), ('band', 'f...  8.13 us
    sort x1, other arithmetic, body(): keys = lax.sort(keys.reshape(edges), is_stable=False).reshape(1, edges)  5.54 us
    ppermute x2, starting transfers between devices, neighbours(): lax.ppermute(rows, 'face', backward)  5.01 us
    ppermute x2, waiting for transfers between devices, neighbours(): lax.ppermute(rows, 'face', forward)  1.91 us
  transfers between devices with their start and end apart: 5, of which 2 were waited for; matrix products, arithmetic and copies ran while one was open for 9% of the time, Pallas kernels for 19%

profile of v5, /device:TPU:1, one launch (start us, length us, event | category | flops | bytes accessed | tf_op | source)
XLA Modules:
  0.0 60.3 jit_solution(16832201236076413827)
XLA Ops:
  0.0 4.9 %shard_map.163 = (bf16[2048,256]{1,0:T(8,128)(2,1)}, s32[1,4096]{1,0:T(1,128)S(1)}) custom-call(bf16[227,2048]{1,0:T(8,128)(2,1)} %bitcast.7, s32[1,2048]{1,0:T(1,128)} %sender_hbm.1, s32[1,2048]{1,0:T(1,128)} %receiver_hbm.1, s32[1,128]{1,0:T(1,128)} %count_hbm.1, s32[1,4096]{1,0:T(1,128)} %from_hbm.1, s32[1,4096]{1,0:T(1,128)} %to_hbm.1), custom_call_target="tpu_custom_call" | custom-call | tf_op jit(solution)/shard_map/pallas_call | solution.py:78
  5.0 11.5 %all-to-all-start = ((bf16[128,16,256]{2,1,0:T(8,128)(2,1)}), bf16[128,16,256]{2,1,0:T(8,128)(2,1)S(1)}, u32[]{:S(2)}, u32[]{:S(2)}) async-start(bf16[128,16,256]{2,1,0:T(8,128)(2,1)} %bitcast.3), calls=%async_computation | async-start | bytes 2097152 | tf_op jit(solution)/shard_map/all_to_all | solution.py:543
  16.5 5.5 %sort.7 = s32[4096]{0:T(1024)} sort(s32[4096]{0:T(1024)S(1)} %bitcast.6), dimensions={0}, to_apply=%region_0.0 | sort | flops 49152 | bytes 32768 | tf_op jit(solution)/shard_map/sort | solution.py:542
  22.0 0.0 copy-done.4
  22.0 4.7 %shard_map.164 = (bf16[512,512]{1,0:T(8,128)(2,1)S(1)}, bf16[512,512]{1,0:T(8,128)(2,1)S(1)}, f32[512,512]{1,0:T(8,128)S(1)}, s32[1,4608]{1,0:T(1,128)S(1)}, s32...) custom-call(bf16[512,512]{1,0:T(8,128)(2,1)} %embed_out_hbm.1, bf16[512,512]{1,0:T(8,128)(2,1)} %proj_grid_hbm.1, ...), custom_call_target="tpu_custom_call" | custom-call | tf_op jit(solution)/shard_map/pallas_call | solution.py:78
  26.7 0.0 copy-start
  26.7 0.6 copy-done
  27.3 0.6 copy-done.2
  27.9 8.1 %all-to-all-done = bf16[128,16,256]{2,1,0:T(8,128)(2,1)S(1)} async-done(((bf16[128,16,256]{2,1,0:T(8,128)(2,1)}), bf16[128,16,256]{2,1,0:T(8,128)(2,1)S(1)}, u32[]{:S(2)}, u32[]{:S(2)}) %all-to-all-start) | async-done | bytes 1048608 | tf_op jit(solution)/shard_map/all_to_all | solution.py:543
  36.1 5.5 %shard_map.165 = (bf16[256,512]{1,0:T(8,128)(2,1)S(1)}, bf16[256,512]{1,0:T(8,128)(2,1)S(1)}, bf16[2048,512]{1,0:T(8,128)(2,1)S(1)}, f32[8,2048]{1,0:T(8,128)S(1)}, bf16[3072,512]{1,0:T(8,128)(2,1)S(1)}) custom-call(bf16[512,512]{1,0:T(8,128)(2,1)} %mesh_hbm.3, bf16[512,512]{1,0:T(8,128)(2,1)} %node_agg_hbm.1, bf16[512,512]{1,0:T(8,128)(2,1)} %edge_send_hbm.1, ...), custom_call_target="tpu_custom_call" | custom-call | tf_op jit(solution)/shard_map/pallas_call | solution.py:78
  41.6 0.4 collective-permute-start.1
  42.0 2.3 %collective-permute-start = (bf16[256,512]{1,0:T(8,128)(2,1)S(1)}, bf16[256,512]{1,0:T(8,128)(2,1)S(1)}, u32[]{:S(2)}, u32[]{:S(2)}) collective-permute-start(bf16[256,512]{1,0:T(8,128)(2,1)S(1)} %get-tuple-element.35.send_low_ref), channel_id=1, source_target_pairs={{1,0},{2,1},{3,2},{0,3},{5,4},{6,5},{7,6},{4,7},{9,8},{10,9},{11,1... | collective-permute-start | bytes 786440 | tf_op jit(solution)/shard_map/ppermute | solution.py:585
  44.3 1.8 %shard_map.166 = (bf16[256,512]{1,0:T(8,128)(2,1)S(1)}, bf16[256,512]{1,0:T(8,128)(2,1)S(1)}, bf16[512,512]{1,0:T(8,128)(2,1)S(1)}, bf16[768,512]{1,0:T(8,128)(2,1)S(1)}, f32[512,512]{1,0:T(8,128)S(1)}) custom-call(bf16[256,512]{1,0:T(8,128)(2,1)S(1)} %get-tuple-element.34.low_ref, bf16[256,512]{1,0:T(8,128)(2,1)S(1)} %get-tuple-element.35.send_low_ref, ...), custom_call_target="tpu_custom_call" | custom-call | tf_op jit(solution)/shard_map/pallas_call | solution.py:78
  46.1 0.1 collective-permute-start.3
  46.2 2.7 %collective-permute-start.2 = (bf16[256,512]{1,0:T(8,128)(2,1)S(1)}, bf16[256,512]{1,0:T(8,128)(2,1)S(1)}, u32[]{:S(2)}, u32[]{:S(2)}) collective-permute-start(bf16[256,512]{1,0:T(8,128)(2,1)S(1)} %get-tuple-element.41), channel_id=1, source_target_pairs={{1,0},{2,1},{3,2},{0,3},{5,4},{6,5},{7,6},{4,7},{9,8},{10,9},{11,1... | collective-permute-start | bytes 786440 | tf_op jit(solution)/shard_map/ppermute | solution.py:585
  48.9 0.0 copy-done.1
  48.9 0.0 copy-done.3
  48.9 2.7 %shard_map.167.acc_in_ref = f32[768,512]{1,0:T(8,128)S(1)} custom-call(s32[6,6]{1,0:T(8,128)S(1)} %get-tuple-element.26.plan_ref, s32[1,4608]{1,0:T(1,128)S(1)} %copy-done.3, s32[24,256]{1,0:T(8,128)S(1)} %copy-done.1, s32[256,48]{1,0:T(8,128)S(1)} %get-tuple-element.29.column_ref, bf16[512,512]{1,0:T(8,128)(2,1)S(1)} %get-tuple-element.39.table_ref, ...), custom_call_target="tpu_custom_call" | custom-call | tf_op jit(solution)/shard_map/pallas_call | solution.py:78
  51.6 0.0 collective-permute-done.1.left_ref
  51.6 0.0 collective-permute-done.right_ref
  51.6 2.4 %shard_map.168.acc_in_ref = f32[768,512]{1,0:T(8,128)S(1)} custom-call(s32[6,6]{1,0:T(8,128)S(1)} %get-tuple-element.26.plan_ref, f32[768,512]{1,0:T(8,128)S(1)} %shard_map.167.acc_in_ref, s32[1,4608]{1,0:T(1,128)S(1)} %copy-done.3, s32[24,256]{1,0:T(8,128)S(1)} %copy-done.1, ...), custom_call_target="tpu_custom_call", output_to_operand_aliasing={{}: (1, {})} | custom-call | tf_op jit(solution)/shard_map/pallas_call | solution.py:78
  54.0 1.9 %collective-permute-done.3.left_ref = bf16[256,512]{1,0:T(8,128)(2,1)S(1)} collective-permute-done((bf16[256,512]{1,0:T(8,128)(2,1)S(1)}, bf16[256,512]{1,0:T(8,128)(2,1)S(1)}, u32[]{:S(2)}, u32[]{:S(2)}) %collective-permute-start.3) | collective-permute-done | bytes 262176 | tf_op jit(solution)/shard_map/ppermute | solution.py:585
  56.0 0.0 collective-permute-done.2.right_ref
  56.0 4.2 %shard_map.169 = (f32[512,512]{1,0:T(8,128)}, f32[768,512]{1,0:T(8,128)S(1)}) custom-call(s32[6,6]{1,0:T(8,128)S(1)} %get-tuple-element.26.plan_ref, f32[768,512]{1,0:T(8,128)S(1)} %shard_map.168.acc_in_ref, s32[1,4608]{1,0:T(1,128)S(1)} %copy-done.3, s32[24,256]{1,0:T(8,128)S(1)} %copy-done.1, ...), custom_call_target="tpu_custom_call", output_to_operand_aliasing={{1}: (1, {})} | custom-call | tf_op jit(solution)/shard_map/pallas_call | solution.py:78
  (5 shorter events, 0.0 us)
Async XLA Ops:
  0.0 22.0 %copy-start.4 = (bf16[227,512]{1,0:T(8,128)(2,1)S(1)}, bf16[227,512]{1,0:T(8,128)(2,1)}, u32[]{:S(2)}) copy-start(bf16[227,512]{1,0:T(8,128)(2,1)} %param.24) | copy-start | bytes 697348
  5.0 31.1 %all-to-all-start = ((bf16[128,16,256]{2,1,0:T(8,128)(2,1)}), bf16[128,16,256]{2,1,0:T(8,128)(2,1)S(1)}, u32[]{:S(2)}, u32[]{:S(2)}) async-start(bf16[128,16,256]{2,1,0:T(8,128)(2,1)} %bitcast.3), calls=%async_computation | async-start | bytes 2097152 | tf_op jit(solution)/shard_map/all_to_all | solution.py:543
  26.7 0.6 %copy-start = (s32[24,256]{1,0:T(8,128)}, s32[24,256]{1,0:T(8,128)S(1)}, u32[]{:S(2)}) copy-start(s32[24,256]{1,0:T(8,128)S(1)} %get-tuple-element.28.line_ref) | copy-start | bytes 73732
  27.3 0.6 copy-start.2
  41.6 10.0 %collective-permute-start.1 = (bf16[256,512]{1,0:T(8,128)(2,1)S(1)}, bf16[256,512]{1,0:T(8,128)(2,1)S(1)}, u32[]{:S(2)}, u32[]{:S(2)}) collective-permute-start(bf16[256,512]{1,0:T(8,128)(2,1)S(1)} %get-tuple-element.35.send_low_ref), channel_id=1, source_target_pairs={{0,1},{1,2},{2,3},{3,0},{4,5},{5,6},{6,7},{7,4},{8,9},{9,10},{10,1... | collective-permute-start | bytes 786440 | tf_op jit(solution)/shard_map/ppermute | solution.py:585
  42.0 9.6 %collective-permute-start = (bf16[256,512]{1,0:T(8,128)(2,1)S(1)}, bf16[256,512]{1,0:T(8,128)(2,1)S(1)}, u32[]{:S(2)}, u32[]{:S(2)}) collective-permute-start(bf16[256,512]{1,0:T(8,128)(2,1)S(1)} %get-tuple-element.35.send_low_ref), channel_id=1, source_target_pairs={{1,0},{2,1},{3,2},{0,3},{5,4},{6,5},{7,6},{4,7},{9,8},{10,9},{11,1... | collective-permute-start | bytes 786440 | tf_op jit(solution)/shard_map/ppermute | solution.py:585
  44.3 4.5 %copy-start.1 = (s32[24,256]{1,0:T(8,128)S(1)}, s32[24,256]{1,0:T(8,128)}, u32[]{:S(2)}) copy-start(s32[24,256]{1,0:T(8,128)} %copy-done) | copy-start | bytes 73732
  44.3 4.5 %copy-start.3 = (s32[1,4608]{1,0:T(1,128)S(1)}, s32[1,4608]{1,0:T(1,128)}, u32[]{:S(2)}) copy-start(s32[1,4608]{1,0:T(1,128)} %copy-done.2) | copy-start | bytes 55300
  46.1 9.8 %collective-permute-start.3 = (bf16[256,512]{1,0:T(8,128)(2,1)S(1)}, bf16[256,512]{1,0:T(8,128)(2,1)S(1)}, u32[]{:S(2)}, u32[]{:S(2)}) collective-permute-start(bf16[256,512]{1,0:T(8,128)(2,1)S(1)} %get-tuple-element.41), channel_id=1, source_target_pairs={{0,1},{1,2},{2,3},{3,0},{4,5},{5,6},{6,7},{7,4},{8,9},{9,10},{10,1... | collective-permute-start | bytes 786440 | tf_op jit(solution)/shard_map/ppermute | solution.py:585
  46.2 9.8 %collective-permute-start.2 = (bf16[256,512]{1,0:T(8,128)(2,1)S(1)}, bf16[256,512]{1,0:T(8,128)(2,1)S(1)}, u32[]{:S(2)}, u32[]{:S(2)}) collective-permute-start(bf16[256,512]{1,0:T(8,128)(2,1)S(1)} %get-tuple-element.41), channel_id=1, source_target_pairs={{1,0},{2,1},{3,2},{0,3},{5,4},{6,5},{7,6},{4,7},{9,8},{10,9},{11,1... | collective-permute-start | bytes 786440 | tf_op jit(solution)/shard_map/ppermute | solution.py:585

commit v6 on v5

--- a/solution.py
+++ b/solution.py
@@ -12,7 +12,7 @@
 I32 = jnp.int32
 WIDE = 256
 DEAD = 1024
-SLOTS = 1024
+SLOTS = 2048
 ARRIVED = 1024
 PARTS = 6
 BLOCKS = 3
@@ -346,12 +346,26 @@
     column_ref[:, rows:] = place_ref[...].T
 
 
-def edge_sums(parts, plan_refs, recv_ref, acc_ref):
+def all_narrow(plan_ref, indices):
+    return functools.reduce(jnp.logical_and, [plan_ref[index, 2] == 1 for index in indices])
+
+
+def reach_of(plan_ref, index, block):
+    return pl.ds(pl.multiple_of(plan_ref[index, 3 + block], ALIGN), SPAN)
+
+
+def pick_receivers(index, block, plan_ref, column_ref, recv_ref):
+    row = index * BLOCKS + block
+    picker = one_hot(column_ref[:, row : row + 1] == iota((EDGES, SPAN), 1))
+    return dot(picker, recv_ref[reach_of(plan_ref, index, block), :])
+
+
+def edge_sums(parts, plan_refs, recv_ref, acc_ref, met_ref=None):
     plan_ref, key_ref, line_ref, column_ref = plan_refs
     half = parts[0][1].shape[0]
     mesh_rows = 2 * half
     rows = line_ref.shape[0]
-    narrow = functools.reduce(jnp.logical_and, [plan_ref[index, 2] == 1 for index, _ in parts])
+    narrow = all_narrow(plan_ref, [index for index, _ in parts])
 
     @pl.when(narrow)
     def _():
@@ -362,15 +376,18 @@
             selector = one_hot(line_ref[row : row + 1, :] == iota((SPAN, EDGES), 0))
             acc_ref[reach, :] += dot(selector, message)
 
-        for index, table in parts:
+        for order, (index, table) in enumerate(parts):
             for block in range(BLOCKS):
                 row = index * BLOCKS + block
-                reach = pl.ds(pl.multiple_of(plan_ref[index, 3 + block], ALIGN), SPAN)
-                receiver = column_ref[:, row : row + 1]
+                reach = reach_of(plan_ref, index, block)
                 place = column_ref[:, rows + row : rows + row + 1]
                 from_table = one_hot(place == iota((EDGES, half), 1))
-                from_recv = one_hot(receiver == iota((EDGES, SPAN), 1))
-                pre = dot(from_table, table[...]) + dot(from_recv, recv_ref[reach, :])
+                if met_ref is None:
+                    met = pick_receivers(index, block, plan_ref, column_ref, recv_ref)
+                else:
+                    at = (order * BLOCKS + block) * EDGES
+                    met = met_ref[at : at + EDGES, :]
+                pre = dot(from_table, table[...]) + met
                 if pending:
                     scatter()
                 pending.append((row, reach, silu(pre).astype(BF16)))
@@ -435,10 +452,27 @@
 
 
 def near_kernel(
-    plan_ref, acc_in_ref, key_ref, line_ref, column_ref, right_ref, left_ref, recv_ref, acc_ref
+    plan_ref,
+    acc_in_ref,
+    key_ref,
+    line_ref,
+    column_ref,
+    right_ref,
+    left_ref,
+    recv_ref,
+    acc_ref,
+    met_ref,
 ):
     parts = [(2, right_ref), (3, left_ref)]
     edge_sums(parts, (plan_ref, key_ref, line_ref, column_ref), recv_ref, acc_ref)
+
+    @pl.when(all_narrow(plan_ref, (4, 5)))
+    def _():
+        for order, index in enumerate((4, 5)):
+            for block in range(BLOCKS):
+                at = (order * BLOCKS + block) * EDGES
+                met = pick_receivers(index, block, plan_ref, column_ref, recv_ref)
+                met_ref[at : at + EDGES, :] = met
 
 
 def far_kernel(
@@ -451,6 +485,7 @@
     left_ref,
     weight_ref,
     recv_ref,
+    met_ref,
     low_ref,
     high_ref,
     own_ref,
@@ -462,7 +497,7 @@
     early = low_ref.shape[0]
     mesh_rows = early + high_ref.shape[0]
     parts = [(4, right_ref), (5, left_ref)]
-    edge_sums(parts, (plan_ref, key_ref, line_ref, column_ref), recv_ref, acc_ref)
+    edge_sums(parts, (plan_ref, key_ref, line_ref, column_ref), recv_ref, acc_ref, met_ref)
     copies = []
     rows = mesh_rows // sems.shape[0]
     for index in range(sems.shape[0]):
@@ -593,9 +628,9 @@
     )
     far = neighbours(send_high)
     acc = call(own_kernel, sums, (), (keys, line, column, own_table, recv), smem=(plan,))
-    acc = call(
+    acc, met = call(
         near_kernel,
-        sums,
+        (sums, pltpu.VMEM((2 * BLOCKS * EDGES, width), F32)),
         (),
         (acc, keys, line, column, *near, recv),
         smem=(plan,),
@@ -605,7 +640,7 @@
         far_kernel,
         (jax.ShapeDtypeStruct((mesh_rows, width), F32), sums),
         (),
-        (acc, keys, line, column, *far, weights, recv, low, high, own),
+        (acc, keys, line, column, *far, weights, recv, met, low, high, own),
         scratch=[rows_wide, dma((4,))],
         out_specs=(there, pl.BlockSpec(memory_space=pltpu.VMEM)),
         smem=(plan,),

time: 60.5 us -> 60.3 us (level)
  transfers between devices with their start and end apart: 5 -> 5, of which waited for: 2 -> 2; matrix products, arithmetic and copies ran while one was open for 9% -> 9% of each run, Pallas kernels for 19% -> 20%
where the time goes in v6:
time: 60.3 us; the launch traced here: 60.1 us
  Pallas kernels  26.6 us (44%)
  starting transfers between devices  17 us (28%)
  waiting for transfers between devices  9.47 us (16%)
  other arithmetic  5.53 us (9%)
  local copies, waits for them, and re-layouts  1.23 us (2%)
    pallas_call x7, Pallas kernels, call(): pl.pallas_call(kernel, out_shape=outs, in_specs=[spec(space) for space in...  26.6 us
    all_to_all x1, starting transfers between devices, body(): lax.all_to_all(packed.reshape(owners, slots // owners, WIDE), ('band', 'f...  11.5 us
    all_to_all x1, waiting for transfers between devices, body(): lax.all_to_all(packed.reshape(owners, slots // owners, WIDE), ('band', 'f...  8.13 us
    sort x1, other arithmetic, body(): keys = lax.sort(keys.reshape(edges), is_stable=False).reshape(1, edges)  5.53 us
    ppermute x2, starting transfers between devices, neighbours(): lax.ppermute(rows, 'face', backward)  5.07 us
    ppermute x2, waiting for transfers between devices, neighbours(): lax.ppermute(rows, 'face', forward)  1.34 us
    unnamed x10, local copies, waits for them, and re-layouts  1.21 us
  transfers between devices with their start and end apart: 5, of which 2 were waited for; matrix products, arithmetic and copies ran while one was open for 9% of the time, Pallas kernels for 20%

profile of v6, /device:TPU:1, one launch (start us, length us, event | category | flops | bytes accessed | tf_op | source)
XLA Modules:
  0.0 60.1 jit_solution(15536795552351294344)
XLA Ops:
  0.0 4.9 %shard_map.163 = (bf16[2048,256]{1,0:T(8,128)(2,1)}, s32[1,4096]{1,0:T(1,128)S(1)}) custom-call(bf16[227,2048]{1,0:T(8,128)(2,1)} %bitcast.7, s32[1,2048]{1,0:T(1,128)} %sender_hbm.1, s32[1,2048]{1,0:T(1,128)} %receiver_hbm.1, s32[1,128]{1,0:T(1,128)} %count_hbm.1, s32[1,4096]{1,0:T(1,128)} %from_hbm.1, s32[1,4096]{1,0:T(1,128)} %to_hbm.1), custom_call_target="tpu_custom_call" | custom-call | tf_op jit(solution)/shard_map/pallas_call | solution.py:78
  4.9 11.5 %all-to-all-start = ((bf16[128,16,256]{2,1,0:T(8,128)(2,1)}), bf16[128,16,256]{2,1,0:T(8,128)(2,1)S(1)}, u32[]{:S(2)}, u32[]{:S(2)}) async-start(bf16[128,16,256]{2,1,0:T(8,128)(2,1)} %bitcast.3), calls=%async_computation | async-start | bytes 2097152 | tf_op jit(solution)/shard_map/all_to_all | solution.py:578
  16.4 5.5 %sort.7 = s32[4096]{0:T(1024)} sort(s32[4096]{0:T(1024)S(1)} %bitcast.6), dimensions={0}, to_apply=%region_0.0 | sort | flops 49152 | bytes 32768 | tf_op jit(solution)/shard_map/sort | solution.py:577
  21.9 0.0 copy-done.4
  21.9 4.7 %shard_map.164 = (bf16[512,512]{1,0:T(8,128)(2,1)S(1)}, bf16[512,512]{1,0:T(8,128)(2,1)S(1)}, f32[512,512]{1,0:T(8,128)S(1)}, s32[1,4608]{1,0:T(1,128)S(1)}, s32...) custom-call(bf16[512,512]{1,0:T(8,128)(2,1)} %embed_out_hbm.1, bf16[512,512]{1,0:T(8,128)(2,1)} %proj_grid_hbm.1, ...), custom_call_target="tpu_custom_call" | custom-call | tf_op jit(solution)/shard_map/pallas_call | solution.py:78
  26.6 0.0 copy-start
  26.6 0.6 %copy-done = s32[24,256]{1,0:T(8,128)} copy-done((s32[24,256]{1,0:T(8,128)}, s32[24,256]{1,0:T(8,128)S(1)}, u32[]{:S(2)}) %copy-start) | copy-done | bytes 24600
  27.2 0.6 copy-done.2
  27.8 8.1 %all-to-all-done = bf16[128,16,256]{2,1,0:T(8,128)(2,1)S(1)} async-done(((bf16[128,16,256]{2,1,0:T(8,128)(2,1)}), bf16[128,16,256]{2,1,0:T(8,128)(2,1)S(1)}, u32[]{:S(2)}, u32[]{:S(2)}) %all-to-all-start) | async-done | bytes 1048608 | tf_op jit(solution)/shard_map/all_to_all | solution.py:578
  36.0 5.5 %shard_map.165 = (bf16[256,512]{1,0:T(8,128)(2,1)S(1)}, bf16[256,512]{1,0:T(8,128)(2,1)S(1)}, bf16[2048,512]{1,0:T(8,128)(2,1)S(1)}, f32[8,2048]{1,0:T(8,128)S(1)}, bf16[3072,512]{1,0:T(8,128)(2,1)S(1)}) custom-call(bf16[512,512]{1,0:T(8,128)(2,1)} %mesh_hbm.3, bf16[512,512]{1,0:T(8,128)(2,1)} %node_agg_hbm.1, bf16[512,512]{1,0:T(8,128)(2,1)} %edge_send_hbm.1, ...), custom_call_target="tpu_custom_call" | custom-call | tf_op jit(solution)/shard_map/pallas_call | solution.py:78
  41.5 0.3 collective-permute-start.1
  41.8 2.4 %collective-permute-start = (bf16[256,512]{1,0:T(8,128)(2,1)S(1)}, bf16[256,512]{1,0:T(8,128)(2,1)S(1)}, u32[]{:S(2)}, u32[]{:S(2)}) collective-permute-start(bf16[256,512]{1,0:T(8,128)(2,1)S(1)} %get-tuple-element.37.send_low_ref), channel_id=1, source_target_pairs={{1,0},{2,1},{3,2},{0,3},{5,4},{6,5},{7,6},{4,7},{9,8},{10,9},{11,1... | collective-permute-start | bytes 786440 | tf_op jit(solution)/shard_map/ppermute | solution.py:620
  44.2 1.8 %shard_map.166 = (bf16[256,512]{1,0:T(8,128)(2,1)S(1)}, bf16[256,512]{1,0:T(8,128)(2,1)S(1)}, bf16[512,512]{1,0:T(8,128)(2,1)S(1)}, bf16[768,512]{1,0:T(8,128)(2,1)S(1)}, f32[512,512]{1,0:T(8,128)S(1)}) custom-call(bf16[256,512]{1,0:T(8,128)(2,1)S(1)} %get-tuple-element.36.low_ref, bf16[256,512]{1,0:T(8,128)(2,1)S(1)} %get-tuple-element.37.send_low_ref, ...), custom_call_target="tpu_custom_call" | custom-call | tf_op jit(solution)/shard_map/pallas_call | solution.py:78
  46.0 0.1 collective-permute-start.3
  46.1 2.7 %collective-permute-start.2 = (bf16[256,512]{1,0:T(8,128)(2,1)S(1)}, bf16[256,512]{1,0:T(8,128)(2,1)S(1)}, u32[]{:S(2)}, u32[]{:S(2)}) collective-permute-start(bf16[256,512]{1,0:T(8,128)(2,1)S(1)} %get-tuple-element.44), channel_id=1, source_target_pairs={{1,0},{2,1},{3,2},{0,3},{5,4},{6,5},{7,6},{4,7},{9,8},{10,9},{11,1... | collective-permute-start | bytes 786440 | tf_op jit(solution)/shard_map/ppermute | solution.py:620
  48.8 0.0 copy-done.1
  48.8 0.0 copy-done.3
  48.8 2.7 %shard_map.167.acc_in_ref = f32[768,512]{1,0:T(8,128)S(1)} custom-call(s32[6,6]{1,0:T(8,128)S(1)} %get-tuple-element.28.plan_ref, s32[1,4608]{1,0:T(1,128)S(1)} %copy-done.3, s32[24,256]{1,0:T(8,128)S(1)} %copy-done.1, s32[256,48]{1,0:T(8,128)S(1)} %get-tuple-element.31.column_ref, bf16[512,512]{1,0:T(8,128)(2,1)S(1)} %get-tuple-element.41.table_ref, ...), custom_call_target="tpu_custom_call" | custom-call | tf_op jit(solution)/shard_map/pallas_call | solution.py:78
  51.5 0.0 collective-permute-done.1.left_ref
  51.5 0.0 collective-permute-done.right_ref
  51.5 3.1 %shard_map.168 = (f32[768,512]{1,0:T(8,128)S(1)}, f32[1536,512]{1,0:T(8,128)S(1)}) custom-call(s32[6,6]{1,0:T(8,128)S(1)} %get-tuple-element.28.plan_ref, f32[768,512]{1,0:T(8,128)S(1)} %shard_map.167.acc_in_ref, s32[1,4608]{1,0:T(1,128)S(1)} %copy-done.3, s32[24,256]{1,0:T(8,128)S(1)} %copy-done.1, ...), custom_call_target="tpu_custom_call", output_to_operand_aliasing={{0}: (1, {})} | custom-call | tf_op jit(solution)/shard_map/pallas_call | solution.py:78
  54.6 1.3 %collective-permute-done.3.left_ref = bf16[256,512]{1,0:T(8,128)(2,1)S(1)} collective-permute-done((bf16[256,512]{1,0:T(8,128)(2,1)S(1)}, bf16[256,512]{1,0:T(8,128)(2,1)S(1)}, u32[]{:S(2)}, u32[]{:S(2)}) %collective-permute-start.3) | collective-permute-done | bytes 262176 | tf_op jit(solution)/shard_map/ppermute | solution.py:620
  55.9 0.0 collective-permute-done.2.right_ref
  55.9 4.0 %shard_map.169 = (f32[512,512]{1,0:T(8,128)}, f32[768,512]{1,0:T(8,128)S(1)}) custom-call(s32[6,6]{1,0:T(8,128)S(1)} %get-tuple-element.28.plan_ref, f32[768,512]{1,0:T(8,128)S(1)} %get-tuple-element.43.acc_in_ref, s32[1,4608]{1,0:T(1,128)S(1)} %copy-done.3, s32[24,256]{1,0:T(8,128)S(1)} %copy-done.1, ...), custom_call_target="tpu_custom_call", output_to_operand_aliasing={{1}: (1, {})} | custom-call | tf_op jit(solution)/shard_map/pallas_call | solution.py:78
  (5 shorter events, 0.0 us)
Async XLA Ops:
  0.0 21.9 %copy-start.4 = (bf16[227,512]{1,0:T(8,128)(2,1)S(1)}, bf16[227,512]{1,0:T(8,128)(2,1)}, u32[]{:S(2)}) copy-start(bf16[227,512]{1,0:T(8,128)(2,1)} %param.24) | copy-start | bytes 697348
  4.9 31.1 %all-to-all-start = ((bf16[128,16,256]{2,1,0:T(8,128)(2,1)}), bf16[128,16,256]{2,1,0:T(8,128)(2,1)S(1)}, u32[]{:S(2)}, u32[]{:S(2)}) async-start(bf16[128,16,256]{2,1,0:T(8,128)(2,1)} %bitcast.3), calls=%async_computation | async-start | bytes 2097152 | tf_op jit(solution)/shard_map/all_to_all | solution.py:578
  26.6 0.6 %copy-start = (s32[24,256]{1,0:T(8,128)}, s32[24,256]{1,0:T(8,128)S(1)}, u32[]{:S(2)}) copy-start(s32[24,256]{1,0:T(8,128)S(1)} %get-tuple-element.30.line_ref) | copy-start | bytes 73732
  27.2 0.6 copy-start.2
  41.5 10.0 %collective-permute-start.1 = (bf16[256,512]{1,0:T(8,128)(2,1)S(1)}, bf16[256,512]{1,0:T(8,128)(2,1)S(1)}, u32[]{:S(2)}, u32[]{:S(2)}) collective-permute-start(bf16[256,512]{1,0:T(8,128)(2,1)S(1)} %get-tuple-element.37.send_low_ref), channel_id=1, source_target_pairs={{0,1},{1,2},{2,3},{3,0},{4,5},{5,6},{6,7},{7,4},{8,9},{9,10},{10,1... | collective-permute-start | bytes 786440 | tf_op jit(solution)/shard_map/ppermute | solution.py:620
  41.8 9.7 %collective-permute-start = (bf16[256,512]{1,0:T(8,128)(2,1)S(1)}, bf16[256,512]{1,0:T(8,128)(2,1)S(1)}, u32[]{:S(2)}, u32[]{:S(2)}) collective-permute-start(bf16[256,512]{1,0:T(8,128)(2,1)S(1)} %get-tuple-element.37.send_low_ref), channel_id=1, source_target_pairs={{1,0},{2,1},{3,2},{0,3},{5,4},{6,5},{7,6},{4,7},{9,8},{10,9},{11,1... | collective-permute-start | bytes 786440 | tf_op jit(solution)/shard_map/ppermute | solution.py:620
  44.2 4.5 %copy-start.1 = (s32[24,256]{1,0:T(8,128)S(1)}, s32[24,256]{1,0:T(8,128)}, u32[]{:S(2)}) copy-start(s32[24,256]{1,0:T(8,128)} %copy-done) | copy-start | bytes 73732
  44.2 4.5 %copy-start.3 = (s32[1,4608]{1,0:T(1,128)S(1)}, s32[1,4608]{1,0:T(1,128)}, u32[]{:S(2)}) copy-start(s32[1,4608]{1,0:T(1,128)} %copy-done.2) | copy-start | bytes 55300
  46.0 9.9 %collective-permute-start.3 = (bf16[256,512]{1,0:T(8,128)(2,1)S(1)}, bf16[256,512]{1,0:T(8,128)(2,1)S(1)}, u32[]{:S(2)}, u32[]{:S(2)}) collective-permute-start(bf16[256,512]{1,0:T(8,128)(2,1)S(1)} %get-tuple-element.44), channel_id=1, source_target_pairs={{0,1},{1,2},{2,3},{3,0},{4,5},{5,6},{6,7},{7,4},{8,9},{9,10},{10,1... | collective-permute-start | bytes 786440 | tf_op jit(solution)/shard_map/ppermute | solution.py:620
  46.1 9.8 %collective-permute-start.2 = (bf16[256,512]{1,0:T(8,128)(2,1)S(1)}, bf16[256,512]{1,0:T(8,128)(2,1)S(1)}, u32[]{:S(2)}, u32[]{:S(2)}) collective-permute-start(bf16[256,512]{1,0:T(8,128)(2,1)S(1)} %get-tuple-element.44), channel_id=1, source_target_pairs={{1,0},{2,1},{3,2},{0,3},{5,4},{6,5},{7,6},{4,7},{9,8},{10,9},{11,1... | collective-permute-start | bytes 786440 | tf_op jit(solution)/shard_map/ppermute | solution.py:620

commit v7 on v6

--- a/solution.py
+++ b/solution.py
@@ -309,13 +309,13 @@
         last = jnp.int32(edges)
         if index < PARTS - 1:
             last = first_at_least((index + 1) * mesh_rows * half)
-        share = (last - first + BLOCKS - 1) // BLOCKS
+        share = jnp.minimum((last - first + BLOCKS - 1) // BLOCKS, EDGES)
 
         def receiver_at(position):
             key = key_scalar[0, jnp.clip(position, 0, edges - 1)]
             return key // half - index * mesh_rows
 
-        narrow = share <= EDGES
+        narrow = jnp.bool_(True)
         for block in range(BLOCKS):
             start = jnp.minimum(first + block * share, last)
             end = jnp.minimum(start + share, last)
@@ -334,6 +334,7 @@
         plan_ref[index, 0] = first
         plan_ref[index, 1] = last
         plan_ref[index, 2] = narrow.astype(I32)
+        plan_ref[index, 3 + BLOCKS] = jnp.minimum(first + BLOCKS * share, last)
         first = last
     rows = line_ref.shape[0]
     for block in range(PARTS * BLOCKS):
@@ -394,23 +395,27 @@
         scatter()
 
     for index, table in parts:
-        origin = plan_ref[index, 0] // 128 * 128
-
-        def general(block, carry):
-            keys = key_ref[:, pl.ds(pl.multiple_of(origin + block * EDGES, 128), EDGES)]
+        first = jnp.where(narrow, plan_ref[index, 3 + BLOCKS], plan_ref[index, 0])
+        last = plan_ref[index, 1]
+        origin = first // 128 * 128
+
+        def general(block, carry, index=index, table=table, first=first, last=last, origin=origin):
+            start = pl.multiple_of(origin + block * EDGES, 128)
+            keys = key_ref[:, pl.ds(start, EDGES)]
             column = as_column(keys)
             receiver = lax.div(column, half) - index * mesh_rows
             from_table = one_hot((column & (half - 1)) == iota((EDGES, half), 1))
             from_recv = one_hot(receiver == iota((EDGES, mesh_rows), 1))
             message = silu(dot(from_table, table[...]) + dot(from_recv, recv_ref[:mesh_rows, :]))
             line = lax.div(keys, half) - index * mesh_rows
-            line = jnp.where((keys < 0) | (line < 0) | (line >= mesh_rows), -mesh_rows, line)
+            place = iota((1, EDGES), 1) + start
+            line = jnp.where((place >= first) & (place < last), line, -mesh_rows)
             selector = one_hot(line == iota((mesh_rows, EDGES), 0))
             acc_ref[:mesh_rows, :] += dot(selector, message.astype(BF16))
             return carry
 
-        blocks = (plan_ref[index, 1] - origin + EDGES - 1) // EDGES
-        lax.fori_loop(0, jnp.where(narrow, 0, blocks), general, 0)
+        blocks = (last - origin + EDGES - 1) // EDGES
+        lax.fori_loop(0, jnp.where(first < last, blocks, 0), general, 0)
 
 
 def high_kernel(
@@ -591,7 +596,7 @@
             pltpu.VMEM((1, edges + 2 * EDGES), I32),
             lines,
             columns,
-            jax.ShapeDtypeStruct((PARTS, 3 + BLOCKS), I32),
+            jax.ShapeDtypeStruct((PARTS, 4 + BLOCKS), I32),
         ),
         (embed_out, proj_grid, mesh_nodes, proj_mesh, node_self, keys),
         (),

time: 60.3 us -> 60.3 us (level)
  no operation moved by 1% of the time
where the time goes in v7:
time: 60.3 us; the launch traced here: 60.1 us
  Pallas kernels  26.6 us (44%)
  starting transfers between devices  17 us (28%)
  waiting for transfers between devices  9.48 us (16%)
  other arithmetic  5.53 us (9%)
  local copies, waits for them, and re-layouts  1.23 us (2%)
    pallas_call x7, Pallas kernels, call(): pl.pallas_call(kernel, out_shape=outs, in_specs=[spec(space) for space in...  26.6 us
    all_to_all x1, starting transfers between devices, body(): lax.all_to_all(packed.reshape(owners, slots // owners, WIDE), ('band', 'f...  11.5 us
    all_to_all x1, waiting for transfers between devices, body(): lax.all_to_all(packed.reshape(owners, slots // owners, WIDE), ('band', 'f...  8.14 us
    sort x1, other arithmetic, body(): keys = lax.sort(keys.reshape(edges), is_stable=False).reshape(1, edges)  5.53 us
    ppermute x2, starting transfers between devices, neighbours(): lax.ppermute(rows, 'face', backward)  5.07 us
    ppermute x2, waiting for transfers between devices, neighbours(): lax.ppermute(rows, 'face', forward)  1.33 us
    unnamed x10, local copies, waits for them, and re-layouts  1.21 us
  transfers between devices with their start and end apart: 5, of which 2 were waited for; matrix products, arithmetic and copies ran while one was open for 9% of the time, Pallas kernels for 20%

profile of v7, /device:TPU:1, one launch (start us, length us, event | category | flops | bytes accessed | tf_op | source)
XLA Modules:
  0.0 60.1 jit_solution(4633391739263609625)
XLA Ops:
  0.0 4.9 %shard_map.163 = (bf16[2048,256]{1,0:T(8,128)(2,1)}, s32[1,4096]{1,0:T(1,128)S(1)}) custom-call(bf16[227,2048]{1,0:T(8,128)(2,1)} %bitcast.7, s32[1,2048]{1,0:T(1,128)} %sender_hbm.1, s32[1,2048]{1,0:T(1,128)} %receiver_hbm.1, s32[1,128]{1,0:T(1,128)} %count_hbm.1, s32[1,4096]{1,0:T(1,128)} %from_hbm.1, s32[1,4096]{1,0:T(1,128)} %to_hbm.1), custom_call_target="tpu_custom_call" | custom-call | tf_op jit(solution)/shard_map/pallas_call | solution.py:78
  4.9 11.5 %all-to-all-start = ((bf16[128,16,256]{2,1,0:T(8,128)(2,1)}), bf16[128,16,256]{2,1,0:T(8,128)(2,1)S(1)}, u32[]{:S(2)}, u32[]{:S(2)}) async-start(bf16[128,16,256]{2,1,0:T(8,128)(2,1)} %bitcast.3), calls=%async_computation | async-start | bytes 2097152 | tf_op jit(solution)/shard_map/all_to_all | solution.py:583
  16.4 5.5 %sort.7 = s32[4096]{0:T(1024)} sort(s32[4096]{0:T(1024)S(1)} %bitcast.6), dimensions={0}, to_apply=%region_0.0 | sort | flops 49152 | bytes 32768 | tf_op jit(solution)/shard_map/sort | solution.py:582
  21.9 0.0 copy-done.4
  21.9 4.7 %shard_map.164 = (bf16[512,512]{1,0:T(8,128)(2,1)S(1)}, bf16[512,512]{1,0:T(8,128)(2,1)S(1)}, f32[512,512]{1,0:T(8,128)S(1)}, s32[1,4608]{1,0:T(1,128)S(1)}, s32...) custom-call(bf16[512,512]{1,0:T(8,128)(2,1)} %embed_out_hbm.1, bf16[512,512]{1,0:T(8,128)(2,1)} %proj_grid_hbm.1, ...), custom_call_target="tpu_custom_call" | custom-call | tf_op jit(solution)/shard_map/pallas_call | solution.py:78
  26.6 0.0 copy-start
  26.6 0.6 %copy-done = s32[24,256]{1,0:T(8,128)} copy-done((s32[24,256]{1,0:T(8,128)}, s32[24,256]{1,0:T(8,128)S(1)}, u32[]{:S(2)}) %copy-start) | copy-done | bytes 24600
  27.2 0.6 copy-done.2
  27.8 8.1 %all-to-all-done = bf16[128,16,256]{2,1,0:T(8,128)(2,1)S(1)} async-done(((bf16[128,16,256]{2,1,0:T(8,128)(2,1)}), bf16[128,16,256]{2,1,0:T(8,128)(2,1)S(1)}, u32[]{:S(2)}, u32[]{:S(2)}) %all-to-all-start) | async-done | bytes 1048608 | tf_op jit(solution)/shard_map/all_to_all | solution.py:583
  36.0 5.5 %shard_map.165 = (bf16[256,512]{1,0:T(8,128)(2,1)S(1)}, bf16[256,512]{1,0:T(8,128)(2,1)S(1)}, bf16[2048,512]{1,0:T(8,128)(2,1)S(1)}, f32[8,2048]{1,0:T(8,128)S(1)}, bf16[3072,512]{1,0:T(8,128)(2,1)S(1)}) custom-call(bf16[512,512]{1,0:T(8,128)(2,1)} %mesh_hbm.3, bf16[512,512]{1,0:T(8,128)(2,1)} %node_agg_hbm.1, bf16[512,512]{1,0:T(8,128)(2,1)} %edge_send_hbm.1, ...), custom_call_target="tpu_custom_call" | custom-call | tf_op jit(solution)/shard_map/pallas_call | solution.py:78
  41.5 0.3 collective-permute-start.1
  41.8 2.4 %collective-permute-start = (bf16[256,512]{1,0:T(8,128)(2,1)S(1)}, bf16[256,512]{1,0:T(8,128)(2,1)S(1)}, u32[]{:S(2)}, u32[]{:S(2)}) collective-permute-start(bf16[256,512]{1,0:T(8,128)(2,1)S(1)} %get-tuple-element.37.send_low_ref), channel_id=1, source_target_pairs={{1,0},{2,1},{3,2},{0,3},{5,4},{6,5},{7,6},{4,7},{9,8},{10,9},{11,1... | collective-permute-start | bytes 786440 | tf_op jit(solution)/shard_map/ppermute | solution.py:625
  44.2 1.8 %shard_map.166 = (bf16[256,512]{1,0:T(8,128)(2,1)S(1)}, bf16[256,512]{1,0:T(8,128)(2,1)S(1)}, bf16[512,512]{1,0:T(8,128)(2,1)S(1)}, bf16[768,512]{1,0:T(8,128)(2,1)S(1)}, f32[512,512]{1,0:T(8,128)S(1)}) custom-call(bf16[256,512]{1,0:T(8,128)(2,1)S(1)} %get-tuple-element.36.low_ref, bf16[256,512]{1,0:T(8,128)(2,1)S(1)} %get-tuple-element.37.send_low_ref, ...), custom_call_target="tpu_custom_call" | custom-call | tf_op jit(solution)/shard_map/pallas_call | solution.py:78
  46.0 0.1 collective-permute-start.3
  46.1 2.7 %collective-permute-start.2 = (bf16[256,512]{1,0:T(8,128)(2,1)S(1)}, bf16[256,512]{1,0:T(8,128)(2,1)S(1)}, u32[]{:S(2)}, u32[]{:S(2)}) collective-permute-start(bf16[256,512]{1,0:T(8,128)(2,1)S(1)} %get-tuple-element.44), channel_id=1, source_target_pairs={{1,0},{2,1},{3,2},{0,3},{5,4},{6,5},{7,6},{4,7},{9,8},{10,9},{11,1... | collective-permute-start | bytes 786440 | tf_op jit(solution)/shard_map/ppermute | solution.py:625
  48.8 0.0 copy-done.1
  48.8 0.0 copy-done.3
  48.8 2.7 %shard_map.167.acc_in_ref = f32[768,512]{1,0:T(8,128)S(1)} custom-call(s32[6,7]{1,0:T(8,128)S(1)} %get-tuple-element.28.plan_ref, s32[1,4608]{1,0:T(1,128)S(1)} %copy-done.3, s32[24,256]{1,0:T(8,128)S(1)} %copy-done.1, s32[256,48]{1,0:T(8,128)S(1)} %get-tuple-element.31.column_ref, bf16[512,512]{1,0:T(8,128)(2,1)S(1)} %get-tuple-element.41.table_ref, ...), custom_call_target="tpu_custom_call" | custom-call | tf_op jit(solution)/shard_map/pallas_call | solution.py:78
  51.5 0.0 collective-permute-done.1.left_ref
  51.5 0.0 collective-permute-done.right_ref
  51.5 3.1 %shard_map.168 = (f32[768,512]{1,0:T(8,128)S(1)}, f32[1536,512]{1,0:T(8,128)S(1)}) custom-call(s32[6,7]{1,0:T(8,128)S(1)} %get-tuple-element.28.plan_ref, f32[768,512]{1,0:T(8,128)S(1)} %shard_map.167.acc_in_ref, s32[1,4608]{1,0:T(1,128)S(1)} %copy-done.3, s32[24,256]{1,0:T(8,128)S(1)} %copy-done.1, ...), custom_call_target="tpu_custom_call", output_to_operand_aliasing={{0}: (1, {})} | custom-call | tf_op jit(solution)/shard_map/pallas_call | solution.py:78
  54.6 1.3 %collective-permute-done.3.left_ref = bf16[256,512]{1,0:T(8,128)(2,1)S(1)} collective-permute-done((bf16[256,512]{1,0:T(8,128)(2,1)S(1)}, bf16[256,512]{1,0:T(8,128)(2,1)S(1)}, u32[]{:S(2)}, u32[]{:S(2)}) %collective-permute-start.3) | collective-permute-done | bytes 262176 | tf_op jit(solution)/shard_map/ppermute | solution.py:625
  55.9 0.0 collective-permute-done.2.right_ref
  55.9 4.0 %shard_map.169 = (f32[512,512]{1,0:T(8,128)}, f32[768,512]{1,0:T(8,128)S(1)}) custom-call(s32[6,7]{1,0:T(8,128)S(1)} %get-tuple-element.28.plan_ref, f32[768,512]{1,0:T(8,128)S(1)} %get-tuple-element.43.acc_in_ref, s32[1,4608]{1,0:T(1,128)S(1)} %copy-done.3, s32[24,256]{1,0:T(8,128)S(1)} %copy-done.1, ...), custom_call_target="tpu_custom_call", output_to_operand_aliasing={{1}: (1, {})} | custom-call | tf_op jit(solution)/shard_map/pallas_call | solution.py:78
  (5 shorter events, 0.0 us)
Async XLA Ops:
  0.0 21.9 %copy-start.4 = (bf16[227,512]{1,0:T(8,128)(2,1)S(1)}, bf16[227,512]{1,0:T(8,128)(2,1)}, u32[]{:S(2)}) copy-start(bf16[227,512]{1,0:T(8,128)(2,1)} %param.24) | copy-start | bytes 697348
  4.9 31.1 %all-to-all-start = ((bf16[128,16,256]{2,1,0:T(8,128)(2,1)}), bf16[128,16,256]{2,1,0:T(8,128)(2,1)S(1)}, u32[]{:S(2)}, u32[]{:S(2)}) async-start(bf16[128,16,256]{2,1,0:T(8,128)(2,1)} %bitcast.3), calls=%async_computation | async-start | bytes 2097152 | tf_op jit(solution)/shard_map/all_to_all | solution.py:583
  26.6 0.6 %copy-start = (s32[24,256]{1,0:T(8,128)}, s32[24,256]{1,0:T(8,128)S(1)}, u32[]{:S(2)}) copy-start(s32[24,256]{1,0:T(8,128)S(1)} %get-tuple-element.30.line_ref) | copy-start | bytes 73732
  27.2 0.6 copy-start.2
  41.5 10.0 %collective-permute-start.1 = (bf16[256,512]{1,0:T(8,128)(2,1)S(1)}, bf16[256,512]{1,0:T(8,128)(2,1)S(1)}, u32[]{:S(2)}, u32[]{:S(2)}) collective-permute-start(bf16[256,512]{1,0:T(8,128)(2,1)S(1)} %get-tuple-element.37.send_low_ref), channel_id=1, source_target_pairs={{0,1},{1,2},{2,3},{3,0},{4,5},{5,6},{6,7},{7,4},{8,9},{9,10},{10,1... | collective-permute-start | bytes 786440 | tf_op jit(solution)/shard_map/ppermute | solution.py:625
  41.8 9.7 %collective-permute-start = (bf16[256,512]{1,0:T(8,128)(2,1)S(1)}, bf16[256,512]{1,0:T(8,128)(2,1)S(1)}, u32[]{:S(2)}, u32[]{:S(2)}) collective-permute-start(bf16[256,512]{1,0:T(8,128)(2,1)S(1)} %get-tuple-element.37.send_low_ref), channel_id=1, source_target_pairs={{1,0},{2,1},{3,2},{0,3},{5,4},{6,5},{7,6},{4,7},{9,8},{10,9},{11,1... | collective-permute-start | bytes 786440 | tf_op jit(solution)/shard_map/ppermute | solution.py:625
  44.2 4.5 %copy-start.1 = (s32[24,256]{1,0:T(8,128)S(1)}, s32[24,256]{1,0:T(8,128)}, u32[]{:S(2)}) copy-start(s32[24,256]{1,0:T(8,128)} %copy-done) | copy-start | bytes 73732
  44.2 4.5 %copy-start.3 = (s32[1,4608]{1,0:T(1,128)S(1)}, s32[1,4608]{1,0:T(1,128)}, u32[]{:S(2)}) copy-start(s32[1,4608]{1,0:T(1,128)} %copy-done.2) | copy-start | bytes 55300
  46.0 9.9 %collective-permute-start.3 = (bf16[256,512]{1,0:T(8,128)(2,1)S(1)}, bf16[256,512]{1,0:T(8,128)(2,1)S(1)}, u32[]{:S(2)}, u32[]{:S(2)}) collective-permute-start(bf16[256,512]{1,0:T(8,128)(2,1)S(1)} %get-tuple-element.44), channel_id=1, source_target_pairs={{0,1},{1,2},{2,3},{3,0},{4,5},{5,6},{6,7},{7,4},{8,9},{9,10},{10,1... | collective-permute-start | bytes 786440 | tf_op jit(solution)/shard_map/ppermute | solution.py:625
  46.1 9.8 %collective-permute-start.2 = (bf16[256,512]{1,0:T(8,128)(2,1)S(1)}, bf16[256,512]{1,0:T(8,128)(2,1)S(1)}, u32[]{:S(2)}, u32[]{:S(2)}) collective-permute-start(bf16[256,512]{1,0:T(8,128)(2,1)S(1)} %get-tuple-element.44), channel_id=1, source_target_pairs={{1,0},{2,1},{3,2},{0,3},{5,4},{6,5},{7,6},{4,7},{9,8},{10,9},{11,1... | collective-permute-start | bytes 786440 | tf_op jit(solution)/shard_map/ppermute | solution.py:625
